TPU v7x, 32 devices: a whole 2x2x4 slice. The times are simulated.
32 devices in a mesh: inp: 2 (over y), pa: 4 (over x, core), pb: 4 (over z).
Axes of the slice: x: 2, y: 2, z: 4, core: 2. Of those that a mesh axis runs over, the one named last changes fastest.
Arguments:
- log_inputs: float32 [2, 256, 256, 256], P('inp', 'pa', 'pb'), may hold values from -6 to 6
- warm_potential: float32 [2, 256, 256, 256], P('inp', 'pa', 'pb'), may hold values from -6 to 6
- bary_weights: float32 [2], P('inp'), may hold values from 0.1 to 0.5
- band_reach: int32 [3], replicated, may hold values from 0 to 2, each once
- bary_cotangent: float32 [256, 256, 256], P('pa', 'pb', 'inp'), may hold values from -6 to 6
Outputs:
- barycenter: float32 [256, 256, 256], P('pa', 'pb', 'inp')
- input_grad: float32 [2, 256, 256, 256], P('inp', 'pa', 'pb')
Inputs may be any that keep to these rules, and one draw needn't show every extreme that they name: `band_reach`: a permutation of 0, 1 and 2, one entry a line direction.
All inputs are finite; a program needn't handle non-finite values.
Results may differ from a plain program's by a relative error of at most 0.00022.
Values sent between devices are 32-bit elements; how exact they have to be, the bound alone decides.
No kernel may reach another device: no remote copies, remote signals or barrier semaphores. Data moves between devices by JAX's collectives and lax.ppermute only.
A program may use at most 128 MiB of HBM per device.

v0:
```python
import functools
import math

import jax
import jax.numpy as jnp
from jax import lax
from jax.experimental import pallas as pl
from jax.experimental.pallas import tpu as pltpu
from jax.sharding import PartitionSpec as P

BLOCK = 4
BLOCK_BITS = 2
HALO = 2 * BLOCK
SIGMA = 3.0
SUB = 8
GROUP = 8
F32 = jnp.float32
BF16 = jnp.bfloat16


def tap(offset):
    gauss = math.exp(-offset * offset / (2.0 * SIGMA * SIGMA)) / (SIGMA * math.sqrt(2.0 * math.pi))
    return 0.5 * gauss + (0.5 if offset == 0 else 0.0)


def weight(i, j, reach):
    offset = (i - j).astype(F32)
    inside = jnp.abs((i >> BLOCK_BITS) - (j >> BLOCK_BITS)) <= reach
    gauss = jnp.exp(-offset * offset / (2.0 * SIGMA * SIGMA)) / (SIGMA * math.sqrt(2.0 * math.pi))
    return jnp.where(i == j, 0.5, 0.0) + 0.5 * jnp.where(inside, gauss, 0.0)


def halves(value):
    high = value.astype(BF16)
    return high, (value - high.astype(F32)).astype(BF16)


def dot(a, b):
    return jnp.dot(a, b, preferred_element_type=F32)


AXES = ("pa", "pb")


def parity(line):
    return lax.rem(lax.axis_index(AXES[line]), 2)


def edge(line, swap, size, first=0):
    return pl.ds(pl.multiple_of(first + jnp.where(parity(line) == swap, size - HALO, 0), HALO), HALO)


def iotas(shape):
    return (lax.broadcasted_iota(jnp.int32, shape, 0), lax.broadcasted_iota(jnp.int32, shape, 1))


def fill_z(ref, reach):
    n = ref.shape[1]
    i, j = iotas((n, n))
    high, low = halves(weight(i, j, reach))
    ref[0:n] = high
    ref[n : 2 * n] = high
    ref[2 * n : 3 * n] = low


def z_product(rows, kz):
    high, low = halves(rows)
    return dot(jnp.concatenate([high, low, high], axis=1), kz[...])


def y_depth(ny, halo):
    return 3 * (ny + 2 * halo)


def fill_y(ref, reach, halo):
    ny, depth = ref.shape
    i, c = iotas((ny, depth))
    wide = 2 * halo
    own = c < 3 * ny
    size = jnp.where(own, ny, max(wide, 1))
    c = jnp.where(own, c, c - 3 * ny)
    part = jnp.where(c >= 2 * size, 2, jnp.where(c >= size, 1, 0))
    j = c - part * size
    if halo:
        swap = jnp.where(j >= halo, 1, 0)
        e = j - swap * halo
        j = jnp.where(own, j, jnp.where(swap == parity(1), ny + e, e - halo))
    value = weight(i + HALO, j + HALO, reach)
    high = value.astype(BF16).astype(F32)
    ref[...] = jnp.where(part == 2, value - high, high).astype(BF16)


def y_product(ky, own, halo=None):
    high, low = halves(own)
    pieces = [high, low, high]
    if halo is not None:
        high, low = halves(halo)
        pieces += [high, low, high]
    return dot(ky[...], jnp.concatenate(pieces, axis=0))


def x_sum(plane, n, reach):
    phase = n % BLOCK
    span = BLOCK * reach
    total = tap(0) * plane(n)
    for d in range(1, span + 1):
        total = total + tap(d) * (plane(n - d) + plane(n + d))
    for d in range(span + 1, span + phase + 1):
        total = total + tap(d) * plane(n - d)
    for d in range(span + 1, span + BLOCK - phase):
        total = total + tap(d) * plane(n + d)
    return total


MATRICES = ("kz", "ky", "ky0")
EDGES = ("even", "odd", "y_even", "y_odd", "corner_even", "corner_odd")
INSIDE = ("warm", "inputs", "t", "d", "t_in", "d_in", "far", "cot", "u", "u_out", "u_ext", *EDGES, *(edge + "_out" for edge in EDGES), *MATRICES)
BOTH = (0, 1)
COST = pl.CostEstimate(flops=1, bytes_accessed=1, transcendentals=0)


class Stage:
    def __init__(self, shape, cut, piece, kind, finish=None, start=(), send=None, fills=False):
        self.cut = cut
        self.piece = piece
        self.shape = tuple(n // 2 if line == cut else n for line, n in enumerate(shape))
        self.kind = kind
        self.finish = finish
        self.start = start
        self.send = send
        self.fills = fills

    def matrices(self):
        nx, ny, nz = self.shape
        shapes = {"kz": (3 * nz, nz)}
        if 1 in self.start:
            shapes["ky0"] = (ny, y_depth(ny, 0))
        else:
            shapes["ky"] = (ny, y_depth(ny, HALO))
        return shapes

    def needs(self):
        if self.fills:
            return ()
        wanted = {"kz": 2 in self.start, "ky": self.finish in (1, BOTH), "ky0": 1 in self.start}
        return tuple(key for key in wanted if wanted[key])

    def scratch(self):
        nx, ny, nz = self.shape
        items = {"work": pltpu.VMEM((GROUP, ny, nz), F32)}
        if self.finish == BOTH:
            items["edge"] = pltpu.VMEM((GROUP, 2 * HALO, nz), F32)
            items["y_ext"] = pltpu.VMEM((nx + 2 * HALO, 2 * HALO, nz), F32)
        for key in self.reads() + self.writes():
            halved = key in ("cot", "far", "send", "keep")
            items[key + "_here"] = pltpu.VMEM((nx, ny, nz // 2 if halved else nz), F32)
        streams = len(self.reads() + self.writes())
        if streams:
            items["sems"] = pltpu.SemaphoreType.DMA((streams, nx // GROUP))
        return items

    def reads(self):
        return ("warm",) if self.kind == "exp" and self.piece == 0 else ()

    def writes(self):
        return {"part": ("send", "keep"), "grad": ("grad",)}.get(self.kind, ())

    def place(self, g):
        nx, ny, _ = self.shape
        x, y = (self.piece * n if self.cut == line else 0 for line, n in enumerate((nx, ny)))
        return (pl.ds(pl.multiple_of(x + g * GROUP, GROUP), GROUP), pl.ds(y, ny))

    def step(self, r, x, n, rows, product):
        kind = self.kind
        at = (x, rows)

        there = (self.piece * self.shape[0] + x if self.cut == 0 else x, rows)

        def get(key):
            return r[key + "_here"][at] if key in self.reads() else r[key][there]

        def put(key, value):
            if key in self.writes():
                r[key + "_here"][at] = value
            else:
                r[key][there] = value

        if kind == "exp":
            return jnp.exp(get("warm"))
        if kind == "none":
            return product
        if kind == "dual":
            value = jnp.exp(get("inputs")) / product
            put("d", value)
            return value
        if kind == "grad":
            put("grad", get("d") * product)
            return None
        scale = r["weights"][0]
        half = self.shape[2] // 2
        first = lax.axis_index("inp") == 0
        if kind == "part":
            part = scale * (get("warm") + jnp.log(product))
            put("t", product)
            left, right = part[:, :half], part[:, half:]
            put("keep", jnp.where(first, left, right))
            put("send", jnp.where(first, right, left))
            return None
        own, far = get("cot"), get("far")
        cot = jnp.concatenate([jnp.where(first, own, far), jnp.where(first, far, own)], axis=1)
        return scale * cot / get("t")

    def tiles(self, body):
        def tile_body(tile, carry):
            body(pl.ds(pl.multiple_of(tile * SUB, SUB), SUB))
            return carry

        lax.fori_loop(0, self.shape[1] // SUB, tile_body, 0)

    def finish_x(self, r, x0, reach):
        span = BLOCK * reach

        def sums(ref, rows, put):
            for q in range(0, GROUP, BLOCK):
                window = {m: ref[HALO + x0 + m, rows] for m in range(q - span, q + BLOCK + span)}
                for n in range(q, q + BLOCK):
                    put(n, x_sum(window.get, n, reach))

        def body(rows):
            def put(n, product):
                if self.finish == BOTH:
                    r["work"][n, rows] = product
                    return
                value = self.step(r, x0 + n, n, rows, product)
                if value is not None:
                    r["work"][n, rows] = value

            sums(r["u_ext"], rows, put)

        self.tiles(body)
        if self.finish == BOTH:
            for swap in range(2):
                rows = pl.ds(swap * HALO, HALO)

                def put_edge(n, product):
                    r["edge"][n, rows] = product

                sums(r["y_ext"], rows, put_edge)

    def group(self, r, g):
        nx, ny, nz = self.shape
        groups = nx // GROUP
        work, out = r["work"], r.get("u_out")
        x0 = pl.multiple_of(g * GROUP, GROUP)
        everything = pl.ds(0, ny)

        def finish_y(n):
            if self.finish == BOTH:
                return y_product(r["ky"], work[n], r["edge"][n])
            x = x0 + n
            return y_product(r["ky"], r["u"][x], jnp.concatenate([r["even"][x], r["odd"][x]], axis=0))

        if self.finish in (0, BOTH):
            for reach in (1, 2):
                pl.when(r["reach"][0] == reach)(lambda: self.finish_x(r, x0, reach))
        if self.finish == 0:
            if 1 in self.start:
                for n in range(GROUP):
                    work[n] = y_product(r["ky0"], work[n])
        elif 0 in self.start:
            if self.finish == 1:
                for n in range(GROUP):
                    work[n] = finish_y(n)

            def body(rows):
                for q in range(0, GROUP, BLOCK):
                    planes = {}
                    for n in range(q, q + BLOCK):
                        product = work[n, rows] if self.finish == 1 else None
                        planes[n] = self.step(r, x0 + n, n, rows, product)
                    for n in range(q, q + BLOCK):
                        work[n, rows] = x_sum(planes.get, n, 0)

            self.tiles(body)
        else:
            for n in range(GROUP):
                product = finish_y(n) if self.finish in (1, BOTH) else None
                value = self.step(r, x0 + n, n, everything, product)
                if value is not None:
                    work[n] = y_product(r["ky0"], value) if 1 in self.start else value
        shift = HALO if self.send in (0, BOTH) else 0
        if 2 in self.start:
            product = z_product(work[...].reshape(GROUP * ny, nz), r["kz"])
            out[pl.ds(x0 + shift, GROUP)] = product.reshape(GROUP, ny, nz)
        if self.send in (1, BOTH):
            names = ("y_even_out", "y_odd_out") if self.send == BOTH else ("even_out", "odd_out")
            for swap, name in enumerate(names):
                r[name][pl.ds(x0, GROUP)] = out[pl.ds(x0 + shift, GROUP), edge(1, swap, ny)]

    def body(self, r):
        groups = self.shape[0] // GROUP
        planes = lambda g: pl.ds(pl.multiple_of(g * GROUP, GROUP), GROUP)

        reads, writes = self.reads(), self.writes()

        def load(n, g):
            source = r[reads[n]]
            source = source.at[self.place(g)]
            return pltpu.make_async_copy(source, r[reads[n] + "_here"].at[planes(g)], r["sems"].at[n, g])

        def save(n, g):
            target = r[writes[n]]
            target = target.at[self.place(g)]
            sem = r["sems"].at[len(reads) + n, g]
            return pltpu.make_async_copy(r[writes[n] + "_here"].at[planes(g)], target, sem)

        for g in range(groups):
            for n in range(len(reads)):
                load(n, g).start()
        if self.fills:
            fill_z(r["kz"], r["reach"][2])
            if "ky" in r:
                fill_y(r["ky"], r["reach"][1], HALO)
            if "ky0" in r:
                fill_y(r["ky0"], 0, 0)
        if self.finish in (0, BOTH):
            nx = self.shape[0]
            ends = [edge(0, swap, nx + 2 * HALO) for swap in range(2)]
            for end, name in zip(ends, ("even", "odd")):
                r["u_ext"][end] = r[name][...]
            if self.finish == BOTH:
                for swap, name in enumerate(("even", "odd")):
                    rows = pl.ds(swap * HALO, HALO)
                    r["y_ext"][HALO : HALO + nx, rows] = r["y_" + name][...]
                    for n, end in enumerate(ends):
                        r["y_ext"][end, rows] = r["corner_" + name][n * HALO : (n + 1) * HALO]

        def run(g, carry):
            for n in range(len(reads)):
                load(n, g).wait()
            self.group(r, g)
            for n in range(len(writes)):
                save(n, g).start()
            return carry

        lax.fori_loop(0, groups, run, 0)
        if self.send in (0, BOTH):
            for swap, name in enumerate(("even_out", "odd_out")):
                r[name][...] = r["u_out"][edge(0, swap, self.shape[0], HALO)]
        for g in range(groups):
            for n in range(len(writes)):
                save(n, g).wait()

    def __call__(self, name, **arrays):
        nx, ny, nz = self.shape
        whole = tuple(n * 2 if line == self.cut else n for line, n in enumerate(self.shape))
        outs = {}
        aliases = {}
        if self.kind == "dual":
            outs["d"] = whole
        if self.kind == "part":
            outs.update(send=(*whole[:2], nz // 2), keep=(*whole[:2], nz // 2), t=whole)
        if self.kind == "grad":
            outs["grad"] = whole
        for n, key in enumerate(arrays):
            if key.endswith("_in"):
                aliases[n] = list(outs).index(key[:-3])
        if self.start:
            outs["u_out"] = self.shape if self.send == 1 else (nx + 2 * HALO, ny, nz)
        if self.send in (0, BOTH):
            outs["even_out"] = outs["odd_out"] = (HALO, ny, nz)
        if self.send == 1:
            outs["even_out"] = outs["odd_out"] = (nx, HALO, nz)
        if self.send == BOTH:
            outs["y_even_out"] = outs["y_odd_out"] = (nx, HALO, nz)
        if self.finish in (0, BOTH):
            outs["u_ext"] = arrays["u"].shape
            aliases[list(arrays).index("u")] = list(outs).index("u_ext")
        if self.fills:
            outs.update(self.matrices())
        scratch = self.scratch()
        names = list(arrays) + list(outs) + list(scratch)
        operands, in_specs = [], []
        stage_reads = self.reads()
        for key, value in arrays.items():
            if key in ("weights", "reach"):
                in_specs.append(pl.BlockSpec(memory_space=pltpu.SMEM))
            elif key in INSIDE and key not in stage_reads:
                value = pltpu.with_memory_space_constraint(value, pltpu.VMEM)
                in_specs.append(pl.BlockSpec(memory_space=pltpu.VMEM))
            else:
                in_specs.append(pl.BlockSpec(memory_space=pl.ANY))
            operands.append(value)
        out_shape, out_specs = [], []
        for key, shape in outs.items():
            space = pltpu.VMEM if key in INSIDE else pltpu.HBM
            out_shape.append(space(shape, BF16 if key in MATRICES else F32))
            out_specs.append(pl.BlockSpec(memory_space=space))
        result = pl.pallas_call(
            lambda *refs: self.body(dict(zip(names, refs))),
            name=name,
            out_shape=out_shape,
            in_specs=in_specs,
            out_specs=out_specs,
            input_output_aliases=aliases,
            scratch_shapes=list(scratch.values()),
            compiler_params=pltpu.CompilerParams(vmem_limit_bytes=(10 if "sems" in scratch else 6) * 2**20),
            cost_estimate=COST,
        )(*operands)
        return dict(zip(outs, result))


def add_body(keep, arrived, after, out, total, sems):
    parts = sems.shape[0]
    step = total.shape[0] // parts
    copies = []
    for n in range(parts):
        planes = pl.ds(n * step, step)
        total[planes] = keep[planes] + arrived[planes]
        copies.append(pltpu.make_async_copy(total.at[planes], out.at[planes], sems.at[n]))
        copies[-1].start()
    for copy in copies:
        copy.wait()


def add(keep, arrived, after):
    in_vmem = [pltpu.with_memory_space_constraint(v, pltpu.VMEM) for v in (keep, arrived)]
    return pl.pallas_call(
        add_body,
        name="barycenter",
        out_shape=pltpu.HBM(keep.shape, F32),
        in_specs=[pl.BlockSpec(memory_space=space) for space in (pltpu.VMEM, pltpu.VMEM, pl.ANY)],
        out_specs=pl.BlockSpec(memory_space=pltpu.HBM),
        scratch_shapes=[pltpu.VMEM(keep.shape, F32), pltpu.SemaphoreType.DMA((4,))],
        compiler_params=pltpu.CompilerParams(vmem_limit_bytes=10 * 2**20),
        cost_estimate=COST,
    )(*in_vmem, after)


def neighbours(sizes, line, even, odd):
    made = []
    for first, value in enumerate((even, odd)):
        pairs = [(i, i + 1) for i in range(first, sizes[line] - 1, 2)]
        made.append(lax.ppermute(value, AXES[line], pairs + [(j, i) for i, j in pairs]))
    return made


def corner_body(even, odd, *outs):
    ny = even.shape[1]
    for swap, out in enumerate(outs):
        for n, ref in enumerate((even, odd)):
            out[pl.ds(n * HALO, HALO)] = ref[:, edge(1, swap, ny)]


def corners(even, odd):
    inside = pl.BlockSpec(memory_space=pltpu.VMEM)
    shape = (2 * HALO, HALO, even.shape[2])
    return pl.pallas_call(
        corner_body,
        name="corners",
        out_shape=[pltpu.VMEM(shape, F32)] * 2,
        in_specs=[inside] * 2,
        out_specs=[inside] * 2,
        compiler_params=pltpu.CompilerParams(vmem_limit_bytes=4 * 2**20),
        cost_estimate=COST,
    )(*(pltpu.with_memory_space_constraint(v, pltpu.VMEM) for v in (even, odd)))


def exchange(sizes, line, made):
    if line != BOTH:
        even, odd = neighbours(sizes, line, made["even_out"], made["odd_out"])
        return dict(u=made["u_out"], even=even, odd=odd)
    even, odd = neighbours(sizes, 0, made["even_out"], made["odd_out"])
    y_even, y_odd = neighbours(sizes, 1, made["y_even_out"], made["y_odd_out"])
    corner_even, corner_odd = neighbours(sizes, 1, *corners(even, odd))
    halos = (even, odd, y_even, y_odd, corner_even, corner_odd)
    return dict(zip(EDGES, halos), u=made["u_out"])


SWAP = [(0, 1), (1, 0)]


class Case:
    def __init__(self, sizes, line, shape):
        self.sizes = sizes
        self.cut = 0 if line == 0 else None
        self.pieces = (0, 1) if line == 0 else (0,)
        self.shape = shape
        self.sent, self.begin = ((1, (0, 2)), (0, (1, 2)), (BOTH, (2,)))[line]

    def run(self, matrices, n, name, kind, arrays, fills=False, **form):
        stage = Stage(self.shape, self.cut, n, kind, fills=fills, **form)
        made = stage(f"{name}_{n}", **arrays, **{key: matrices[key] for key in stage.needs()})
        if fills:
            matrices.update({key: made.pop(key) for key in stage.matrices()})
        return made

    def scalings(self, inputs, warm, weights, reach):
        matrices = {}
        begin = dict(start=self.begin, send=self.sent)
        made = {
            n: self.run(matrices, n, "scaling", "exp", dict(warm=warm, reach=reach), fills=n == 0, **begin)
            for n in self.pieces
        }
        arrays = {n: exchange(self.sizes, self.sent, made[n]) for n in made}
        whole = {}
        for n in self.pieces:
            given = dict(inputs=inputs, reach=reach, **arrays[n], **whole)
            made[n] = self.run(matrices, n, "dual", "dual", given, finish=self.sent, **begin)
            whole = dict(d_in=made[n]["d"])
        d = whole["d_in"]
        arrays = {n: exchange(self.sizes, self.sent, made[n]) for n in made}
        whole = {}
        for n in self.pieces:
            given = dict(warm=warm, weights=weights, reach=reach, **arrays[n], **whole)
            part = self.run(matrices, n, "partial", "part", given, finish=self.sent)
            whole = {key + "_in": part[key] for key in ("send", "keep", "t")}
        return part["send"], part["keep"], part["t"], d

    def gradient(self, weights, reach, cotangent, far, t, d):
        matrices, made = {}, {}
        for n in self.pieces:
            given = dict(t=t, weights=weights, far=far, cot=cotangent, reach=reach)
            form = dict(start=self.begin, send=self.sent, fills=n == 0)
            made[n] = self.run(matrices, n, "cotangent", "cot", given, **form)
        arrays = {n: exchange(self.sizes, self.sent, made[n]) for n in made}
        whole = {}
        for n in self.pieces:
            given = dict(d=d, reach=reach, **arrays[n], **whole)
            whole = dict(grad_in=self.run(matrices, n, "gradient", "grad", given, finish=self.sent)["grad"])
        return whole["grad_in"]


def per_device(sizes, log_inputs, warm_potential, bary_weights, band_reach, bary_cotangent):
    shape = log_inputs.shape[1:]
    line = jnp.sum(jnp.where(band_reach == 0, jnp.arange(3, dtype=jnp.int32), 0))
    cases = [Case(sizes, n, shape) for n in range(3)]
    inputs, warm = log_inputs.reshape(shape), warm_potential.reshape(shape)
    far = lax.ppermute(bary_cotangent, "inp", SWAP)
    send, keep, t, d = lax.switch(
        line, [case.scalings for case in cases], inputs, warm, bary_weights, band_reach
    )
    arrived = lax.ppermute(send, "inp", SWAP)
    grad = lax.switch(
        line, [case.gradient for case in cases], bary_weights, band_reach, bary_cotangent, far, t, d
    )
    return (add(keep, arrived, grad), grad[None])


def solution(mesh):
    sizes = (mesh.shape["pa"], mesh.shape["pb"])
    return jax.shard_map(
        functools.partial(per_device, sizes),
        mesh=mesh,
        in_specs=(
            P("inp", "pa", "pb", None),
            P("inp", "pa", "pb", None),
            P("inp"),
            P(),
            P("pa", "pb", "inp"),
        ),
        out_specs=(P("pa", "pb", "inp"), P("inp", "pa", "pb", None)),
        check_vma=False,
    )
```

profile of v0, /device:TPU:1, one launch (start us, length us, event | category | flops | bytes accessed | tf_op | source)
XLA Modules:
  0.0 98.7 jit_solution(4591502783935049407)
XLA Ops:
  0.6 2.1 %collective-permute-start.37 = (f32[64,64,128]{2,1,0:T(8,128)}, f32[64,64,128]{2,1,0:T(8,128)S(1)}, u32[]{:S(2)}, u32[]{:S(2)}) collective-permute-start(f32[64,64,128]{2,1,0:T(8,128)} %param.15), channel_id=1, source_target_pairs={{0,16},{16,0},{1,17},{17,1},{2,18},{18,2},{3,19},{19,3},{4,20},{20... | collective-permute-start | bytes 6291464 | tf_op jit(solution)/shard_map/ppermute | solution.py:539
  2.8 1.3 %fusion = s32[]{:T(128)} fusion(s32[3]{0:T(128)} %param.14), kind=kLoop, calls=%fused_computation.1 | loop fusion | flops 8 | bytes 16 | tf_op jit(solution)/shard_map/reduce_sum | solution.py:536
  4.7 49.0 %conditional.2 = (f32[64,64,128]{2,1,0:T(8,128)}, f32[64,64,128]{2,1,0:T(8,128)}, f32[64,64,256]{2,1,0:T(8,128)S(1)}, f32[64,64,256]{2,1,0:T(8,128)S(1)}) conditional(s32[]{:T(128)} %clamp.4, (f32[64,64,256]{2,1,0:T(8,128)}, s32[3]{0:T(128)}, f32[64,64,256]{2,1,0:T(8,128)}, f32[1]{0:T(128)}) %tuple.41, (f32[64,64,256]{2,1,0:T(8,128)}, ...), branch_computations={%region_1.2_spmd, %region_2.3_spmd, %region_3.4_spmd} | conditional | flops 6 | bytes 52429444 | solution.py:540
  4.7 0.0 copy-start.4
  4.7 0.0 copy-start.11
  4.8 6.8 %scaling_0.4 = (f32[80,64,256]{2,1,0:T(8,128)S(1)}, f32[8,64,256]{2,1,0:T(8,128)S(1)}, f32[8,64,256]{2,1,0:T(8,128)S(1)}, bf16[768,256]{1,0:T(8,128)(2,1)S(1)}, bf16[64,192]{1,0:T(8,128)(2,1)S(1)}) custom-call(f32[64,64,256]{2,1,0:T(8,128)} %get-tuple-element.90.refs_0_, s32[3]{0:T(128)} %get-tuple-element.92.refs_1_.refs_2_), custom_call_target="tpu_custom_call" | custom-call | flops 1 | bytes 1 | tf_op jit(solution)/shard_map/cond/branch_1_fun/scaling_0/pallas_call | solution.py:399
  11.5 1.0 %collective-permute-start.8 = (f32[8,64,256]{2,1,0:T(8,128)S(1)}, f32[8,64,256]{2,1,0:T(8,128)S(1)}, u32[]{:S(2)}, u32[]{:S(2)}) collective-permute-start(f32[8,64,256]{2,1,0:T(8,128)S(1)} %get-tuple-element.95), channel_id=1, source_target_pairs={{0,4},{8,12},{4,0},{12,8},{1,5},{9,13},{5,1},{13,9},{2,6},{10,14},... | collective-permute-start | bytes 1572872 | tf_op jit(solution)/shard_map/cond/branch_1_fun/ppermute | solution.py:444
  12.5 3.0 %collective-permute-start.9 = (f32[8,64,256]{2,1,0:T(8,128)S(1)}, f32[8,64,256]{2,1,0:T(8,128)S(1)}, u32[]{:S(2)}, u32[]{:S(2)}) collective-permute-start(f32[8,64,256]{2,1,0:T(8,128)S(1)} %get-tuple-element.96), channel_id=1, source_target_pairs={{4,8},{8,4},{5,9},{9,5},{6,10},{10,6},{7,11},{11,7},{20,24},{24,20... | collective-permute-start | bytes 1572872 | tf_op jit(solution)/shard_map/cond/branch_1_fun/ppermute | solution.py:444
  15.6 0.0 collective-permute-done.8.refs_3_
  15.6 7.7 %collective-permute-done.9.refs_4_ = f32[8,64,256]{2,1,0:T(8,128)S(1)} collective-permute-done((f32[8,64,256]{2,1,0:T(8,128)S(1)}, f32[8,64,256]{2,1,0:T(8,128)S(1)}, u32[]{:S(2)}, u32[]{:S(2)}) %collective-permute-start.9) | collective-permute-done | bytes 524320 | tf_op jit(solution)/shard_map/cond/branch_1_fun/ppermute | solution.py:444
  23.3 0.0 copy-done.4
  23.3 0.0 copy-done.11
  23.3 0.0 copy-start.1
  23.3 10.9 %dual_0.4 = (f32[64,64,256]{2,1,0:T(8,128)S(1)}, f32[80,64,256]{2,1,0:T(8,128)S(1)}, f32[8,64,256]{2,1,0:T(8,128)S(1)}, f32[8,64,256]{2,1,0:T(8,128)S(1)}, f32[80,64,256]{2,1,0:T(8,128)S(1)}) custom-call(f32[64,64,256]{2,1,0:T(8,128)S(1)} %copy-done.4, s32[3]{0:T(128)S(1)} %copy-done.11, ...), custom_call_target="tpu_custom_call", output_to_operand_aliasing={{4}: (2, {})} | custom-call | flops 1 | bytes 1 | tf_op jit(solution)/shard_map/cond/branch_1_fun/dual_0/pallas_call | solution.py:399
  34.3 0.1 collective-permute-start.10
  34.4 2.7 %collective-permute-start.11 = (f32[8,64,256]{2,1,0:T(8,128)S(1)}, f32[8,64,256]{2,1,0:T(8,128)S(1)}, u32[]{:S(2)}, u32[]{:S(2)}) collective-permute-start(f32[8,64,256]{2,1,0:T(8,128)S(1)} %get-tuple-element.101), channel_id=1, source_target_pairs={{4,8},{8,4},{5,9},{9,5},{6,10},{10,6},{7,11},{11,7},{20,24},{24,20... | collective-permute-start | bytes 1572872 | tf_op jit(solution)/shard_map/cond/branch_1_fun/ppermute | solution.py:444
  37.1 0.0 collective-permute-done.10.refs_4_
  37.1 8.0 %collective-permute-done.11.refs_5_ = f32[8,64,256]{2,1,0:T(8,128)S(1)} collective-permute-done((f32[8,64,256]{2,1,0:T(8,128)S(1)}, f32[8,64,256]{2,1,0:T(8,128)S(1)}, u32[]{:S(2)}, u32[]{:S(2)}) %collective-permute-start.11) | collective-permute-done | bytes 524320 | tf_op jit(solution)/shard_map/cond/branch_1_fun/ppermute | solution.py:444
  45.2 0.0 copy-done.1
  45.2 8.5 %partial_0.4 = (f32[64,64,128]{2,1,0:T(8,128)}, f32[64,64,128]{2,1,0:T(8,128)}, f32[64,64,256]{2,1,0:T(8,128)S(1)}, f32[80,64,256]{2,1,0:T(8,128)S(1)}) custom-call(f32[64,64,256]{2,1,0:T(8,128)S(1)} %copy-done.1, f32[1]{0:T(128)} %get-tuple-element.91.refs_1_, s32[3]{0:T(128)S(1)} %copy-done.11, ...), custom_call_target="tpu_custom_call", output_to_operand_aliasing={{3}: (3, {})} | custom-call | flops 1 | bytes 1 | tf_op jit(solution)/shard_map/cond/branch_1_fun/partial_0/pallas_call | solution.py:399
  53.7 0.1 collective-permute-start.36
  53.8 0.0 collective-permute-done.37
  53.8 25.9 %conditional.3 = (f32[64,64,256]{2,1,0:T(8,128)}) conditional(s32[]{:T(128)} %clamp.4, (f32[64,64,256]{2,1,0:T(8,128)S(1)}, f32[1]{0:T(128)}, f32[64,64,128]{2,1,0:T(8,128)S(1)}, f32[64,64,128]{2,1,0:T(8,128)}, s32[3]{0:T(128)}, /*index=5*/f32[64,64,256]{2,1,0:T(8,128)S(1)}) %tuple.30, (f32[64,64,256]{2,1,0:T(8,128)S(1)}, ...), branch_computations={%region_4.5_spmd, %region_5.6_spmd, %region_6.7_spmd} | conditional | flops 4 | bytes 17826144 | solution.py:544
  54.0 0.0 copy-start.7
  54.0 1.6 %copy-done.7 = f32[64,64,128]{2,1,0:T(8,128)S(1)} copy-done((f32[64,64,128]{2,1,0:T(8,128)S(1)}, f32[64,64,128]{2,1,0:T(8,128)}, u32[]{:S(2)}) %copy-start.7) | copy-done | bytes 2097176 | tf_op jit(solution)/shard_map/cond
  55.6 0.0 copy-start.14
  55.6 6.2 %cotangent_0.4 = (f32[80,64,256]{2,1,0:T(8,128)S(1)}, f32[8,64,256]{2,1,0:T(8,128)S(1)}, f32[8,64,256]{2,1,0:T(8,128)S(1)}, bf16[768,256]{1,0:T(8,128)(2,1)}, bf16[64,192]{1,0:T(8,128)(2,1)}) custom-call(f32[64,64,256]{2,1,0:T(8,128)S(1)} %get-tuple-element.146.refs_0_, f32[1]{0:T(128)} %get-tuple-element.147.refs_1_, ...), custom_call_target="tpu_custom_call" | custom-call | flops 1 | bytes 1 | tf_op jit(solution)/shard_map/cond/branch_1_fun/cotangent_0/pallas_call | solution.py:399
  61.8 0.0 collective-permute-start.28
  61.8 2.7 %collective-permute-start.29 = (f32[8,64,256]{2,1,0:T(8,128)S(1)}, f32[8,64,256]{2,1,0:T(8,128)S(1)}, u32[]{:S(2)}, u32[]{:S(2)}) collective-permute-start(f32[8,64,256]{2,1,0:T(8,128)S(1)} %get-tuple-element.152), channel_id=1, source_target_pairs={{4,8},{8,4},{5,9},{9,5},{6,10},{10,6},{7,11},{11,7},{20,24},{24,20... | collective-permute-start | bytes 1572872 | tf_op jit(solution)/shard_map/cond/branch_1_fun/ppermute | solution.py:444
  64.5 0.0 collective-permute-done.28.refs_3_
  64.5 8.2 %collective-permute-done.29.refs_4_ = f32[8,64,256]{2,1,0:T(8,128)S(1)} collective-permute-done((f32[8,64,256]{2,1,0:T(8,128)S(1)}, f32[8,64,256]{2,1,0:T(8,128)S(1)}, u32[]{:S(2)}, u32[]{:S(2)}) %collective-permute-start.29) | collective-permute-done | bytes 524320 | tf_op jit(solution)/shard_map/cond/branch_1_fun/ppermute | solution.py:444
  72.7 0.0 copy-done.14
  72.7 7.0 %gradient_0.4 = (f32[64,64,256]{2,1,0:T(8,128)}, f32[80,64,256]{2,1,0:T(8,128)S(1)}) custom-call(f32[64,64,256]{2,1,0:T(8,128)S(1)} %get-tuple-element.144.refs_0_, s32[3]{0:T(128)S(1)} %copy-done.14, f32[80,64,256]{2,1,0:T(8,128)S(1)} %get-tuple-element.150.refs_2_, ...), custom_call_target="tpu_custom_call", output_to_operand_aliasing={{1}: (2, {})} | custom-call | flops 1 | bytes 1 | tf_op jit(solution)/shard_map/cond/branch_1_fun/gradient_0/pallas_call | solution.py:399
  79.8 14.2 %collective-permute-done.36.arrived = f32[64,64,128]{2,1,0:T(8,128)} collective-permute-done((f32[64,64,128]{2,1,0:T(8,128)}, f32[64,64,128]{2,1,0:T(8,128)}, u32[]{:S(2)}, u32[]{:S(2)}) %collective-permute-start.36) | collective-permute-done | bytes 2097184 | tf_op jit(solution)/shard_map/ppermute | solution.py:543
  93.9 0.0 copy-start.9
  93.9 1.6 %copy-done.9 = f32[64,64,128]{2,1,0:T(8,128)S(1)} copy-done((f32[64,64,128]{2,1,0:T(8,128)S(1)}, f32[64,64,128]{2,1,0:T(8,128)}, u32[]{:S(2)}) %copy-start.9) | copy-done | bytes 2097176
  95.5 3.0 %barycenter.1 = f32[64,64,128]{2,1,0:T(8,128)} custom-call(f32[64,64,128]{2,1,0:T(8,128)S(1)} %copy-done.9, f32[64,64,128]{2,1,0:T(8,128)} %collective-permute-done.36.arrived, f32[64,64,256]{2,1,0:T(8,128)} %get-tuple-element.191.after), custom_call_target="tpu_custom_call" | custom-call | flops 1 | bytes 1 | tf_op jit(solution)/shard_map/barycenter/pallas_call | solution.py:428
Async XLA Ops:
  0.6 53.2 %collective-permute-start.37 = (f32[64,64,128]{2,1,0:T(8,128)}, f32[64,64,128]{2,1,0:T(8,128)S(1)}, u32[]{:S(2)}, u32[]{:S(2)}) collective-permute-start(f32[64,64,128]{2,1,0:T(8,128)} %param.15), channel_id=1, source_target_pairs={{0,16},{16,0},{1,17},{17,1},{2,18},{18,2},{3,19},{19,3},{4,20},{20... | collective-permute-start | bytes 6291464 | tf_op jit(solution)/shard_map/ppermute | solution.py:539
  4.7 18.6 %copy-start.4 = (f32[64,64,256]{2,1,0:T(8,128)S(1)}, f32[64,64,256]{2,1,0:T(8,128)}, u32[]{:S(2)}) copy-start(f32[64,64,256]{2,1,0:T(8,128)} %get-tuple-element.93.refs_0_) | copy-start | bytes 12582916 | tf_op jit(solution)/shard_map/cond
  4.7 18.6 %copy-start.11 = (s32[3]{0:T(128)S(1)}, s32[3]{0:T(128)}, u32[]{:S(2)}) copy-start(s32[3]{0:T(128)} %get-tuple-element.92.refs_1_.refs_2_) | copy-start | bytes 40 | tf_op jit(solution)/shard_map/cond
  11.5 4.1 %collective-permute-start.8 = (f32[8,64,256]{2,1,0:T(8,128)S(1)}, f32[8,64,256]{2,1,0:T(8,128)S(1)}, u32[]{:S(2)}, u32[]{:S(2)}) collective-permute-start(f32[8,64,256]{2,1,0:T(8,128)S(1)} %get-tuple-element.95), channel_id=1, source_target_pairs={{0,4},{8,12},{4,0},{12,8},{1,5},{9,13},{5,1},{13,9},{2,6},{10,14},... | collective-permute-start | bytes 1572872 | tf_op jit(solution)/shard_map/cond/branch_1_fun/ppermute | solution.py:444
  12.5 10.8 %collective-permute-start.9 = (f32[8,64,256]{2,1,0:T(8,128)S(1)}, f32[8,64,256]{2,1,0:T(8,128)S(1)}, u32[]{:S(2)}, u32[]{:S(2)}) collective-permute-start(f32[8,64,256]{2,1,0:T(8,128)S(1)} %get-tuple-element.96), channel_id=1, source_target_pairs={{4,8},{8,4},{5,9},{9,5},{6,10},{10,6},{7,11},{11,7},{20,24},{24,20... | collective-permute-start | bytes 1572872 | tf_op jit(solution)/shard_map/cond/branch_1_fun/ppermute | solution.py:444
  23.3 21.8 %copy-start.1 = (f32[64,64,256]{2,1,0:T(8,128)S(1)}, f32[64,64,256]{2,1,0:T(8,128)}, u32[]{:S(2)}) copy-start(f32[64,64,256]{2,1,0:T(8,128)} %get-tuple-element.90.refs_0_) | copy-start | bytes 12582916 | tf_op jit(solution)/shard_map/cond
  34.3 2.8 %collective-permute-start.10 = (f32[8,64,256]{2,1,0:T(8,128)S(1)}, f32[8,64,256]{2,1,0:T(8,128)S(1)}, u32[]{:S(2)}, u32[]{:S(2)}) collective-permute-start(f32[8,64,256]{2,1,0:T(8,128)S(1)} %get-tuple-element.100), channel_id=1, source_target_pairs={{0,4},{8,12},{4,0},{12,8},{1,5},{9,13},{5,1},{13,9},{2,6},{10,14},... | collective-permute-start | bytes 1572872 | tf_op jit(solution)/shard_map/cond/branch_1_fun/ppermute | solution.py:444
  34.4 10.8 %collective-permute-start.11 = (f32[8,64,256]{2,1,0:T(8,128)S(1)}, f32[8,64,256]{2,1,0:T(8,128)S(1)}, u32[]{:S(2)}, u32[]{:S(2)}) collective-permute-start(f32[8,64,256]{2,1,0:T(8,128)S(1)} %get-tuple-element.101), channel_id=1, source_target_pairs={{4,8},{8,4},{5,9},{9,5},{6,10},{10,6},{7,11},{11,7},{20,24},{24,20... | collective-permute-start | bytes 1572872 | tf_op jit(solution)/shard_map/cond/branch_1_fun/ppermute | solution.py:444
  53.7 40.2 %collective-permute-start.36 = (f32[64,64,128]{2,1,0:T(8,128)}, f32[64,64,128]{2,1,0:T(8,128)}, u32[]{:S(2)}, u32[]{:S(2)}) collective-permute-start(f32[64,64,128]{2,1,0:T(8,128)} %get-tuple-element.176), channel_id=1, source_target_pairs={{0,16},{16,0},{1,17},{17,1},{2,18},{18,2},{3,19},{19,3},{4,20},{20... | collective-permute-start | bytes 6291464 | tf_op jit(solution)/shard_map/ppermute | solution.py:543
  54.0 1.6 %copy-start.7 = (f32[64,64,128]{2,1,0:T(8,128)S(1)}, f32[64,64,128]{2,1,0:T(8,128)}, u32[]{:S(2)}) copy-start(f32[64,64,128]{2,1,0:T(8,128)} %get-tuple-element.149.refs_3_) | copy-start | bytes 6291460 | tf_op jit(solution)/shard_map/cond
  55.6 17.1 %copy-start.14 = (s32[3]{0:T(128)S(1)}, s32[3]{0:T(128)}, u32[]{:S(2)}) copy-start(s32[3]{0:T(128)} %get-tuple-element.145.refs_4_.refs_1_) | copy-start | bytes 40 | tf_op jit(solution)/shard_map/cond
  61.8 2.7 %collective-permute-start.28 = (f32[8,64,256]{2,1,0:T(8,128)S(1)}, f32[8,64,256]{2,1,0:T(8,128)S(1)}, u32[]{:S(2)}, u32[]{:S(2)}) collective-permute-start(f32[8,64,256]{2,1,0:T(8,128)S(1)} %get-tuple-element.151), channel_id=1, source_target_pairs={{0,4},{8,12},{4,0},{12,8},{1,5},{9,13},{5,1},{13,9},{2,6},{10,14},... | collective-permute-start | bytes 1572872 | tf_op jit(solution)/shard_map/cond/branch_1_fun/ppermute | solution.py:444
  61.8 10.9 %collective-permute-start.29 = (f32[8,64,256]{2,1,0:T(8,128)S(1)}, f32[8,64,256]{2,1,0:T(8,128)S(1)}, u32[]{:S(2)}, u32[]{:S(2)}) collective-permute-start(f32[8,64,256]{2,1,0:T(8,128)S(1)} %get-tuple-element.152), channel_id=1, source_target_pairs={{4,8},{8,4},{5,9},{9,5},{6,10},{10,6},{7,11},{11,7},{20,24},{24,20... | collective-permute-start | bytes 1572872 | tf_op jit(solution)/shard_map/cond/branch_1_fun/ppermute | solution.py:444
  93.9 1.6 %copy-start.9 = (f32[64,64,128]{2,1,0:T(8,128)S(1)}, f32[64,64,128]{2,1,0:T(8,128)}, u32[]{:S(2)}) copy-start(f32[64,64,128]{2,1,0:T(8,128)} %get-tuple-element.175.keep) | copy-start | bytes 6291460
where the time goes:
time: 99.3 us; the launch traced here: 98.7 us
  Pallas kernels  42.5 us (43%)
  waiting for transfers between devices  38.1 us (38%)
  starting transfers between devices  11.8 us (12%)
  local copies, waits for them, and re-layouts  3.2 us (3%)
  between operations  1.48 us (1%)
  other arithmetic  1.29 us (1%)
    pallas_call x5, Pallas kernels, __call__(): pl.pallas_call(lambda *refs: self.body(dict(zip(names, refs))), name=name...  39.5 us
    ppermute x6, waiting for transfers between devices, neighbours(): lax.ppermute(value, AXES[line], pairs + [(j, i) for i, j in pairs])  24 us
    ppermute x1, waiting for transfers between devices, per_device(): arrived = lax.ppermute(send, 'inp', SWAP)  14.2 us
    ppermute x6, starting transfers between devices, neighbours(): lax.ppermute(value, AXES[line], pairs + [(j, i) for i, j in pairs])  9.55 us
    pallas_call x1, Pallas kernels, add(): pl.pallas_call(add_body, name='barycenter', out_shape=pltpu.HBM(keep.shap...  2.99 us
    ppermute x1, starting transfers between devices, per_device(): far = lax.ppermute(bary_cotangent, 'inp', SWAP)  2.13 us
  transfers between devices with their start and end apart: 8, of which 4 were waited for; matrix products, arithmetic and copies ran while one was open for 1% of the time, Pallas kernels for 40%

commit v1 on v0

--- a/solution.py
+++ b/solution.py
@@ -14,6 +14,7 @@
 SIGMA = 3.0
 SUB = 8
 GROUP = 8
+SLOTS = 4
 F32 = jnp.float32
 BF16 = jnp.bfloat16
 
@@ -46,8 +47,8 @@
     return lax.rem(lax.axis_index(AXES[line]), 2)
 
 
-def edge(line, swap, size, first=0):
-    return pl.ds(pl.multiple_of(first + jnp.where(parity(line) == swap, size - HALO, 0), HALO), HALO)
+def edge(line, swap, size):
+    return pl.ds(pl.multiple_of(jnp.where(parity(line) == swap, size - HALO, 0), HALO), HALO)
 
 
 def iotas(shape):
@@ -114,13 +115,13 @@
 
 MATRICES = ("kz", "ky", "ky0")
 EDGES = ("even", "odd", "y_even", "y_odd", "corner_even", "corner_odd")
-INSIDE = ("warm", "inputs", "t", "d", "t_in", "d_in", "far", "cot", "u", "u_out", "u_ext", *EDGES, *(edge + "_out" for edge in EDGES), *MATRICES)
+INSIDE = ("warm", "inputs", "d", "far", "u", "u_out", "u_out_in", *EDGES, *(edge + "_out" for edge in EDGES), *MATRICES)
 BOTH = (0, 1)
 COST = pl.CostEstimate(flops=1, bytes_accessed=1, transcendentals=0)
 
 
 class Stage:
-    def __init__(self, shape, cut, piece, kind, finish=None, start=(), send=None, fills=False):
+    def __init__(self, shape, cut, piece, kind, finish=None, start=(), send=None, fills=False, part="all"):
         self.cut = cut
         self.piece = piece
         self.shape = tuple(n // 2 if line == cut else n for line, n in enumerate(shape))
@@ -129,6 +130,8 @@
         self.start = start
         self.send = send
         self.fills = fills
+        self.part = part
+        self.groups = self.shape[0] // GROUP
 
     def matrices(self):
         nx, ny, nz = self.shape
@@ -148,22 +151,27 @@
     def scratch(self):
         nx, ny, nz = self.shape
         items = {"work": pltpu.VMEM((GROUP, ny, nz), F32)}
+        if self.finish == 0 and self.part != "inner":
+            items["sides"] = pltpu.VMEM((2 * HALO, ny, nz), F32)
         if self.finish == BOTH:
             items["edge"] = pltpu.VMEM((GROUP, 2 * HALO, nz), F32)
             items["y_ext"] = pltpu.VMEM((nx + 2 * HALO, 2 * HALO, nz), F32)
         for key in self.reads() + self.writes():
-            halved = key in ("cot", "far", "send", "keep")
-            items[key + "_here"] = pltpu.VMEM((nx, ny, nz // 2 if halved else nz), F32)
+            halved = key in ("cot", "send", "keep")
+            depth = nx if key in self.reads() else SLOTS * GROUP
+            items[key + "_here"] = pltpu.VMEM((depth, ny, nz // 2 if halved else nz), F32)
         streams = len(self.reads() + self.writes())
         if streams:
             items["sems"] = pltpu.SemaphoreType.DMA((streams, nx // GROUP))
         return items
 
     def reads(self):
-        return ("warm",) if self.kind == "exp" and self.piece == 0 else ()
+        if self.kind == "cot":
+            return ("t", "cot")
+        return ("warm",) if self.kind == "exp" and self.piece == 0 and self.part != "inner" else ()
 
     def writes(self):
-        return {"part": ("send", "keep"), "grad": ("grad",)}.get(self.kind, ())
+        return {"dual": ("d",), "part": ("send", "keep", "t"), "grad": ("grad",)}.get(self.kind, ())
 
     def place(self, g):
         nx, ny, _ = self.shape
@@ -181,7 +189,7 @@
 
         def put(key, value):
             if key in self.writes():
-                r[key + "_here"][at] = value
+                r[key + "_here"][r["slot"] * GROUP + n, rows] = value
             else:
                 r[key][there] = value
 
@@ -217,52 +225,67 @@
 
         lax.fori_loop(0, self.shape[1] // SUB, tile_body, 0)
 
-    def finish_x(self, r, x0, reach):
+    def x_sums(self, plane, reach, put):
         span = BLOCK * reach
-
-        def sums(ref, rows, put):
-            for q in range(0, GROUP, BLOCK):
-                window = {m: ref[HALO + x0 + m, rows] for m in range(q - span, q + BLOCK + span)}
-                for n in range(q, q + BLOCK):
-                    put(n, x_sum(window.get, n, reach))
-
+        for q in range(0, GROUP, BLOCK):
+            window = {m: plane(m) for m in range(q - span, q + BLOCK + span)}
+            for n in range(q, q + BLOCK):
+                put(n, x_sum(window.get, n, reach))
+
+    def finish_x(self, r, x0, reach, first, last):
         def body(rows):
+            def plane(m):
+                if m < 0 and first:
+                    return r["sides"][HALO + m, rows]
+                if m >= GROUP and last:
+                    return r["sides"][HALO + m - GROUP, rows]
+                return r["u"][x0 + m, rows]
+
             def put(n, product):
-                if self.finish == BOTH:
-                    r["work"][n, rows] = product
-                    return
                 value = self.step(r, x0 + n, n, rows, product)
-                if value is not None:
+                if value is not None and self.start:
                     r["work"][n, rows] = value
-
-            sums(r["u_ext"], rows, put)
+                elif value is not None:
+                    r["u_out"][x0 + n, rows] = value
+
+            self.x_sums(plane, reach, put)
 
         self.tiles(body)
-        if self.finish == BOTH:
-            for swap in range(2):
-                rows = pl.ds(swap * HALO, HALO)
-
-                def put_edge(n, product):
-                    r["edge"][n, rows] = product
-
-                sums(r["y_ext"], rows, put_edge)
+
+    def edge_sums(self, r, x0, reach):
+        for swap in range(2):
+            rows = pl.ds(swap * HALO, HALO)
+
+            def put(n, product):
+                r["edge"][n, rows] = product
+
+            self.x_sums(lambda m: r["y_ext"][HALO + x0 + m, rows], reach, put)
 
     def group(self, r, g):
         nx, ny, nz = self.shape
-        groups = nx // GROUP
         work, out = r["work"], r.get("u_out")
         x0 = pl.multiple_of(g * GROUP, GROUP)
         everything = pl.ds(0, ny)
 
         def finish_y(n):
+            x = x0 + n
             if self.finish == BOTH:
-                return y_product(r["ky"], work[n], r["edge"][n])
-            x = x0 + n
+                return y_product(r["ky"], r["u"][x], r["edge"][n])
             return y_product(r["ky"], r["u"][x], jnp.concatenate([r["even"][x], r["odd"][x]], axis=0))
 
-        if self.finish in (0, BOTH):
-            for reach in (1, 2):
-                pl.when(r["reach"][0] == reach)(lambda: self.finish_x(r, x0, reach))
+        for reach in (1, 2):
+            chosen = r["reach"][0] == reach
+            if self.finish == BOTH:
+                pl.when(chosen)(lambda: self.edge_sums(r, x0, reach))
+            if self.finish == 0:
+                last = self.groups - 1
+                if self.part != "inner":
+                    pl.when(chosen & (g == 0))(lambda: self.finish_x(r, x0, reach, True, last == 0))
+                    if last > 0:
+                        pl.when(chosen & (g == last))(lambda: self.finish_x(r, x0, reach, False, True))
+                if self.part != "outer" and last > 1:
+                    within = (g > 0) & (g < last)
+                    pl.when(chosen & within)(lambda: self.finish_x(r, x0, reach, False, False))
         if self.finish == 0:
             if 1 in self.start:
                 for n in range(GROUP):
@@ -288,17 +311,30 @@
                 value = self.step(r, x0 + n, n, everything, product)
                 if value is not None:
                     work[n] = y_product(r["ky0"], value) if 1 in self.start else value
-        shift = HALO if self.send in (0, BOTH) else 0
         if 2 in self.start:
             product = z_product(work[...].reshape(GROUP * ny, nz), r["kz"])
-            out[pl.ds(x0 + shift, GROUP)] = product.reshape(GROUP, ny, nz)
+            out[pl.ds(x0, GROUP)] = product.reshape(GROUP, ny, nz)
         if self.send in (1, BOTH):
             names = ("y_even_out", "y_odd_out") if self.send == BOTH else ("even_out", "odd_out")
             for swap, name in enumerate(names):
-                r[name][pl.ds(x0, GROUP)] = out[pl.ds(x0 + shift, GROUP), edge(1, swap, ny)]
+                r[name][pl.ds(x0, GROUP)] = out[pl.ds(x0, GROUP), edge(1, swap, ny)]
+
+    def complete(self, r, parts, planes):
+        if "u_out_in" not in r:
+            return
+        others = parts["inner" if self.part == "outer" else "outer"]
+
+        def copy(i, carry):
+            at = planes(others.start + others.step * i)
+            r["u_out"][at] = r["u_out_in"][at]
+            return carry
+
+        lax.fori_loop(0, len(others), copy, 0)
 
     def body(self, r):
-        groups = self.shape[0] // GROUP
+        last = self.groups - 1
+        parts = {"all": range(last + 1), "inner": range(1, last), "outer": range(0, last + 1, max(last, 1))}
+        groups = parts[self.part]
         planes = lambda g: pl.ds(pl.multiple_of(g * GROUP, GROUP), GROUP)
 
         reads, writes = self.reads(), self.writes()
@@ -308,13 +344,16 @@
             source = source.at[self.place(g)]
             return pltpu.make_async_copy(source, r[reads[n] + "_here"].at[planes(g)], r["sems"].at[n, g])
 
+        def slot(g):
+            return jnp.minimum(g, 1) if self.part == "outer" else lax.rem(g, SLOTS)
+
         def save(n, g):
             target = r[writes[n]]
             target = target.at[self.place(g)]
             sem = r["sems"].at[len(reads) + n, g]
-            return pltpu.make_async_copy(r[writes[n] + "_here"].at[planes(g)], target, sem)
-
-        for g in range(groups):
+            return pltpu.make_async_copy(r[writes[n] + "_here"].at[planes(slot(g))], target, sem)
+
+        for g in groups:
             for n in range(len(reads)):
                 load(n, g).start()
         if self.fills:
@@ -323,31 +362,34 @@
                 fill_y(r["ky"], r["reach"][1], HALO)
             if "ky0" in r:
                 fill_y(r["ky0"], 0, 0)
-        if self.finish in (0, BOTH):
-            nx = self.shape[0]
-            ends = [edge(0, swap, nx + 2 * HALO) for swap in range(2)]
-            for end, name in zip(ends, ("even", "odd")):
-                r["u_ext"][end] = r[name][...]
-            if self.finish == BOTH:
-                for swap, name in enumerate(("even", "odd")):
-                    rows = pl.ds(swap * HALO, HALO)
-                    r["y_ext"][HALO : HALO + nx, rows] = r["y_" + name][...]
-                    for n, end in enumerate(ends):
-                        r["y_ext"][end, rows] = r["corner_" + name][n * HALO : (n + 1) * HALO]
-
-        def run(g, carry):
+        nx = self.shape[0]
+        for swap, name in enumerate(("even", "odd")):
+            if "sides" in r:
+                r["sides"][edge(0, swap, 2 * HALO)] = r[name][...]
+            if "y_ext" in r:
+                rows = pl.ds(swap * HALO, HALO)
+                r["y_ext"][HALO : HALO + nx, rows] = r["y_" + name][...]
+                for n in range(2):
+                    corner = r["corner_" + name][n * HALO : (n + 1) * HALO]
+                    r["y_ext"][edge(0, n, nx + 2 * HALO), rows] = corner
+
+        def run(i, carry):
+            g = groups.start + groups.step * i
             for n in range(len(reads)):
                 load(n, g).wait()
-            self.group(r, g)
+            for n in range(len(writes) if len(groups) > SLOTS else 0):
+                pl.when(i >= SLOTS)(lambda: save(n, g - SLOTS).wait())
+            self.group(dict(r, slot=slot(g)), g)
             for n in range(len(writes)):
                 save(n, g).start()
             return carry
 
-        lax.fori_loop(0, groups, run, 0)
-        if self.send in (0, BOTH):
+        lax.fori_loop(0, len(groups), run, 0)
+        self.complete(r, parts, planes)
+        if "even_out" in r and self.send in (0, BOTH):
             for swap, name in enumerate(("even_out", "odd_out")):
-                r[name][...] = r["u_out"][edge(0, swap, self.shape[0], HALO)]
-        for g in range(groups):
+                r[name][...] = r["u_out"][edge(0, swap, nx)]
+        for g in groups[-SLOTS:]:
             for n in range(len(writes)):
                 save(n, g).wait()
 
@@ -362,22 +404,20 @@
             outs.update(send=(*whole[:2], nz // 2), keep=(*whole[:2], nz // 2), t=whole)
         if self.kind == "grad":
             outs["grad"] = whole
+        if self.start or self.kind == "none":
+            outs["u_out"] = self.shape
+        if self.part != "inner":
+            if self.send in (0, BOTH):
+                outs["even_out"] = outs["odd_out"] = (HALO, ny, nz)
+            if self.send == 1:
+                outs["even_out"] = outs["odd_out"] = (nx, HALO, nz)
+            if self.send == BOTH:
+                outs["y_even_out"] = outs["y_odd_out"] = (nx, HALO, nz)
+        if self.fills:
+            outs.update(self.matrices())
         for n, key in enumerate(arrays):
             if key.endswith("_in"):
                 aliases[n] = list(outs).index(key[:-3])
-        if self.start:
-            outs["u_out"] = self.shape if self.send == 1 else (nx + 2 * HALO, ny, nz)
-        if self.send in (0, BOTH):
-            outs["even_out"] = outs["odd_out"] = (HALO, ny, nz)
-        if self.send == 1:
-            outs["even_out"] = outs["odd_out"] = (nx, HALO, nz)
-        if self.send == BOTH:
-            outs["y_even_out"] = outs["y_odd_out"] = (nx, HALO, nz)
-        if self.finish in (0, BOTH):
-            outs["u_ext"] = arrays["u"].shape
-            aliases[list(arrays).index("u")] = list(outs).index("u_ext")
-        if self.fills:
-            outs.update(self.matrices())
         scratch = self.scratch()
         names = list(arrays) + list(outs) + list(scratch)
         operands, in_specs = [], []
@@ -393,7 +433,7 @@
             operands.append(value)
         out_shape, out_specs = [], []
         for key, shape in outs.items():
-            space = pltpu.VMEM if key in INSIDE else pltpu.HBM
+            space = pltpu.VMEM if key in INSIDE and key not in self.writes() else pltpu.HBM
             out_shape.append(space(shape, BF16 if key in MATRICES else F32))
             out_specs.append(pl.BlockSpec(memory_space=space))
         result = pl.pallas_call(
@@ -404,37 +444,44 @@
             out_specs=out_specs,
             input_output_aliases=aliases,
             scratch_shapes=list(scratch.values()),
-            compiler_params=pltpu.CompilerParams(vmem_limit_bytes=(10 if "sems" in scratch else 6) * 2**20),
+            compiler_params=pltpu.CompilerParams(vmem_limit_bytes=(14 if "sems" in scratch else 8) * 2**20),
             cost_estimate=COST,
         )(*operands)
         return dict(zip(outs, result))
 
 
-def add_body(keep, arrived, after, out, total, sems):
-    parts = sems.shape[0]
+def add_body(keep, arrived, after, out, left, right, total, sems):
+    parts = sems.shape[1]
     step = total.shape[0] // parts
-    copies = []
-    for n in range(parts):
-        planes = pl.ds(n * step, step)
-        total[planes] = keep[planes] + arrived[planes]
-        copies.append(pltpu.make_async_copy(total.at[planes], out.at[planes], sems.at[n]))
-        copies[-1].start()
-    for copy in copies:
+    planes = [pl.ds(n * step, step) for n in range(parts)]
+    loads = [
+        pltpu.make_async_copy(source.at[p], target.at[p], sems.at[m, n])
+        for n, p in enumerate(planes)
+        for m, (source, target) in enumerate(((keep, left), (arrived, right)))
+    ]
+    saves = [pltpu.make_async_copy(total.at[p], out.at[p], sems.at[2, n]) for n, p in enumerate(planes)]
+    for copy in loads:
+        copy.start()
+    for n, p in enumerate(planes):
+        loads[2 * n].wait()
+        loads[2 * n + 1].wait()
+        total[p] = left[p] + right[p]
+        saves[n].start()
+    for copy in saves:
         copy.wait()
 
 
 def add(keep, arrived, after):
-    in_vmem = [pltpu.with_memory_space_constraint(v, pltpu.VMEM) for v in (keep, arrived)]
     return pl.pallas_call(
         add_body,
         name="barycenter",
         out_shape=pltpu.HBM(keep.shape, F32),
-        in_specs=[pl.BlockSpec(memory_space=space) for space in (pltpu.VMEM, pltpu.VMEM, pl.ANY)],
+        in_specs=[pl.BlockSpec(memory_space=pl.ANY)] * 3,
         out_specs=pl.BlockSpec(memory_space=pltpu.HBM),
-        scratch_shapes=[pltpu.VMEM(keep.shape, F32), pltpu.SemaphoreType.DMA((4,))],
-        compiler_params=pltpu.CompilerParams(vmem_limit_bytes=10 * 2**20),
+        scratch_shapes=[pltpu.VMEM(keep.shape, F32)] * 3 + [pltpu.SemaphoreType.DMA((3, 4))],
+        compiler_params=pltpu.CompilerParams(vmem_limit_bytes=8 * 2**20),
         cost_estimate=COST,
-    )(*in_vmem, after)
+    )(keep, arrived, after)
 
 
 def neighbours(sizes, line, even, odd):
@@ -445,36 +492,33 @@
     return made
 
 
-def corner_body(even, odd, *outs):
+def corner_body(even, odd, after, *outs):
     ny = even.shape[1]
     for swap, out in enumerate(outs):
         for n, ref in enumerate((even, odd)):
             out[pl.ds(n * HALO, HALO)] = ref[:, edge(1, swap, ny)]
 
 
-def corners(even, odd):
+def corners(even, odd, after):
     inside = pl.BlockSpec(memory_space=pltpu.VMEM)
     shape = (2 * HALO, HALO, even.shape[2])
     return pl.pallas_call(
         corner_body,
         name="corners",
         out_shape=[pltpu.VMEM(shape, F32)] * 2,
-        in_specs=[inside] * 2,
+        in_specs=[inside] * 2 + [pl.BlockSpec(memory_space=pl.ANY)],
         out_specs=[inside] * 2,
         compiler_params=pltpu.CompilerParams(vmem_limit_bytes=4 * 2**20),
         cost_estimate=COST,
-    )(*(pltpu.with_memory_space_constraint(v, pltpu.VMEM) for v in (even, odd)))
+    )(*(pltpu.with_memory_space_constraint(v, pltpu.VMEM) for v in (even, odd)), after)
 
 
 def exchange(sizes, line, made):
     if line != BOTH:
-        even, odd = neighbours(sizes, line, made["even_out"], made["odd_out"])
-        return dict(u=made["u_out"], even=even, odd=odd)
-    even, odd = neighbours(sizes, 0, made["even_out"], made["odd_out"])
-    y_even, y_odd = neighbours(sizes, 1, made["y_even_out"], made["y_odd_out"])
-    corner_even, corner_odd = neighbours(sizes, 1, *corners(even, odd))
-    halos = (even, odd, y_even, y_odd, corner_even, corner_odd)
-    return dict(zip(EDGES, halos), u=made["u_out"])
+        return dict(zip(EDGES, neighbours(sizes, line, made["even_out"], made["odd_out"])))
+    x = neighbours(sizes, 0, made["even_out"], made["odd_out"])
+    y = neighbours(sizes, 1, made["y_even_out"], made["y_odd_out"])
+    return dict(zip(EDGES, (*x, *y)))
 
 
 SWAP = [(0, 1), (1, 0)]
@@ -486,6 +530,7 @@
         self.cut = 0 if line == 0 else None
         self.pieces = (0, 1) if line == 0 else (0,)
         self.shape = shape
+        self.groups = shape[0] // GROUP
         self.sent, self.begin = ((1, (0, 2)), (0, (1, 2)), (BOTH, (2,)))[line]
 
     def run(self, matrices, n, name, kind, arrays, fills=False, **form):
@@ -495,39 +540,66 @@
             matrices.update({key: made.pop(key) for key in stage.matrices()})
         return made
 
+    def begin_lines(self, matrices, n, name, kind, arrays, fills):
+        form = dict(start=self.begin, send=self.sent)
+        if self.sent != 0 or self.groups < 3:
+            return self.run(matrices, n, name, kind, arrays, fills=fills, **form)
+        made = self.run(matrices, n, name + "_outer", kind, arrays, fills=fills, part="outer", **form)
+        arrays = dict(arrays, u_out_in=made["u_out"])
+        made.update(self.run(matrices, n, name + "_inner", kind, arrays, part="inner", **form))
+        return made
+
+    def end_lines(self, matrices, n, name, kind, arrays, u, halos, **form):
+        if self.sent == 1:
+            return self.run(matrices, n, name, kind, dict(arrays, u=u, **halos), finish=1, **form)
+        x_halos = {key: halos.pop(key) for key in ("even", "odd")}
+        if self.sent == 0:
+            x_name, x_kind, x_form, given = name, kind, form, dict(arrays, u=u)
+        else:
+            x_name, x_kind, x_form, given = name + "_x", "none", {}, dict(reach=arrays["reach"], u=u)
+        whole, part = {}, "all"
+        if self.groups > 2:
+            made = self.run(matrices, n, x_name + "_inner", x_kind, given, finish=0, part="inner", **x_form)
+            whole, part = {key + "_in": made[key] for key in made}, "outer"
+        if self.sent == BOTH:
+            made = corners(*x_halos.values(), whole.get("u_out_in", u))
+            halos.update(zip(EDGES[4:], neighbours(self.sizes, 1, *made)))
+        given = dict(given, **whole, **x_halos)
+        made = self.run(matrices, n, f"{x_name}_{part}", x_kind, given, finish=0, part=part, **x_form)
+        if self.sent == 0:
+            return made
+        return self.run(matrices, n, name, kind, dict(arrays, u=made["u_out"], **halos), finish=BOTH, **form)
+
     def scalings(self, inputs, warm, weights, reach):
         matrices = {}
-        begin = dict(start=self.begin, send=self.sent)
-        made = {
-            n: self.run(matrices, n, "scaling", "exp", dict(warm=warm, reach=reach), fills=n == 0, **begin)
-            for n in self.pieces
-        }
-        arrays = {n: exchange(self.sizes, self.sent, made[n]) for n in made}
+        form = dict(start=self.begin, send=self.sent)
+        given = dict(warm=warm, reach=reach)
+        made = {n: self.begin_lines(matrices, n, "scaling", "exp", given, n == 0) for n in self.pieces}
+        halos = {n: exchange(self.sizes, self.sent, made[n]) for n in made}
         whole = {}
         for n in self.pieces:
-            given = dict(inputs=inputs, reach=reach, **arrays[n], **whole)
-            made[n] = self.run(matrices, n, "dual", "dual", given, finish=self.sent, **begin)
+            given = dict(inputs=inputs, reach=reach, **whole)
+            made[n] = self.end_lines(matrices, n, "dual", "dual", given, made[n]["u_out"], halos[n], **form)
             whole = dict(d_in=made[n]["d"])
         d = whole["d_in"]
-        arrays = {n: exchange(self.sizes, self.sent, made[n]) for n in made}
+        halos = {n: exchange(self.sizes, self.sent, made[n]) for n in made}
         whole = {}
         for n in self.pieces:
-            given = dict(warm=warm, weights=weights, reach=reach, **arrays[n], **whole)
-            part = self.run(matrices, n, "partial", "part", given, finish=self.sent)
+            given = dict(warm=warm, weights=weights, reach=reach, **whole)
+            part = self.end_lines(matrices, n, "partial", "part", given, made[n]["u_out"], halos[n])
             whole = {key + "_in": part[key] for key in ("send", "keep", "t")}
         return part["send"], part["keep"], part["t"], d
 
     def gradient(self, weights, reach, cotangent, far, t, d):
-        matrices, made = {}, {}
-        for n in self.pieces:
-            given = dict(t=t, weights=weights, far=far, cot=cotangent, reach=reach)
-            form = dict(start=self.begin, send=self.sent, fills=n == 0)
-            made[n] = self.run(matrices, n, "cotangent", "cot", given, **form)
-        arrays = {n: exchange(self.sizes, self.sent, made[n]) for n in made}
+        matrices = {}
+        given = dict(t=t, weights=weights, far=far, cot=cotangent, reach=reach)
+        made = {n: self.begin_lines(matrices, n, "cotangent", "cot", given, n == 0) for n in self.pieces}
+        halos = {n: exchange(self.sizes, self.sent, made[n]) for n in made}
         whole = {}
         for n in self.pieces:
-            given = dict(d=d, reach=reach, **arrays[n], **whole)
-            whole = dict(grad_in=self.run(matrices, n, "gradient", "grad", given, finish=self.sent)["grad"])
+            given = dict(d=d, reach=reach, **whole)
+            made[n] = self.end_lines(matrices, n, "gradient", "grad", given, made[n]["u_out"], halos[n])
+            whole = dict(grad_in=made[n]["grad"])
         return whole["grad_in"]
 
 

time: 99.3 us -> 117 us (1.18)
  the two profiles are of different devices: /device:TPU:1 before, /device:TPU:17 now
where the time goes in v1:
time: 117 us; the launch traced here: 116 us
  Pallas kernels  53.9 us (46%)
  waiting for transfers between devices  32.6 us (28%)
  starting transfers between devices  26.5 us (23%)
  between operations  1.46 us (1%)
  other arithmetic  1.29 us (1%)
    pallas_call x11, Pallas kernels, __call__(): pl.pallas_call(lambda *refs: self.body(dict(zip(names, refs))), name=name...  50.8 us
    ppermute x18, starting transfers between devices, neighbours(): lax.ppermute(value, AXES[line], pairs + [(j, i) for i, j in pairs])  24.9 us
    ppermute x18, waiting for transfers between devices, neighbours(): lax.ppermute(value, AXES[line], pairs + [(j, i) for i, j in pairs])  17.1 us
    ppermute x1, waiting for transfers between devices, per_device(): arrived = lax.ppermute(send, 'inp', SWAP)  15.5 us
    pallas_call x1, Pallas kernels, add(): pl.pallas_call(add_body, name='barycenter', out_shape=pltpu.HBM(keep.shap...  3.09 us
  transfers between devices with their start and end apart: 20, of which 11 were waited for; matrix products, arithmetic and copies ran while one was open for 1% of the time, Pallas kernels for 44%

profile of v1, /device:TPU:17, one launch (start us, length us, event | category | flops | bytes accessed | tf_op | source)
XLA Modules:
  0.0 116.3 jit_solution(13435495315664872392)
XLA Ops:
  0.6 1.3 %collective-permute-start.37 = (f32[64,64,128]{2,1,0:T(8,128)}, f32[64,64,128]{2,1,0:T(8,128)S(1)}, u32[]{:S(2)}, u32[]{:S(2)}) collective-permute-start(f32[64,64,128]{2,1,0:T(8,128)} %param.15), channel_id=1, source_target_pairs={{0,16},{16,0},{1,17},{17,1},{2,18},{18,2},{3,19},{19,3},{4,20},{20... | collective-permute-start | bytes 6291464 | tf_op jit(solution)/shard_map/ppermute | solution.py:611
  1.9 1.3 %fusion = s32[]{:T(128)} fusion(s32[3]{0:T(128)} %param.14), kind=kLoop, calls=%fused_computation.1 | loop fusion | flops 8 | bytes 16 | tf_op jit(solution)/shard_map/reduce_sum | solution.py:608
  3.9 61.3 %conditional.2 = (f32[64,64,128]{2,1,0:T(8,128)}, f32[64,64,128]{2,1,0:T(8,128)}, f32[64,64,256]{2,1,0:T(8,128)}, f32[64,64,256]{2,1,0:T(8,128)}) conditional(s32[]{:T(128)} %clamp.4, (f32[64,64,256]{2,1,0:T(8,128)}, s32[3]{0:T(128)}, f32[64,64,256]{2,1,0:T(8,128)}, f32[1]{0:T(128)}) %tuple.41, (f32[64,64,256]{2,1,0:T(8,128)}, ...), branch_computations={%region_1.2_spmd, %region_2.3_spmd, %region_3.4_spmd} | conditional | flops 9 | bytes 52429444 | solution.py:612
  3.9 0.0 copy-start.15
  3.9 5.1 %scaling_0.3 = (f32[64,64,256]{2,1,0:T(8,128)S(1)}, f32[8,64,256]{2,1,0:T(8,128)S(1)}, f32[8,64,256]{2,1,0:T(8,128)S(1)}, f32[64,8,256]{2,1,0:T(8,128)S(1)}, f32...) custom-call(f32[64,64,256]{2,1,0:T(8,128)} %get-tuple-element.111.refs_0_, ...), custom_call_target="tpu_custom_call" | custom-call | flops 1 | bytes 1 | tf_op jit(solution)/shard_map/cond/branch_2_fun/scaling_0/pallas_call | solution.py:439
  9.0 1.0 collective-permute-start.12
  10.1 3.0 %collective-permute-start.13 = (f32[8,64,256]{2,1,0:T(8,128)S(1)}, f32[8,64,256]{2,1,0:T(8,128)S(1)}, u32[]{:S(2)}, u32[]{:S(2)}) collective-permute-start(f32[8,64,256]{2,1,0:T(8,128)S(1)} %get-tuple-element.117), channel_id=1, source_target_pairs={{4,8},{8,4},{5,9},{9,5},{6,10},{10,6},{7,11},{11,7},{20,24},{24,20... | collective-permute-start | bytes 1572872 | tf_op jit(solution)/shard_map/cond/branch_2_fun/ppermute | solution.py:491
  13.1 1.3 %collective-permute-start.14 = (f32[64,8,256]{2,1,0:T(8,128)S(1)}, f32[64,8,256]{2,1,0:T(8,128)S(1)}, u32[]{:S(2)}, u32[]{:S(2)}) collective-permute-start(f32[64,8,256]{2,1,0:T(8,128)S(1)} %get-tuple-element.118), channel_id=1, source_target_pairs={{0,1},{2,3},{1,0},{3,2},{4,5},{6,7},{5,4},{7,6},{8,9},{10,11},{9,8... | collective-permute-start | bytes 1572872 | tf_op jit(solution)/shard_map/cond/branch_2_fun/ppermute | solution.py:491
  14.4 1.9 %collective-permute-start.15 = (f32[64,8,256]{2,1,0:T(8,128)S(1)}, f32[64,8,256]{2,1,0:T(8,128)S(1)}, u32[]{:S(2)}, u32[]{:S(2)}) collective-permute-start(f32[64,8,256]{2,1,0:T(8,128)S(1)} %get-tuple-element.119), channel_id=1, source_target_pairs={{1,2},{2,1},{5,6},{6,5},{9,10},{10,9},{13,14},{14,13},{17,18},{18,... | collective-permute-start | bytes 1572872 | tf_op jit(solution)/shard_map/cond/branch_2_fun/ppermute | solution.py:491
  16.4 4.6 %dual_x_inner_0.1.refs_2_.after = f32[64,64,256]{2,1,0:T(8,128)S(1)} custom-call(s32[3]{0:T(128)S(1)} %copy-done.15, f32[64,64,256]{2,1,0:T(8,128)S(1)} %get-tuple-element.115.refs_1_), custom_call_target="tpu_custom_call" | custom-call | flops 1 | bytes 1 | tf_op jit(solution)/shard_map/cond/branch_2_fun/dual_x_inner_0/pallas_call | solution.py:439
  21.0 1.2 %collective-permute-start.16 = (f32[16,8,256]{2,1,0:T(8,128)S(1)}, f32[16,8,256]{2,1,0:T(8,128)S(1)}, u32[]{:S(2)}, u32[]{:S(2)}) collective-permute-start(f32[16,8,256]{2,1,0:T(8,128)S(1)} %get-tuple-element.120), channel_id=1, source_target_pairs={{0,1},{2,3},{1,0},{3,2},{4,5},{6,7},{5,4},{7,6},{8,9},{10,11},{9,8... | collective-permute-start | bytes 393224 | tf_op jit(solution)/shard_map/cond/branch_2_fun/ppermute | solution.py:491
  22.2 2.5 %collective-permute-start.17 = (f32[16,8,256]{2,1,0:T(8,128)S(1)}, f32[16,8,256]{2,1,0:T(8,128)S(1)}, u32[]{:S(2)}, u32[]{:S(2)}) collective-permute-start(f32[16,8,256]{2,1,0:T(8,128)S(1)} %get-tuple-element.121), channel_id=1, source_target_pairs={{1,2},{2,1},{5,6},{6,5},{9,10},{10,9},{13,14},{14,13},{17,18},{18,... | collective-permute-start | bytes 393224 | tf_op jit(solution)/shard_map/cond/branch_2_fun/ppermute | solution.py:491
  24.7 2.4 %dual_x_outer_0.1.refs_2_ = f32[64,64,256]{2,1,0:T(8,128)S(1)} custom-call(s32[3]{0:T(128)S(1)} %copy-done.15, f32[64,64,256]{2,1,0:T(8,128)S(1)} %get-tuple-element.115.refs_1_, f32[64,64,256]{2,1,0:T(8,128)S(1)} %dual_x_inner_0.1.refs_2_.after, f32[8,64,256]{2,1,0:T(8,128)S(1)} %collective-permute-done.12.refs_3_.even, ...), custom_call_target="tpu_custom_call", output_to_operand_aliasing={{}: (2, {})} | custom-call | flops 1 | bytes 1 | tf_op jit(solution)/shard_map/cond/branch_2_fun/dual_x_outer_0/pallas_call | solution.py:439
  27.1 3.0 %collective-permute-done.15.refs_4_ = f32[64,8,256]{2,1,0:T(8,128)S(1)} collective-permute-done((f32[64,8,256]{2,1,0:T(8,128)S(1)}, f32[64,8,256]{2,1,0:T(8,128)S(1)}, u32[]{:S(2)}, u32[]{:S(2)}) %collective-permute-start.15) | collective-permute-done | bytes 524320 | tf_op jit(solution)/shard_map/cond/branch_2_fun/ppermute | solution.py:491
  30.1 1.4 %collective-permute-done.17.refs_6_ = f32[16,8,256]{2,1,0:T(8,128)S(1)} collective-permute-done((f32[16,8,256]{2,1,0:T(8,128)S(1)}, f32[16,8,256]{2,1,0:T(8,128)S(1)}, u32[]{:S(2)}, u32[]{:S(2)}) %collective-permute-start.17) | collective-permute-done | bytes 131104 | tf_op jit(solution)/shard_map/cond/branch_2_fun/ppermute | solution.py:491
  31.5 7.1 %dual_0.3 = (f32[64,64,256]{2,1,0:T(8,128)}, f32[64,64,256]{2,1,0:T(8,128)S(1)}, f32[8,64,256]{2,1,0:T(8,128)S(1)}, f32[8,64,256]{2,1,0:T(8,128)S(1)}, f32[64,8,...) custom-call(f32[64,64,256]{2,1,0:T(8,128)S(1)} %copy-done.8, s32[3]{0:T(128)S(1)} %copy-done.15, ...), custom_call_target="tpu_custom_call" | custom-call | flops 1 | bytes 1 | tf_op jit(solution)/shard_map/cond/branch_2_fun/dual_0/pallas_call | solution.py:439
  38.6 0.1 collective-permute-start.18
  38.7 2.6 %collective-permute-start.19 = (f32[8,64,256]{2,1,0:T(8,128)S(1)}, f32[8,64,256]{2,1,0:T(8,128)S(1)}, u32[]{:S(2)}, u32[]{:S(2)}) collective-permute-start(f32[8,64,256]{2,1,0:T(8,128)S(1)} %get-tuple-element.126), channel_id=1, source_target_pairs={{4,8},{8,4},{5,9},{9,5},{6,10},{10,6},{7,11},{11,7},{20,24},{24,20... | collective-permute-start | bytes 1572872 | tf_op jit(solution)/shard_map/cond/branch_2_fun/ppermute | solution.py:491
  41.3 0.1 collective-permute-start.20
  41.4 1.9 %collective-permute-start.21 = (f32[64,8,256]{2,1,0:T(8,128)S(1)}, f32[64,8,256]{2,1,0:T(8,128)S(1)}, u32[]{:S(2)}, u32[]{:S(2)}) collective-permute-start(f32[64,8,256]{2,1,0:T(8,128)S(1)} %get-tuple-element.128), channel_id=1, source_target_pairs={{1,2},{2,1},{5,6},{6,5},{9,10},{10,9},{13,14},{14,13},{17,18},{18,... | collective-permute-start | bytes 1572872 | tf_op jit(solution)/shard_map/cond/branch_2_fun/ppermute | solution.py:491
  43.3 4.6 %partial_x_inner_0.1.refs_2_.after = f32[64,64,256]{2,1,0:T(8,128)S(1)} custom-call(s32[3]{0:T(128)S(1)} %copy-done.15, f32[64,64,256]{2,1,0:T(8,128)S(1)} %get-tuple-element.124.refs_1_), custom_call_target="tpu_custom_call" | custom-call | flops 1 | bytes 1 | tf_op jit(solution)/shard_map/cond/branch_2_fun/partial_x_inner_0/pallas_call | solution.py:439
  47.9 1.5 %collective-permute-done.19.refs_4_.odd = f32[8,64,256]{2,1,0:T(8,128)S(1)} collective-permute-done((f32[8,64,256]{2,1,0:T(8,128)S(1)}, f32[8,64,256]{2,1,0:T(8,128)S(1)}, u32[]{:S(2)}, u32[]{:S(2)}) %collective-permute-start.19) | collective-permute-done | bytes 524320 | tf_op jit(solution)/shard_map/cond/branch_2_fun/ppermute | solution.py:491
  49.5 0.1 collective-permute-start.22
  49.6 0.0 copy-start.2
  49.6 2.2 %collective-permute-start.23 = (f32[16,8,256]{2,1,0:T(8,128)S(1)}, f32[16,8,256]{2,1,0:T(8,128)S(1)}, u32[]{:S(2)}, u32[]{:S(2)}) collective-permute-start(f32[16,8,256]{2,1,0:T(8,128)S(1)} %get-tuple-element.130), channel_id=1, source_target_pairs={{1,2},{2,1},{5,6},{6,5},{9,10},{10,9},{13,14},{14,13},{17,18},{18,... | collective-permute-start | bytes 393224 | tf_op jit(solution)/shard_map/cond/branch_2_fun/ppermute | solution.py:491
  51.8 2.4 %partial_x_outer_0.1.refs_3_ = f32[64,64,256]{2,1,0:T(8,128)S(1)} custom-call(s32[3]{0:T(128)S(1)} %copy-done.15, f32[64,64,256]{2,1,0:T(8,128)S(1)} %get-tuple-element.124.refs_1_, f32[64,64,256]{2,1,0:T(8,128)S(1)} %partial_x_inner_0.1.refs_2_.after, f32[8,64,256]{2,1,0:T(8,128)S(1)} %collective-permute-done.18.refs_3_.even, ...), custom_call_target="tpu_custom_call", output_to_operand_aliasing={{}: (2, {})} | custom-call | flops 1 | bytes 1 | tf_op jit(solution)/shard_map/cond/branch_2_fun/partial_x_outer_0/pallas_call | solution.py:439
  54.1 1.2 %collective-permute-done.20.refs_4_ = f32[64,8,256]{2,1,0:T(8,128)S(1)} collective-permute-done((f32[64,8,256]{2,1,0:T(8,128)S(1)}, f32[64,8,256]{2,1,0:T(8,128)S(1)}, u32[]{:S(2)}, u32[]{:S(2)}) %collective-permute-start.20) | collective-permute-done | bytes 524320 | tf_op jit(solution)/shard_map/cond/branch_2_fun/ppermute | solution.py:491
  55.3 1.9 %collective-permute-done.21.refs_5_ = f32[64,8,256]{2,1,0:T(8,128)S(1)} collective-permute-done((f32[64,8,256]{2,1,0:T(8,128)S(1)}, f32[64,8,256]{2,1,0:T(8,128)S(1)}, u32[]{:S(2)}, u32[]{:S(2)}) %collective-permute-start.21) | collective-permute-done | bytes 524320 | tf_op jit(solution)/shard_map/cond/branch_2_fun/ppermute | solution.py:491
  57.2 1.5 %collective-permute-done.23.refs_7_ = f32[16,8,256]{2,1,0:T(8,128)S(1)} collective-permute-done((f32[16,8,256]{2,1,0:T(8,128)S(1)}, f32[16,8,256]{2,1,0:T(8,128)S(1)}, u32[]{:S(2)}, u32[]{:S(2)}) %collective-permute-start.23) | collective-permute-done | bytes 131104 | tf_op jit(solution)/shard_map/cond/branch_2_fun/ppermute | solution.py:491
  58.7 6.2 %partial_0.3 = (f32[64,64,128]{2,1,0:T(8,128)}, f32[64,64,128]{2,1,0:T(8,128)}, f32[64,64,256]{2,1,0:T(8,128)}) custom-call(f32[64,64,256]{2,1,0:T(8,128)S(1)} %copy-done.2, f32[1]{0:T(128)} %get-tuple-element.112.refs_1_, s32[3]{0:T(128)S(1)} %copy-done.15, f32[64,64,256]{2,1,0:T(8,128)S(1)} %partial_x_outer_0.1.refs_3_, ...), custom_call_target="tpu_custom_call" | custom-call | flops 1 | bytes 1 | tf_op jit(solution)/shard_map/cond/branch_2_fun/partial_0/pallas_call | solution.py:439
  65.2 0.3 collective-permute-start.36
  65.5 32.1 %conditional.3 = (f32[64,64,256]{2,1,0:T(8,128)}) conditional(s32[]{:T(128)} %clamp.4, (f32[64,64,256]{2,1,0:T(8,128)}, f32[1]{0:T(128)}, f32[64,64,128]{2,1,0:T(8,128)S(1)}, f32[64,64,128]{2,1,0:T(8,128)}, s32[3]{0:T(128)}, /*index=5*/f32[64,64,256]{2,1,0:T(8,128)}) %tuple.30, (f32[64,64,256]{2,1,0:T(8,128)}, f32[1]{0:T(128)}, ...), branch_computations={%region_4.5_spmd, %region_5.6_spmd, %region_6.7_spmd} | conditional | flops 5 | bytes 46137672 | solution.py:616
  65.5 6.4 %cotangent_0.3 = (f32[64,64,256]{2,1,0:T(8,128)S(1)}, f32[8,64,256]{2,1,0:T(8,128)S(1)}, f32[8,64,256]{2,1,0:T(8,128)S(1)}, f32[64,8,256]{2,1,0:T(8,128)S(1)}, f...) custom-call(f32[64,64,256]{2,1,0:T(8,128)} %get-tuple-element.162.refs_0_, ...), custom_call_target="tpu_custom_call" | custom-call | flops 1 | bytes 1 | tf_op jit(solution)/shard_map/cond/branch_2_fun/cotangent_0/pallas_call | solution.py:439
  71.9 0.1 collective-permute-start.30
  72.0 2.6 %collective-permute-start.31 = (f32[8,64,256]{2,1,0:T(8,128)S(1)}, f32[8,64,256]{2,1,0:T(8,128)S(1)}, u32[]{:S(2)}, u32[]{:S(2)}) collective-permute-start(f32[8,64,256]{2,1,0:T(8,128)S(1)} %get-tuple-element.168), channel_id=1, source_target_pairs={{4,8},{8,4},{5,9},{9,5},{6,10},{10,6},{7,11},{11,7},{20,24},{24,20... | collective-permute-start | bytes 1572872 | tf_op jit(solution)/shard_map/cond/branch_2_fun/ppermute | solution.py:491
  74.6 0.1 collective-permute-start.32
  74.7 1.9 %collective-permute-start.33 = (f32[64,8,256]{2,1,0:T(8,128)S(1)}, f32[64,8,256]{2,1,0:T(8,128)S(1)}, u32[]{:S(2)}, u32[]{:S(2)}) collective-permute-start(f32[64,8,256]{2,1,0:T(8,128)S(1)} %get-tuple-element.170), channel_id=1, source_target_pairs={{1,2},{2,1},{5,6},{6,5},{9,10},{10,9},{13,14},{14,13},{17,18},{18,... | collective-permute-start | bytes 1572872 | tf_op jit(solution)/shard_map/cond/branch_2_fun/ppermute | solution.py:491
  76.6 4.6 %gradient_x_inner_0.1.refs_2_.after = f32[64,64,256]{2,1,0:T(8,128)S(1)} custom-call(s32[3]{0:T(128)S(1)} %copy-done.18, f32[64,64,256]{2,1,0:T(8,128)S(1)} %get-tuple-element.166.refs_1_), custom_call_target="tpu_custom_call" | custom-call | flops 1 | bytes 1 | tf_op jit(solution)/shard_map/cond/branch_2_fun/gradient_x_inner_0/pallas_call | solution.py:439
  81.2 1.6 %collective-permute-done.31.refs_4_.odd = f32[8,64,256]{2,1,0:T(8,128)S(1)} collective-permute-done((f32[8,64,256]{2,1,0:T(8,128)S(1)}, f32[8,64,256]{2,1,0:T(8,128)S(1)}, u32[]{:S(2)}, u32[]{:S(2)}) %collective-permute-start.31) | collective-permute-done | bytes 524320 | tf_op jit(solution)/shard_map/cond/branch_2_fun/ppermute | solution.py:491
  82.9 0.1 collective-permute-start.34
  83.0 2.2 %collective-permute-start.35 = (f32[16,8,256]{2,1,0:T(8,128)S(1)}, f32[16,8,256]{2,1,0:T(8,128)S(1)}, u32[]{:S(2)}, u32[]{:S(2)}) collective-permute-start(f32[16,8,256]{2,1,0:T(8,128)S(1)} %get-tuple-element.172), channel_id=1, source_target_pairs={{1,2},{2,1},{5,6},{6,5},{9,10},{10,9},{13,14},{14,13},{17,18},{18,... | collective-permute-start | bytes 393224 | tf_op jit(solution)/shard_map/cond/branch_2_fun/ppermute | solution.py:491
  85.2 2.4 %gradient_x_outer_0.1.refs_2_ = f32[64,64,256]{2,1,0:T(8,128)S(1)} custom-call(s32[3]{0:T(128)S(1)} %copy-done.18, f32[64,64,256]{2,1,0:T(8,128)S(1)} %get-tuple-element.166.refs_1_, f32[64,64,256]{2,1,0:T(8,128)S(1)} %gradient_x_inner_0.1.refs_2_.after, f32[8,64,256]{2,1,0:T(8,128)S(1)} %collective-permute-done.30.refs_3_.even, ...), custom_call_target="tpu_custom_call", output_to_operand_aliasing={{}: (2, {})} | custom-call | flops 1 | bytes 1 | tf_op jit(solution)/shard_map/cond/branch_2_fun/gradient_x_outer_0/pallas_call | solution.py:439
  87.5 1.2 %collective-permute-done.32.refs_3_ = f32[64,8,256]{2,1,0:T(8,128)S(1)} collective-permute-done((f32[64,8,256]{2,1,0:T(8,128)S(1)}, f32[64,8,256]{2,1,0:T(8,128)S(1)}, u32[]{:S(2)}, u32[]{:S(2)}) %collective-permute-start.32) | collective-permute-done | bytes 524320 | tf_op jit(solution)/shard_map/cond/branch_2_fun/ppermute | solution.py:491
  88.7 1.9 %collective-permute-done.33.refs_4_ = f32[64,8,256]{2,1,0:T(8,128)S(1)} collective-permute-done((f32[64,8,256]{2,1,0:T(8,128)S(1)}, f32[64,8,256]{2,1,0:T(8,128)S(1)}, u32[]{:S(2)}, u32[]{:S(2)}) %collective-permute-start.33) | collective-permute-done | bytes 524320 | tf_op jit(solution)/shard_map/cond/branch_2_fun/ppermute | solution.py:491
  90.6 1.8 %collective-permute-done.35.refs_6_ = f32[16,8,256]{2,1,0:T(8,128)S(1)} collective-permute-done((f32[16,8,256]{2,1,0:T(8,128)S(1)}, f32[16,8,256]{2,1,0:T(8,128)S(1)}, u32[]{:S(2)}, u32[]{:S(2)}) %collective-permute-start.35) | collective-permute-done | bytes 131104 | tf_op jit(solution)/shard_map/cond/branch_2_fun/ppermute | solution.py:491
  92.5 5.1 %gradient_0.3 = f32[64,64,256]{2,1,0:T(8,128)} custom-call(f32[64,64,256]{2,1,0:T(8,128)S(1)} %copy-done.5, s32[3]{0:T(128)S(1)} %copy-done.18, f32[64,64,256]{2,1,0:T(8,128)S(1)} %gradient_x_outer_0.1.refs_2_, f32[64,8,256]{2,1,0:T(8,128)S(1)} %collective-permute-done.32.refs_3_, f32[64,8,256]{2,1,0:T(8,128)S(1)} %collective-permute-done.33.refs_4_, ...), custom_call_target="tpu_custom_call" | custom-call | flops 1 | bytes 1 | tf_op jit(solution)/shard_map/cond/branch_2_fun/gradient_0/pallas_call | solution.py:439
  97.6 15.5 %collective-permute-done.36.arrived = f32[64,64,128]{2,1,0:T(8,128)} collective-permute-done((f32[64,64,128]{2,1,0:T(8,128)}, f32[64,64,128]{2,1,0:T(8,128)}, u32[]{:S(2)}, u32[]{:S(2)}) %collective-permute-start.36) | collective-permute-done | bytes 2097184 | tf_op jit(solution)/shard_map/ppermute | solution.py:615
  113.1 3.1 %barycenter.1 = f32[64,64,128]{2,1,0:T(8,128)} custom-call(f32[64,64,128]{2,1,0:T(8,128)} %get-tuple-element.180.keep, f32[64,64,128]{2,1,0:T(8,128)} %collective-permute-done.36.arrived, f32[64,64,256]{2,1,0:T(8,128)} %get-tuple-element.196.after), custom_call_target="tpu_custom_call" | custom-call | flops 1 | bytes 1 | tf_op jit(solution)/shard_map/barycenter/pallas_call | solution.py:475
  (20 shorter events, 0.1 us)
Async XLA Ops:
  0.6 64.8 %collective-permute-start.37 = (f32[64,64,128]{2,1,0:T(8,128)}, f32[64,64,128]{2,1,0:T(8,128)S(1)}, u32[]{:S(2)}, u32[]{:S(2)}) collective-permute-start(f32[64,64,128]{2,1,0:T(8,128)} %param.15), channel_id=1, source_target_pairs={{0,16},{16,0},{1,17},{17,1},{2,18},{18,2},{3,19},{19,3},{4,20},{20... | collective-permute-start | bytes 6291464 | tf_op jit(solution)/shard_map/ppermute | solution.py:611
  3.9 12.4 %copy-start.15 = (s32[3]{0:T(128)S(1)}, s32[3]{0:T(128)}, u32[]{:S(2)}) copy-start(s32[3]{0:T(128)} %get-tuple-element.113.refs_1_.refs_0_.refs_2_) | copy-start | bytes 40 | tf_op jit(solution)/shard_map/cond
  9.0 11.9 %collective-permute-start.12 = (f32[8,64,256]{2,1,0:T(8,128)S(1)}, f32[8,64,256]{2,1,0:T(8,128)S(1)}, u32[]{:S(2)}, u32[]{:S(2)}) collective-permute-start(f32[8,64,256]{2,1,0:T(8,128)S(1)} %get-tuple-element.116), channel_id=1, source_target_pairs={{0,4},{8,12},{4,0},{12,8},{1,5},{9,13},{5,1},{13,9},{2,6},{10,14},... | collective-permute-start | bytes 1572872 | tf_op jit(solution)/shard_map/cond/branch_2_fun/ppermute | solution.py:491
  10.1 10.9 %collective-permute-start.13 = (f32[8,64,256]{2,1,0:T(8,128)S(1)}, f32[8,64,256]{2,1,0:T(8,128)S(1)}, u32[]{:S(2)}, u32[]{:S(2)}) collective-permute-start(f32[8,64,256]{2,1,0:T(8,128)S(1)} %get-tuple-element.117), channel_id=1, source_target_pairs={{4,8},{8,4},{5,9},{9,5},{6,10},{10,6},{7,11},{11,7},{20,24},{24,20... | collective-permute-start | bytes 1572872 | tf_op jit(solution)/shard_map/cond/branch_2_fun/ppermute | solution.py:491
  13.1 14.0 %collective-permute-start.14 = (f32[64,8,256]{2,1,0:T(8,128)S(1)}, f32[64,8,256]{2,1,0:T(8,128)S(1)}, u32[]{:S(2)}, u32[]{:S(2)}) collective-permute-start(f32[64,8,256]{2,1,0:T(8,128)S(1)} %get-tuple-element.118), channel_id=1, source_target_pairs={{0,1},{2,3},{1,0},{3,2},{4,5},{6,7},{5,4},{7,6},{8,9},{10,11},{9,8... | collective-permute-start | bytes 1572872 | tf_op jit(solution)/shard_map/cond/branch_2_fun/ppermute | solution.py:491
  14.4 15.7 %collective-permute-start.15 = (f32[64,8,256]{2,1,0:T(8,128)S(1)}, f32[64,8,256]{2,1,0:T(8,128)S(1)}, u32[]{:S(2)}, u32[]{:S(2)}) collective-permute-start(f32[64,8,256]{2,1,0:T(8,128)S(1)} %get-tuple-element.119), channel_id=1, source_target_pairs={{1,2},{2,1},{5,6},{6,5},{9,10},{10,9},{13,14},{14,13},{17,18},{18,... | collective-permute-start | bytes 1572872 | tf_op jit(solution)/shard_map/cond/branch_2_fun/ppermute | solution.py:491
  21.0 9.1 %collective-permute-start.16 = (f32[16,8,256]{2,1,0:T(8,128)S(1)}, f32[16,8,256]{2,1,0:T(8,128)S(1)}, u32[]{:S(2)}, u32[]{:S(2)}) collective-permute-start(f32[16,8,256]{2,1,0:T(8,128)S(1)} %get-tuple-element.120), channel_id=1, source_target_pairs={{0,1},{2,3},{1,0},{3,2},{4,5},{6,7},{5,4},{7,6},{8,9},{10,11},{9,8... | collective-permute-start | bytes 393224 | tf_op jit(solution)/shard_map/cond/branch_2_fun/ppermute | solution.py:491
  22.2 9.3 %copy-start.8 = (f32[64,64,256]{2,1,0:T(8,128)S(1)}, f32[64,64,256]{2,1,0:T(8,128)}, u32[]{:S(2)}) copy-start(f32[64,64,256]{2,1,0:T(8,128)} %get-tuple-element.114.refs_0_) | copy-start | bytes 12582916 | tf_op jit(solution)/shard_map/cond
  22.2 9.3 %collective-permute-start.17 = (f32[16,8,256]{2,1,0:T(8,128)S(1)}, f32[16,8,256]{2,1,0:T(8,128)S(1)}, u32[]{:S(2)}, u32[]{:S(2)}) collective-permute-start(f32[16,8,256]{2,1,0:T(8,128)S(1)} %get-tuple-element.121), channel_id=1, source_target_pairs={{1,2},{2,1},{5,6},{6,5},{9,10},{10,9},{13,14},{14,13},{17,18},{18,... | collective-permute-start | bytes 393224 | tf_op jit(solution)/shard_map/cond/branch_2_fun/ppermute | solution.py:491
  38.6 9.3 %collective-permute-start.18 = (f32[8,64,256]{2,1,0:T(8,128)S(1)}, f32[8,64,256]{2,1,0:T(8,128)S(1)}, u32[]{:S(2)}, u32[]{:S(2)}) collective-permute-start(f32[8,64,256]{2,1,0:T(8,128)S(1)} %get-tuple-element.125), channel_id=1, source_target_pairs={{0,4},{8,12},{4,0},{12,8},{1,5},{9,13},{5,1},{13,9},{2,6},{10,14},... | collective-permute-start | bytes 1572872 | tf_op jit(solution)/shard_map/cond/branch_2_fun/ppermute | solution.py:491
  38.7 10.8 %collective-permute-start.19 = (f32[8,64,256]{2,1,0:T(8,128)S(1)}, f32[8,64,256]{2,1,0:T(8,128)S(1)}, u32[]{:S(2)}, u32[]{:S(2)}) collective-permute-start(f32[8,64,256]{2,1,0:T(8,128)S(1)} %get-tuple-element.126), channel_id=1, source_target_pairs={{4,8},{8,4},{5,9},{9,5},{6,10},{10,6},{7,11},{11,7},{20,24},{24,20... | collective-permute-start | bytes 1572872 | tf_op jit(solution)/shard_map/cond/branch_2_fun/ppermute | solution.py:491
  41.3 14.0 %collective-permute-start.20 = (f32[64,8,256]{2,1,0:T(8,128)S(1)}, f32[64,8,256]{2,1,0:T(8,128)S(1)}, u32[]{:S(2)}, u32[]{:S(2)}) collective-permute-start(f32[64,8,256]{2,1,0:T(8,128)S(1)} %get-tuple-element.127), channel_id=1, source_target_pairs={{0,1},{2,3},{1,0},{3,2},{4,5},{6,7},{5,4},{7,6},{8,9},{10,11},{9,8... | collective-permute-start | bytes 1572872 | tf_op jit(solution)/shard_map/cond/branch_2_fun/ppermute | solution.py:491
  41.4 15.8 %collective-permute-start.21 = (f32[64,8,256]{2,1,0:T(8,128)S(1)}, f32[64,8,256]{2,1,0:T(8,128)S(1)}, u32[]{:S(2)}, u32[]{:S(2)}) collective-permute-start(f32[64,8,256]{2,1,0:T(8,128)S(1)} %get-tuple-element.128), channel_id=1, source_target_pairs={{1,2},{2,1},{5,6},{6,5},{9,10},{10,9},{13,14},{14,13},{17,18},{18,... | collective-permute-start | bytes 1572872 | tf_op jit(solution)/shard_map/cond/branch_2_fun/ppermute | solution.py:491
  49.5 7.7 %collective-permute-start.22 = (f32[16,8,256]{2,1,0:T(8,128)S(1)}, f32[16,8,256]{2,1,0:T(8,128)S(1)}, u32[]{:S(2)}, u32[]{:S(2)}) collective-permute-start(f32[16,8,256]{2,1,0:T(8,128)S(1)} %get-tuple-element.129), channel_id=1, source_target_pairs={{0,1},{2,3},{1,0},{3,2},{4,5},{6,7},{5,4},{7,6},{8,9},{10,11},{9,8... | collective-permute-start | bytes 393224 | tf_op jit(solution)/shard_map/cond/branch_2_fun/ppermute | solution.py:491
  49.6 9.2 %copy-start.2 = (f32[64,64,256]{2,1,0:T(8,128)S(1)}, f32[64,64,256]{2,1,0:T(8,128)}, u32[]{:S(2)}) copy-start(f32[64,64,256]{2,1,0:T(8,128)} %get-tuple-element.111.refs_0_) | copy-start | bytes 12582916 | tf_op jit(solution)/shard_map/cond
  49.6 9.2 %collective-permute-start.23 = (f32[16,8,256]{2,1,0:T(8,128)S(1)}, f32[16,8,256]{2,1,0:T(8,128)S(1)}, u32[]{:S(2)}, u32[]{:S(2)}) collective-permute-start(f32[16,8,256]{2,1,0:T(8,128)S(1)} %get-tuple-element.130), channel_id=1, source_target_pairs={{1,2},{2,1},{5,6},{6,5},{9,10},{10,9},{13,14},{14,13},{17,18},{18,... | collective-permute-start | bytes 393224 | tf_op jit(solution)/shard_map/cond/branch_2_fun/ppermute | solution.py:491
  65.2 47.9 %collective-permute-start.36 = (f32[64,64,128]{2,1,0:T(8,128)}, f32[64,64,128]{2,1,0:T(8,128)}, u32[]{:S(2)}, u32[]{:S(2)}) collective-permute-start(f32[64,64,128]{2,1,0:T(8,128)} %get-tuple-element.181), channel_id=1, source_target_pairs={{0,16},{16,0},{1,17},{17,1},{2,18},{18,2},{3,19},{19,3},{4,20},{20... | collective-permute-start | bytes 6291464 | tf_op jit(solution)/shard_map/ppermute | solution.py:615
  65.5 11.2 %copy-start.18 = (s32[3]{0:T(128)S(1)}, s32[3]{0:T(128)}, u32[]{:S(2)}) copy-start(s32[3]{0:T(128)} %get-tuple-element.161.refs_4_.refs_0_.refs_1_) | copy-start | bytes 40 | tf_op jit(solution)/shard_map/cond
  71.9 9.3 %collective-permute-start.30 = (f32[8,64,256]{2,1,0:T(8,128)S(1)}, f32[8,64,256]{2,1,0:T(8,128)S(1)}, u32[]{:S(2)}, u32[]{:S(2)}) collective-permute-start(f32[8,64,256]{2,1,0:T(8,128)S(1)} %get-tuple-element.167), channel_id=1, source_target_pairs={{0,4},{8,12},{4,0},{12,8},{1,5},{9,13},{5,1},{13,9},{2,6},{10,14},... | collective-permute-start | bytes 1572872 | tf_op jit(solution)/shard_map/cond/branch_2_fun/ppermute | solution.py:491
  72.0 10.9 %collective-permute-start.31 = (f32[8,64,256]{2,1,0:T(8,128)S(1)}, f32[8,64,256]{2,1,0:T(8,128)S(1)}, u32[]{:S(2)}, u32[]{:S(2)}) collective-permute-start(f32[8,64,256]{2,1,0:T(8,128)S(1)} %get-tuple-element.168), channel_id=1, source_target_pairs={{4,8},{8,4},{5,9},{9,5},{6,10},{10,6},{7,11},{11,7},{20,24},{24,20... | collective-permute-start | bytes 1572872 | tf_op jit(solution)/shard_map/cond/branch_2_fun/ppermute | solution.py:491
  74.6 14.1 %collective-permute-start.32 = (f32[64,8,256]{2,1,0:T(8,128)S(1)}, f32[64,8,256]{2,1,0:T(8,128)S(1)}, u32[]{:S(2)}, u32[]{:S(2)}) collective-permute-start(f32[64,8,256]{2,1,0:T(8,128)S(1)} %get-tuple-element.169), channel_id=1, source_target_pairs={{0,1},{2,3},{1,0},{3,2},{4,5},{6,7},{5,4},{7,6},{8,9},{10,11},{9,8... | collective-permute-start | bytes 1572872 | tf_op jit(solution)/shard_map/cond/branch_2_fun/ppermute | solution.py:491
  74.7 15.9 %collective-permute-start.33 = (f32[64,8,256]{2,1,0:T(8,128)S(1)}, f32[64,8,256]{2,1,0:T(8,128)S(1)}, u32[]{:S(2)}, u32[]{:S(2)}) collective-permute-start(f32[64,8,256]{2,1,0:T(8,128)S(1)} %get-tuple-element.170), channel_id=1, source_target_pairs={{1,2},{2,1},{5,6},{6,5},{9,10},{10,9},{13,14},{14,13},{17,18},{18,... | collective-permute-start | bytes 1572872 | tf_op jit(solution)/shard_map/cond/branch_2_fun/ppermute | solution.py:491
  82.9 7.7 %collective-permute-start.34 = (f32[16,8,256]{2,1,0:T(8,128)S(1)}, f32[16,8,256]{2,1,0:T(8,128)S(1)}, u32[]{:S(2)}, u32[]{:S(2)}) collective-permute-start(f32[16,8,256]{2,1,0:T(8,128)S(1)} %get-tuple-element.171), channel_id=1, source_target_pairs={{0,1},{2,3},{1,0},{3,2},{4,5},{6,7},{5,4},{7,6},{8,9},{10,11},{9,8... | collective-permute-start | bytes 393224 | tf_op jit(solution)/shard_map/cond/branch_2_fun/ppermute | solution.py:491
  83.0 9.5 %copy-start.5 = (f32[64,64,256]{2,1,0:T(8,128)S(1)}, f32[64,64,256]{2,1,0:T(8,128)}, u32[]{:S(2)}) copy-start(f32[64,64,256]{2,1,0:T(8,128)} %get-tuple-element.160.refs_0_) | copy-start | bytes 12582916 | tf_op jit(solution)/shard_map/cond
  83.0 9.5 %collective-permute-start.35 = (f32[16,8,256]{2,1,0:T(8,128)S(1)}, f32[16,8,256]{2,1,0:T(8,128)S(1)}, u32[]{:S(2)}, u32[]{:S(2)}) collective-permute-start(f32[16,8,256]{2,1,0:T(8,128)S(1)} %get-tuple-element.172), channel_id=1, source_target_pairs={{1,2},{2,1},{5,6},{6,5},{9,10},{10,9},{13,14},{14,13},{17,18},{18,... | collective-permute-start | bytes 393224 | tf_op jit(solution)/shard_map/cond/branch_2_fun/ppermute | solution.py:491

commit v2 on v1

--- a/solution.py
+++ b/solution.py
@@ -450,38 +450,52 @@
         return dict(zip(outs, result))
 
 
-def add_body(keep, arrived, after, out, left, right, total, sems):
+def fetch_body(source, after, out, sem):
+    copy = pltpu.make_async_copy(source, out, sem.at[0])
+    copy.start()
+    copy.wait()
+
+
+def fetch(value, after):
+    return pl.pallas_call(
+        fetch_body,
+        name="fetch",
+        out_shape=pltpu.VMEM(value.shape, F32),
+        in_specs=[pl.BlockSpec(memory_space=pl.ANY)] * 2,
+        out_specs=pl.BlockSpec(memory_space=pltpu.VMEM),
+        scratch_shapes=[pltpu.SemaphoreType.DMA((1,))],
+        compiler_params=pltpu.CompilerParams(vmem_limit_bytes=6 * 2**20),
+        cost_estimate=COST,
+    )(value, after)
+
+
+def add_body(keep, arrived, out, here, sems):
     parts = sems.shape[1]
-    step = total.shape[0] // parts
+    step = here.shape[0] // parts
     planes = [pl.ds(n * step, step) for n in range(parts)]
-    loads = [
-        pltpu.make_async_copy(source.at[p], target.at[p], sems.at[m, n])
-        for n, p in enumerate(planes)
-        for m, (source, target) in enumerate(((keep, left), (arrived, right)))
-    ]
-    saves = [pltpu.make_async_copy(total.at[p], out.at[p], sems.at[2, n]) for n, p in enumerate(planes)]
+    loads = [pltpu.make_async_copy(arrived.at[p], here.at[p], sems.at[0, n]) for n, p in enumerate(planes)]
+    saves = [pltpu.make_async_copy(here.at[p], out.at[p], sems.at[1, n]) for n, p in enumerate(planes)]
     for copy in loads:
         copy.start()
     for n, p in enumerate(planes):
-        loads[2 * n].wait()
-        loads[2 * n + 1].wait()
-        total[p] = left[p] + right[p]
+        loads[n].wait()
+        here[p] = here[p] + keep[p]
         saves[n].start()
     for copy in saves:
         copy.wait()
 
 
-def add(keep, arrived, after):
+def add(keep, arrived):
     return pl.pallas_call(
         add_body,
         name="barycenter",
         out_shape=pltpu.HBM(keep.shape, F32),
-        in_specs=[pl.BlockSpec(memory_space=pl.ANY)] * 3,
+        in_specs=[pl.BlockSpec(memory_space=pltpu.VMEM), pl.BlockSpec(memory_space=pl.ANY)],
         out_specs=pl.BlockSpec(memory_space=pltpu.HBM),
-        scratch_shapes=[pltpu.VMEM(keep.shape, F32)] * 3 + [pltpu.SemaphoreType.DMA((3, 4))],
+        scratch_shapes=[pltpu.VMEM(keep.shape, F32), pltpu.SemaphoreType.DMA((2, 8))],
         compiler_params=pltpu.CompilerParams(vmem_limit_bytes=8 * 2**20),
         cost_estimate=COST,
-    )(keep, arrived, after)
+    )(pltpu.with_memory_space_constraint(keep, pltpu.VMEM), arrived)
 
 
 def neighbours(sizes, line, even, odd):
@@ -616,7 +630,7 @@
     grad = lax.switch(
         line, [case.gradient for case in cases], bary_weights, band_reach, bary_cotangent, far, t, d
     )
-    return (add(keep, arrived, grad), grad[None])
+    return (add(fetch(keep, grad), arrived), grad[None])
 
 
 def solution(mesh):

time: 117 us -> 97.4 us (0.83)
  the two profiles are of different devices: /device:TPU:17 before, /device:TPU:1 now
where the time goes in v2:
time: 97.4 us; the launch traced here: 96 us
  Pallas kernels  47.4 us (49%)
  waiting for transfers between devices  30.5 us (31%)
  starting transfers between devices  14.7 us (15%)
  between operations  1.47 us (2%)
  other arithmetic  1.29 us (1%)
    pallas_call x10, Pallas kernels, __call__(): pl.pallas_call(lambda *refs: self.body(dict(zip(names, refs))), name=name...  43.4 us
    ppermute x1, waiting for transfers between devices, per_device(): arrived = lax.ppermute(send, 'inp', SWAP)  21.5 us
    ppermute x6, starting transfers between devices, neighbours(): lax.ppermute(value, AXES[line], pairs + [(j, i) for i, j in pairs])  12.3 us
    ppermute x1, waiting for transfers between devices, per_device(): far = lax.ppermute(bary_cotangent, 'inp', SWAP)  6.55 us
    ppermute x6, waiting for transfers between devices, neighbours(): lax.ppermute(value, AXES[line], pairs + [(j, i) for i, j in pairs])  2.51 us
    pallas_call x1, Pallas kernels, add(): pl.pallas_call(add_body, name='barycenter', out_shape=pltpu.HBM(keep.shap...  2.42 us
    ppermute x1, starting transfers between devices, per_device(): far = lax.ppermute(bary_cotangent, 'inp', SWAP)  2.13 us
  transfers between devices with their start and end apart: 8, of which 3 were waited for; matrix products, arithmetic and copies ran while one was open for 1% of the time, Pallas kernels for 47%

profile of v2, /device:TPU:1, one launch (start us, length us, event | category | flops | bytes accessed | tf_op | source)
XLA Modules:
  0.0 96.0 jit_solution(12616976934237564604)
XLA Ops:
  0.6 2.1 %collective-permute-start.36 = (f32[64,64,128]{2,1,0:T(8,128)}, f32[64,64,128]{2,1,0:T(8,128)S(1)}, u32[]{:S(2)}, u32[]{:S(2)}) collective-permute-start(f32[64,64,128]{2,1,0:T(8,128)} %param.15), channel_id=1, source_target_pairs={{0,16},{16,0},{1,17},{17,1},{2,18},{18,2},{3,19},{19,3},{4,20},{20... | collective-permute-start | bytes 6291464 | tf_op jit(solution)/shard_map/ppermute | solution.py:625
  2.8 1.3 %fusion = s32[]{:T(128)} fusion(s32[3]{0:T(128)} %param.14), kind=kLoop, calls=%fused_computation.1 | loop fusion | flops 8 | bytes 16 | tf_op jit(solution)/shard_map/reduce_sum | solution.py:622
  4.7 36.8 %conditional.2 = (f32[64,64,128]{2,1,0:T(8,128)}, f32[64,64,128]{2,1,0:T(8,128)}, f32[64,64,256]{2,1,0:T(8,128)}, f32[64,64,256]{2,1,0:T(8,128)}) conditional(s32[]{:T(128)} %clamp.4, (f32[64,64,256]{2,1,0:T(8,128)}, s32[3]{0:T(128)}, f32[64,64,256]{2,1,0:T(8,128)}, f32[1]{0:T(128)}) %tuple.41, (f32[64,64,256]{2,1,0:T(8,128)}, ...), branch_computations={%region_1.2_spmd, %region_2.3_spmd, %region_3.4_spmd} | conditional | flops 9 | bytes 52429444 | solution.py:626
  4.7 0.0 copy-start.1
  4.7 0.0 copy-start.14
  4.8 3.5 %scaling_outer_0.1 = (f32[64,64,256]{2,1,0:T(8,128)S(1)}, f32[8,64,256]{2,1,0:T(8,128)S(1)}, f32[8,64,256]{2,1,0:T(8,128)S(1)}, bf16[768,256]{1,0:T(8,128)(2,1)S(1)}, bf16[64,192]{1,0:T(8,128)(2,1)S(1)}) custom-call(f32[64,64,256]{2,1,0:T(8,128)} %get-tuple-element.90.refs_0_, s32[3]{0:T(128)} %get-tuple-element.92.refs_1_.refs_2_), custom_call_target="tpu_custom_call" | custom-call | flops 1 | bytes 1 | tf_op jit(solution)/shard_map/cond/branch_1_fun/scaling_outer_0/pallas_call | solution.py:439
  8.2 1.0 %collective-permute-start.8 = (f32[8,64,256]{2,1,0:T(8,128)S(1)}, f32[8,64,256]{2,1,0:T(8,128)S(1)}, u32[]{:S(2)}, u32[]{:S(2)}) collective-permute-start(f32[8,64,256]{2,1,0:T(8,128)S(1)} %get-tuple-element.99), channel_id=1, source_target_pairs={{0,4},{8,12},{4,0},{12,8},{1,5},{9,13},{5,1},{13,9},{2,6},{10,14},... | collective-permute-start | bytes 1572872 | tf_op jit(solution)/shard_map/cond/branch_1_fun/ppermute | solution.py:505
  9.3 3.0 %collective-permute-start.9 = (f32[8,64,256]{2,1,0:T(8,128)S(1)}, f32[8,64,256]{2,1,0:T(8,128)S(1)}, u32[]{:S(2)}, u32[]{:S(2)}) collective-permute-start(f32[8,64,256]{2,1,0:T(8,128)S(1)} %get-tuple-element.100), channel_id=1, source_target_pairs={{4,8},{8,4},{5,9},{9,5},{6,10},{10,6},{7,11},{11,7},{20,24},{24,20... | collective-permute-start | bytes 1572872 | tf_op jit(solution)/shard_map/cond/branch_1_fun/ppermute | solution.py:505
  12.3 0.0 copy-done.1
  12.3 0.0 copy-done.14
  12.3 0.0 copy-start.7
  12.3 3.9 %scaling_inner_0.1.refs_2_ = f32[64,64,256]{2,1,0:T(8,128)S(1)} custom-call(f32[64,64,256]{2,1,0:T(8,128)S(1)} %copy-done.1, s32[3]{0:T(128)S(1)} %copy-done.14, f32[64,64,256]{2,1,0:T(8,128)S(1)} %get-tuple-element.94.refs_2_, bf16[768,256]{1,0:T(8,128)(2,1)S(1)} %get-tuple-element.95.refs_3_.refs_7_, ...), custom_call_target="tpu_custom_call", output_to_operand_aliasing={{}: (2, {})} | custom-call | flops 1 | bytes 1 | tf_op jit(solution)/shard_map/cond/branch_1_fun/scaling_inner_0/pallas_call | solution.py:439
  16.3 0.0 copy-done.7
  16.3 7.2 %dual_inner_0.1 = (f32[64,64,256]{2,1,0:T(8,128)}, f32[64,64,256]{2,1,0:T(8,128)S(1)}) custom-call(f32[64,64,256]{2,1,0:T(8,128)S(1)} %copy-done.7, s32[3]{0:T(128)S(1)} %copy-done.14, f32[64,64,256]{2,1,0:T(8,128)S(1)} %scaling_inner_0.1.refs_2_, bf16[768,256]{1,0:T(8,128)(2,1)S(1)} %get-tuple-element.95.refs_3_.refs_7_, ...), custom_call_target="tpu_custom_call" | custom-call | flops 1 | bytes 1 | tf_op jit(solution)/shard_map/cond/branch_1_fun/dual_inner_0/pallas_call | solution.py:439
  23.5 0.0 collective-permute-done.8.refs_5_
  23.5 0.0 collective-permute-done.9.refs_6_
  23.5 3.3 %dual_outer_0.1 = (f32[64,64,256]{2,1,0:T(8,128)}, f32[64,64,256]{2,1,0:T(8,128)S(1)}, f32[8,64,256]{2,1,0:T(8,128)S(1)}, f32[8,64,256]{2,1,0:T(8,128)S(1)}) custom-call(f32[64,64,256]{2,1,0:T(8,128)S(1)} %copy-done.7, s32[3]{0:T(128)S(1)} %copy-done.14, f32[64,64,256]{2,1,0:T(8,128)S(1)} %scaling_inner_0.1.refs_2_, ...), custom_call_target="tpu_custom_call", output_to_operand_aliasing={{0}: (3, {}), {1}: (4, {})} | custom-call | flops 1 | bytes 1 | tf_op jit(solution)/shard_map/cond/branch_1_fun/dual_outer_0/pallas_call | solution.py:439
  26.8 0.1 collective-permute-start.10
  26.9 2.5 %collective-permute-start.11 = (f32[8,64,256]{2,1,0:T(8,128)S(1)}, f32[8,64,256]{2,1,0:T(8,128)S(1)}, u32[]{:S(2)}, u32[]{:S(2)}) collective-permute-start(f32[8,64,256]{2,1,0:T(8,128)S(1)} %get-tuple-element.106), channel_id=1, source_target_pairs={{4,8},{8,4},{5,9},{9,5},{6,10},{10,6},{7,11},{11,7},{20,24},{24,20... | collective-permute-start | bytes 1572872 | tf_op jit(solution)/shard_map/cond/branch_1_fun/ppermute | solution.py:505
  29.4 5.7 %partial_inner_0.1 = (f32[64,64,128]{2,1,0:T(8,128)}, f32[64,64,128]{2,1,0:T(8,128)}, f32[64,64,256]{2,1,0:T(8,128)}) custom-call(f32[64,64,256]{2,1,0:T(8,128)S(1)} %copy-done.1, f32[1]{0:T(128)} %get-tuple-element.91.refs_1_, s32[3]{0:T(128)S(1)} %copy-done.14, f32[64,64,256]{2,1,0:T(8,128)S(1)} %get-tuple-element.101.refs_3_), custom_call_target="tpu_custom_call" | custom-call | flops 1 | bytes 1 | tf_op jit(solution)/shard_map/cond/branch_1_fun/partial_inner_0/pallas_call | solution.py:439
  35.2 0.0 collective-permute-done.10.refs_7_
  35.2 2.5 %collective-permute-done.11.refs_8_ = f32[8,64,256]{2,1,0:T(8,128)S(1)} collective-permute-done((f32[8,64,256]{2,1,0:T(8,128)S(1)}, f32[8,64,256]{2,1,0:T(8,128)S(1)}, u32[]{:S(2)}, u32[]{:S(2)}) %collective-permute-start.11) | collective-permute-done | bytes 524320 | tf_op jit(solution)/shard_map/cond/branch_1_fun/ppermute | solution.py:505
  37.7 3.6 %partial_outer_0.1 = (f32[64,64,128]{2,1,0:T(8,128)}, f32[64,64,128]{2,1,0:T(8,128)}, f32[64,64,256]{2,1,0:T(8,128)}) custom-call(f32[64,64,256]{2,1,0:T(8,128)S(1)} %copy-done.1, f32[1]{0:T(128)} %get-tuple-element.91.refs_1_, s32[3]{0:T(128)S(1)} %copy-done.14, ...), custom_call_target="tpu_custom_call", output_to_operand_aliasing={{0}: (4, {}), {1}: (5, {}), {2}: (6, {})} | custom-call | flops 1 | bytes 1 | tf_op jit(solution)/shard_map/cond/branch_1_fun/partial_outer_0/pallas_call | solution.py:439
  41.5 0.3 collective-permute-start.37
  41.8 6.5 %collective-permute-done.36 = f32[64,64,128]{2,1,0:T(8,128)S(1)} collective-permute-done((f32[64,64,128]{2,1,0:T(8,128)}, f32[64,64,128]{2,1,0:T(8,128)S(1)}, u32[]{:S(2)}, u32[]{:S(2)}) %collective-permute-start.36) | collective-permute-done | bytes 2097184 | tf_op jit(solution)/shard_map/ppermute | solution.py:625
  48.3 21.9 %conditional.3 = (f32[64,64,256]{2,1,0:T(8,128)}) conditional(s32[]{:T(128)} %clamp.4, (f32[64,64,256]{2,1,0:T(8,128)}, f32[1]{0:T(128)}, f32[64,64,128]{2,1,0:T(8,128)S(1)}, f32[64,64,128]{2,1,0:T(8,128)}, s32[3]{0:T(128)}, /*index=5*/f32[64,64,256]{2,1,0:T(8,128)}) %tuple.30, (f32[64,64,256]{2,1,0:T(8,128)}, f32[1]{0:T(128)}, ...), branch_computations={%region_4.5_spmd, %region_5.6_spmd, %region_6.7_spmd} | conditional | flops 5 | bytes 46137672 | solution.py:630
  48.3 0.0 copy-start.10
  48.3 0.0 copy-start.12
  48.3 0.0 copy-start.17
  48.3 4.3 %cotangent_outer_0.1 = (f32[64,64,256]{2,1,0:T(8,128)S(1)}, f32[8,64,256]{2,1,0:T(8,128)S(1)}, f32[8,64,256]{2,1,0:T(8,128)S(1)}, bf16[768,256]{1,0:T(8,128)(2,1)S(1)}, bf16[64,192]{1,0:T(8,128)(2,1)S(1)}) custom-call(f32[64,64,256]{2,1,0:T(8,128)} %get-tuple-element.151.refs_0_, f32[1]{0:T(128)} %get-tuple-element.152.refs_1_, ...), custom_call_target="tpu_custom_call" | custom-call | flops 1 | bytes 1 | tf_op jit(solution)/shard_map/cond/branch_1_fun/cotangent_outer_0/pallas_call | solution.py:439
  52.7 2.1 %collective-permute-start.28 = (f32[8,64,256]{2,1,0:T(8,128)S(1)}, f32[8,64,256]{2,1,0:T(8,128)S(1)}, u32[]{:S(2)}, u32[]{:S(2)}) collective-permute-start(f32[8,64,256]{2,1,0:T(8,128)S(1)} %get-tuple-element.158), channel_id=1, source_target_pairs={{0,4},{8,12},{4,0},{12,8},{1,5},{9,13},{5,1},{13,9},{2,6},{10,14},... | collective-permute-start | bytes 1572872 | tf_op jit(solution)/shard_map/cond/branch_1_fun/ppermute | solution.py:505
  54.8 3.6 %collective-permute-start.29 = (f32[8,64,256]{2,1,0:T(8,128)S(1)}, f32[8,64,256]{2,1,0:T(8,128)S(1)}, u32[]{:S(2)}, u32[]{:S(2)}) collective-permute-start(f32[8,64,256]{2,1,0:T(8,128)S(1)} %get-tuple-element.159), channel_id=1, source_target_pairs={{4,8},{8,4},{5,9},{9,5},{6,10},{10,6},{7,11},{11,7},{20,24},{24,20... | collective-permute-start | bytes 1572872 | tf_op jit(solution)/shard_map/cond/branch_1_fun/ppermute | solution.py:505
  58.4 0.0 copy-done.10
  58.4 0.0 copy-done.12
  58.4 0.0 copy-done.17
  58.4 0.0 copy-start.4
  58.4 5.3 %cotangent_inner_0.1.refs_2_ = f32[64,64,256]{2,1,0:T(8,128)S(1)} custom-call(f32[64,64,256]{2,1,0:T(8,128)S(1)} %copy-done.10, f32[1]{0:T(128)} %get-tuple-element.152.refs_1_, f32[64,64,128]{2,1,0:T(8,128)S(1)} %get-tuple-element.153.refs_2_, f32[64,64,128]{2,1,0:T(8,128)S(1)} %copy-done.12, s32[3]{0:T(128)S(1)} %copy-done.17, ...), custom_call_target="tpu_custom_call", output_to_operand_aliasing={{}: (5, {})} | custom-call | flops 1 | bytes 1 | tf_op jit(solution)/shard_map/cond/branch_1_fun/cotangent_inner_0/pallas_call | solution.py:439
  63.7 0.0 copy-done.4
  63.7 4.1 %gradient_inner_0.1.refs_3_ = f32[64,64,256]{2,1,0:T(8,128)} custom-call(f32[64,64,256]{2,1,0:T(8,128)S(1)} %copy-done.4, s32[3]{0:T(128)S(1)} %copy-done.17, f32[64,64,256]{2,1,0:T(8,128)S(1)} %cotangent_inner_0.1.refs_2_), custom_call_target="tpu_custom_call" | custom-call | flops 1 | bytes 1 | tf_op jit(solution)/shard_map/cond/branch_1_fun/gradient_inner_0/pallas_call | solution.py:439
  67.8 0.0 collective-permute-done.28.refs_4_
  67.8 0.0 collective-permute-done.29.refs_5_
  67.9 2.4 %gradient_outer_0.1 = f32[64,64,256]{2,1,0:T(8,128)} custom-call(f32[64,64,256]{2,1,0:T(8,128)S(1)} %copy-done.4, s32[3]{0:T(128)S(1)} %copy-done.17, f32[64,64,256]{2,1,0:T(8,128)S(1)} %cotangent_inner_0.1.refs_2_, f32[64,64,256]{2,1,0:T(8,128)} %gradient_inner_0.1.refs_3_, ...), custom_call_target="tpu_custom_call", output_to_operand_aliasing={{}: (3, {})} | custom-call | flops 1 | bytes 1 | tf_op jit(solution)/shard_map/cond/branch_1_fun/gradient_outer_0/pallas_call | solution.py:439
  70.3 1.6 %fetch.1.keep = f32[64,64,128]{2,1,0:T(8,128)S(1)} custom-call(f32[64,64,128]{2,1,0:T(8,128)} %get-tuple-element.180.source, f32[64,64,256]{2,1,0:T(8,128)} %get-tuple-element.196.after), custom_call_target="tpu_custom_call" | custom-call | flops 1 | bytes 1 | tf_op jit(solution)/shard_map/fetch/pallas_call | solution.py:460
  71.9 21.5 %collective-permute-done.37.arrived = f32[64,64,128]{2,1,0:T(8,128)} collective-permute-done((f32[64,64,128]{2,1,0:T(8,128)}, f32[64,64,128]{2,1,0:T(8,128)}, u32[]{:S(2)}, u32[]{:S(2)}) %collective-permute-start.37) | collective-permute-done | bytes 2097184 | tf_op jit(solution)/shard_map/ppermute | solution.py:629
  93.4 2.4 %barycenter.1 = f32[64,64,128]{2,1,0:T(8,128)} custom-call(f32[64,64,128]{2,1,0:T(8,128)S(1)} %fetch.1.keep, f32[64,64,128]{2,1,0:T(8,128)} %collective-permute-done.37.arrived), custom_call_target="tpu_custom_call" | custom-call | flops 1 | bytes 1 | tf_op jit(solution)/shard_map/barycenter/pallas_call | solution.py:489
Async XLA Ops:
  0.6 47.7 %collective-permute-start.36 = (f32[64,64,128]{2,1,0:T(8,128)}, f32[64,64,128]{2,1,0:T(8,128)S(1)}, u32[]{:S(2)}, u32[]{:S(2)}) collective-permute-start(f32[64,64,128]{2,1,0:T(8,128)} %param.15), channel_id=1, source_target_pairs={{0,16},{16,0},{1,17},{17,1},{2,18},{18,2},{3,19},{19,3},{4,20},{20... | collective-permute-start | bytes 6291464 | tf_op jit(solution)/shard_map/ppermute | solution.py:625
  4.7 7.6 %copy-start.1 = (f32[64,64,256]{2,1,0:T(8,128)S(1)}, f32[64,64,256]{2,1,0:T(8,128)}, u32[]{:S(2)}) copy-start(f32[64,64,256]{2,1,0:T(8,128)} %get-tuple-element.90.refs_0_) | copy-start | bytes 12582916 | tf_op jit(solution)/shard_map/cond
  4.7 7.5 %copy-start.14 = (s32[3]{0:T(128)S(1)}, s32[3]{0:T(128)}, u32[]{:S(2)}) copy-start(s32[3]{0:T(128)} %get-tuple-element.92.refs_1_.refs_2_) | copy-start | bytes 40 | tf_op jit(solution)/shard_map/cond
  8.2 15.3 %collective-permute-start.8 = (f32[8,64,256]{2,1,0:T(8,128)S(1)}, f32[8,64,256]{2,1,0:T(8,128)S(1)}, u32[]{:S(2)}, u32[]{:S(2)}) collective-permute-start(f32[8,64,256]{2,1,0:T(8,128)S(1)} %get-tuple-element.99), channel_id=1, source_target_pairs={{0,4},{8,12},{4,0},{12,8},{1,5},{9,13},{5,1},{13,9},{2,6},{10,14},... | collective-permute-start | bytes 1572872 | tf_op jit(solution)/shard_map/cond/branch_1_fun/ppermute | solution.py:505
  9.3 14.3 %collective-permute-start.9 = (f32[8,64,256]{2,1,0:T(8,128)S(1)}, f32[8,64,256]{2,1,0:T(8,128)S(1)}, u32[]{:S(2)}, u32[]{:S(2)}) collective-permute-start(f32[8,64,256]{2,1,0:T(8,128)S(1)} %get-tuple-element.100), channel_id=1, source_target_pairs={{4,8},{8,4},{5,9},{9,5},{6,10},{10,6},{7,11},{11,7},{20,24},{24,20... | collective-permute-start | bytes 1572872 | tf_op jit(solution)/shard_map/cond/branch_1_fun/ppermute | solution.py:505
  12.3 4.0 %copy-start.7 = (f32[64,64,256]{2,1,0:T(8,128)S(1)}, f32[64,64,256]{2,1,0:T(8,128)}, u32[]{:S(2)}) copy-start(f32[64,64,256]{2,1,0:T(8,128)} %get-tuple-element.93.refs_0_) | copy-start | bytes 12582916 | tf_op jit(solution)/shard_map/cond
  26.8 8.4 %collective-permute-start.10 = (f32[8,64,256]{2,1,0:T(8,128)S(1)}, f32[8,64,256]{2,1,0:T(8,128)S(1)}, u32[]{:S(2)}, u32[]{:S(2)}) collective-permute-start(f32[8,64,256]{2,1,0:T(8,128)S(1)} %get-tuple-element.105), channel_id=1, source_target_pairs={{0,4},{8,12},{4,0},{12,8},{1,5},{9,13},{5,1},{13,9},{2,6},{10,14},... | collective-permute-start | bytes 1572872 | tf_op jit(solution)/shard_map/cond/branch_1_fun/ppermute | solution.py:505
  26.9 10.8 %collective-permute-start.11 = (f32[8,64,256]{2,1,0:T(8,128)S(1)}, f32[8,64,256]{2,1,0:T(8,128)S(1)}, u32[]{:S(2)}, u32[]{:S(2)}) collective-permute-start(f32[8,64,256]{2,1,0:T(8,128)S(1)} %get-tuple-element.106), channel_id=1, source_target_pairs={{4,8},{8,4},{5,9},{9,5},{6,10},{10,6},{7,11},{11,7},{20,24},{24,20... | collective-permute-start | bytes 1572872 | tf_op jit(solution)/shard_map/cond/branch_1_fun/ppermute | solution.py:505
  41.5 51.9 %collective-permute-start.37 = (f32[64,64,128]{2,1,0:T(8,128)}, f32[64,64,128]{2,1,0:T(8,128)}, u32[]{:S(2)}, u32[]{:S(2)}) collective-permute-start(f32[64,64,128]{2,1,0:T(8,128)} %get-tuple-element.183), channel_id=1, source_target_pairs={{0,16},{16,0},{1,17},{17,1},{2,18},{18,2},{3,19},{19,3},{4,20},{20... | collective-permute-start | bytes 6291464 | tf_op jit(solution)/shard_map/ppermute | solution.py:629
  48.3 10.0 %copy-start.10 = (f32[64,64,256]{2,1,0:T(8,128)S(1)}, f32[64,64,256]{2,1,0:T(8,128)}, u32[]{:S(2)}) copy-start(f32[64,64,256]{2,1,0:T(8,128)} %get-tuple-element.151.refs_0_) | copy-start | bytes 12582916 | tf_op jit(solution)/shard_map/cond
  48.3 10.0 %copy-start.12 = (f32[64,64,128]{2,1,0:T(8,128)S(1)}, f32[64,64,128]{2,1,0:T(8,128)}, u32[]{:S(2)}) copy-start(f32[64,64,128]{2,1,0:T(8,128)} %get-tuple-element.154.refs_3_) | copy-start | bytes 6291460 | tf_op jit(solution)/shard_map/cond
  48.3 10.0 %copy-start.17 = (s32[3]{0:T(128)S(1)}, s32[3]{0:T(128)}, u32[]{:S(2)}) copy-start(s32[3]{0:T(128)} %get-tuple-element.150.refs_4_.refs_1_) | copy-start | bytes 40 | tf_op jit(solution)/shard_map/cond
  52.7 15.2 %collective-permute-start.28 = (f32[8,64,256]{2,1,0:T(8,128)S(1)}, f32[8,64,256]{2,1,0:T(8,128)S(1)}, u32[]{:S(2)}, u32[]{:S(2)}) collective-permute-start(f32[8,64,256]{2,1,0:T(8,128)S(1)} %get-tuple-element.158), channel_id=1, source_target_pairs={{0,4},{8,12},{4,0},{12,8},{1,5},{9,13},{5,1},{13,9},{2,6},{10,14},... | collective-permute-start | bytes 1572872 | tf_op jit(solution)/shard_map/cond/branch_1_fun/ppermute | solution.py:505
  54.8 13.1 %collective-permute-start.29 = (f32[8,64,256]{2,1,0:T(8,128)S(1)}, f32[8,64,256]{2,1,0:T(8,128)S(1)}, u32[]{:S(2)}, u32[]{:S(2)}) collective-permute-start(f32[8,64,256]{2,1,0:T(8,128)S(1)} %get-tuple-element.159), channel_id=1, source_target_pairs={{4,8},{8,4},{5,9},{9,5},{6,10},{10,6},{7,11},{11,7},{20,24},{24,20... | collective-permute-start | bytes 1572872 | tf_op jit(solution)/shard_map/cond/branch_1_fun/ppermute | solution.py:505
  58.4 5.3 %copy-start.4 = (f32[64,64,256]{2,1,0:T(8,128)S(1)}, f32[64,64,256]{2,1,0:T(8,128)}, u32[]{:S(2)}) copy-start(f32[64,64,256]{2,1,0:T(8,128)} %get-tuple-element.149.refs_0_) | copy-start | bytes 12582916 | tf_op jit(solution)/shard_map/cond

commit v3 on v2

--- a/solution.py
+++ b/solution.py
@@ -13,6 +13,8 @@
 HALO = 2 * BLOCK
 SIGMA = 3.0
 SUB = 8
+SUB_BITS = 3
+XOUT = 16
 GROUP = 8
 SLOTS = 4
 F32 = jnp.float32
@@ -100,6 +102,16 @@
     return dot(ky[...], jnp.concatenate(pieces, axis=0))
 
 
+def fill_x(ref, reach):
+    m = (XOUT + 2 * HALO) * SUB
+    i, j = iotas((XOUT * SUB, m))
+    value = jnp.where((i & (SUB - 1)) == (j & (SUB - 1)), weight((i >> SUB_BITS) + HALO, j >> SUB_BITS, reach), 0.0)
+    high, low = halves(value)
+    ref[:, 0:m] = high
+    ref[:, m : 2 * m] = high
+    ref[:, 2 * m : 3 * m] = low
+
+
 def x_sum(plane, n, reach):
     phase = n % BLOCK
     span = BLOCK * reach
@@ -113,7 +125,7 @@
     return total
 
 
-MATRICES = ("kz", "ky", "ky0")
+MATRICES = ("kz", "ky", "ky0", "kx")
 EDGES = ("even", "odd", "y_even", "y_odd", "corner_even", "corner_odd")
 INSIDE = ("warm", "inputs", "d", "far", "u", "u_out", "u_out_in", *EDGES, *(edge + "_out" for edge in EDGES), *MATRICES)
 BOTH = (0, 1)
@@ -140,12 +152,18 @@
             shapes["ky0"] = (ny, y_depth(ny, 0))
         else:
             shapes["ky"] = (ny, y_depth(ny, HALO))
+        if self.send == BOTH:
+            shapes["kx"] = (XOUT * SUB, 3 * (XOUT + 2 * HALO) * SUB)
         return shapes
+
+    def by_blocks(self):
+        return self.kind == "none" and self.part == "inner" and (self.shape[0] - 2 * HALO) % XOUT == 0
 
     def needs(self):
         if self.fills:
             return ()
         wanted = {"kz": 2 in self.start, "ky": self.finish in (1, BOTH), "ky0": 1 in self.start}
+        wanted["kx"] = self.by_blocks()
         return tuple(key for key in wanted if wanted[key])
 
     def scratch(self):
@@ -319,6 +337,18 @@
             for swap, name in enumerate(names):
                 r[name][pl.ds(x0, GROUP)] = out[pl.ds(x0, GROUP), edge(1, swap, ny)]
 
+    def blocks(self, r):
+        nx, _, nz = self.shape
+        wide = XOUT + 2 * HALO
+
+        def body(rows):
+            for x in range(0, nx - 2 * HALO, XOUT):
+                high, low = halves(r["u"][x : x + wide, rows].reshape(wide * SUB, nz))
+                product = dot(r["kx"][...], jnp.concatenate([high, low, high], axis=0))
+                r["u_out"][x + HALO : x + HALO + XOUT, rows] = product.reshape(XOUT, SUB, nz)
+
+        self.tiles(body)
+
     def complete(self, r, parts, planes):
         if "u_out_in" not in r:
             return
@@ -332,6 +362,9 @@
         lax.fori_loop(0, len(others), copy, 0)
 
     def body(self, r):
+        if self.by_blocks():
+            self.blocks(r)
+            return
         last = self.groups - 1
         parts = {"all": range(last + 1), "inner": range(1, last), "outer": range(0, last + 1, max(last, 1))}
         groups = parts[self.part]
@@ -362,6 +395,8 @@
                 fill_y(r["ky"], r["reach"][1], HALO)
             if "ky0" in r:
                 fill_y(r["ky0"], 0, 0)
+            if "kx" in r:
+                fill_x(r["kx"], r["reach"][0])
         nx = self.shape[0]
         for swap, name in enumerate(("even", "odd")):
             if "sides" in r:

time: 97.4 us -> 97.4 us (level)
  Pallas kernels: 47.4 us -> 53.2 us
  waiting for transfers between devices: 30.5 us -> 24.8 us
    pallas_call x10, Pallas kernels: 43.4 us -> 49.1 us  [__call__(): pl.pallas_call(lambda *refs: self.body(dict(zip(names, refs))), name=name...]
    ppermute x1, waiting for transfers between devices: 6.55 us -> 4.21 us  [per_device(): far = lax.ppermute(bary_cotangent, 'inp', SWAP)]
    ppermute x1, waiting for transfers between devices: 21.5 us -> 19.5 us  [per_device(): arrived = lax.ppermute(send, 'inp', SWAP)]
    ppermute x6, waiting for transfers between devices: 2.51 us -> 1.05 us  [neighbours(): lax.ppermute(value, AXES[line], pairs + [(j, i) for i, j in pairs])]
  transfers between devices with their start and end apart: 8 -> 8, of which waited for: 3 -> 3; matrix products, arithmetic and copies ran while one was open for 1% -> 1% of each run, Pallas kernels for 47% -> 53%
where the time goes in v3:
time: 97.4 us; the launch traced here: 96 us
  Pallas kernels  53.2 us (55%)
  waiting for transfers between devices  24.8 us (25%)
  starting transfers between devices  14.8 us (15%)
  between operations  1.47 us (2%)
  other arithmetic  1.29 us (1%)
    pallas_call x10, Pallas kernels, __call__(): pl.pallas_call(lambda *refs: self.body(dict(zip(names, refs))), name=name...  49.1 us
    ppermute x1, waiting for transfers between devices, per_device(): arrived = lax.ppermute(send, 'inp', SWAP)  19.5 us
    ppermute x6, starting transfers between devices, neighbours(): lax.ppermute(value, AXES[line], pairs + [(j, i) for i, j in pairs])  12.3 us
    ppermute x1, waiting for transfers between devices, per_device(): far = lax.ppermute(bary_cotangent, 'inp', SWAP)  4.21 us
    pallas_call x1, Pallas kernels, add(): pl.pallas_call(add_body, name='barycenter', out_shape=pltpu.HBM(keep.shap...  2.42 us
    ppermute x1, starting transfers between devices, per_device(): far = lax.ppermute(bary_cotangent, 'inp', SWAP)  2.13 us
  transfers between devices with their start and end apart: 8, of which 3 were waited for; matrix products, arithmetic and copies ran while one was open for 1% of the time, Pallas kernels for 53%

profile of v3, /device:TPU:1, one launch (start us, length us, event | category | flops | bytes accessed | tf_op | source)
XLA Modules:
  0.0 96.0 jit_solution(15301729079888847330)
XLA Ops:
  0.6 2.1 %collective-permute-start.36 = (f32[64,64,128]{2,1,0:T(8,128)}, f32[64,64,128]{2,1,0:T(8,128)S(1)}, u32[]{:S(2)}, u32[]{:S(2)}) collective-permute-start(f32[64,64,128]{2,1,0:T(8,128)} %param.15), channel_id=1, source_target_pairs={{0,16},{16,0},{1,17},{17,1},{2,18},{18,2},{3,19},{19,3},{4,20},{20... | collective-permute-start | bytes 6291464 | tf_op jit(solution)/shard_map/ppermute | solution.py:660
  2.8 1.3 %fusion = s32[]{:T(128)} fusion(s32[3]{0:T(128)} %param.14), kind=kLoop, calls=%fused_computation.1 | loop fusion | flops 8 | bytes 16 | tf_op jit(solution)/shard_map/reduce_sum | solution.py:657
  4.7 39.1 %conditional.2 = (f32[64,64,128]{2,1,0:T(8,128)}, f32[64,64,128]{2,1,0:T(8,128)}, f32[64,64,256]{2,1,0:T(8,128)}, f32[64,64,256]{2,1,0:T(8,128)}) conditional(s32[]{:T(128)} %clamp.4, (f32[64,64,256]{2,1,0:T(8,128)}, s32[3]{0:T(128)}, f32[64,64,256]{2,1,0:T(8,128)}, f32[1]{0:T(128)}) %tuple.41, (f32[64,64,256]{2,1,0:T(8,128)}, ...), branch_computations={%region_1.2_spmd, %region_2.3_spmd, %region_3.4_spmd} | conditional | flops 9 | bytes 52429444 | solution.py:661
  4.7 0.0 copy-start.1
  4.7 0.0 copy-start.14
  4.8 3.5 %scaling_outer_0.1 = (f32[64,64,256]{2,1,0:T(8,128)S(1)}, f32[8,64,256]{2,1,0:T(8,128)S(1)}, f32[8,64,256]{2,1,0:T(8,128)S(1)}, bf16[768,256]{1,0:T(8,128)(2,1)S(1)}, bf16[64,192]{1,0:T(8,128)(2,1)S(1)}) custom-call(f32[64,64,256]{2,1,0:T(8,128)} %get-tuple-element.90.refs_0_, s32[3]{0:T(128)} %get-tuple-element.92.refs_1_.refs_2_), custom_call_target="tpu_custom_call" | custom-call | flops 1 | bytes 1 | tf_op jit(solution)/shard_map/cond/branch_1_fun/scaling_outer_0/pallas_call | solution.py:474
  8.2 1.0 %collective-permute-start.8 = (f32[8,64,256]{2,1,0:T(8,128)S(1)}, f32[8,64,256]{2,1,0:T(8,128)S(1)}, u32[]{:S(2)}, u32[]{:S(2)}) collective-permute-start(f32[8,64,256]{2,1,0:T(8,128)S(1)} %get-tuple-element.99), channel_id=1, source_target_pairs={{0,4},{8,12},{4,0},{12,8},{1,5},{9,13},{5,1},{13,9},{2,6},{10,14},... | collective-permute-start | bytes 1572872 | tf_op jit(solution)/shard_map/cond/branch_1_fun/ppermute | solution.py:540
  9.3 3.0 %collective-permute-start.9 = (f32[8,64,256]{2,1,0:T(8,128)S(1)}, f32[8,64,256]{2,1,0:T(8,128)S(1)}, u32[]{:S(2)}, u32[]{:S(2)}) collective-permute-start(f32[8,64,256]{2,1,0:T(8,128)S(1)} %get-tuple-element.100), channel_id=1, source_target_pairs={{4,8},{8,4},{5,9},{9,5},{6,10},{10,6},{7,11},{11,7},{20,24},{24,20... | collective-permute-start | bytes 1572872 | tf_op jit(solution)/shard_map/cond/branch_1_fun/ppermute | solution.py:540
  12.3 0.0 copy-done.1
  12.3 0.0 copy-done.14
  12.3 0.0 copy-start.7
  12.3 3.9 %scaling_inner_0.1.refs_2_ = f32[64,64,256]{2,1,0:T(8,128)S(1)} custom-call(f32[64,64,256]{2,1,0:T(8,128)S(1)} %copy-done.1, s32[3]{0:T(128)S(1)} %copy-done.14, f32[64,64,256]{2,1,0:T(8,128)S(1)} %get-tuple-element.94.refs_2_, bf16[768,256]{1,0:T(8,128)(2,1)S(1)} %get-tuple-element.95.refs_3_.refs_7_, ...), custom_call_target="tpu_custom_call", output_to_operand_aliasing={{}: (2, {})} | custom-call | flops 1 | bytes 1 | tf_op jit(solution)/shard_map/cond/branch_1_fun/scaling_inner_0/pallas_call | solution.py:474
  16.3 0.0 copy-done.7
  16.3 8.7 %dual_inner_0.1 = (f32[64,64,256]{2,1,0:T(8,128)}, f32[64,64,256]{2,1,0:T(8,128)S(1)}) custom-call(f32[64,64,256]{2,1,0:T(8,128)S(1)} %copy-done.7, s32[3]{0:T(128)S(1)} %copy-done.14, f32[64,64,256]{2,1,0:T(8,128)S(1)} %scaling_inner_0.1.refs_2_, bf16[768,256]{1,0:T(8,128)(2,1)S(1)} %get-tuple-element.95.refs_3_.refs_7_, ...), custom_call_target="tpu_custom_call" | custom-call | flops 1 | bytes 1 | tf_op jit(solution)/shard_map/cond/branch_1_fun/dual_inner_0/pallas_call | solution.py:474
  24.9 0.0 collective-permute-done.8.refs_5_
  24.9 0.0 collective-permute-done.9.refs_6_
  25.0 3.7 %dual_outer_0.1 = (f32[64,64,256]{2,1,0:T(8,128)}, f32[64,64,256]{2,1,0:T(8,128)S(1)}, f32[8,64,256]{2,1,0:T(8,128)S(1)}, f32[8,64,256]{2,1,0:T(8,128)S(1)}) custom-call(f32[64,64,256]{2,1,0:T(8,128)S(1)} %copy-done.7, s32[3]{0:T(128)S(1)} %copy-done.14, f32[64,64,256]{2,1,0:T(8,128)S(1)} %scaling_inner_0.1.refs_2_, ...), custom_call_target="tpu_custom_call", output_to_operand_aliasing={{0}: (3, {}), {1}: (4, {})} | custom-call | flops 1 | bytes 1 | tf_op jit(solution)/shard_map/cond/branch_1_fun/dual_outer_0/pallas_call | solution.py:474
  28.7 0.1 collective-permute-start.10
  28.8 2.5 %collective-permute-start.11 = (f32[8,64,256]{2,1,0:T(8,128)S(1)}, f32[8,64,256]{2,1,0:T(8,128)S(1)}, u32[]{:S(2)}, u32[]{:S(2)}) collective-permute-start(f32[8,64,256]{2,1,0:T(8,128)S(1)} %get-tuple-element.106), channel_id=1, source_target_pairs={{4,8},{8,4},{5,9},{9,5},{6,10},{10,6},{7,11},{11,7},{20,24},{24,20... | collective-permute-start | bytes 1572872 | tf_op jit(solution)/shard_map/cond/branch_1_fun/ppermute | solution.py:540
  31.3 7.2 %partial_inner_0.1 = (f32[64,64,128]{2,1,0:T(8,128)}, f32[64,64,128]{2,1,0:T(8,128)}, f32[64,64,256]{2,1,0:T(8,128)}) custom-call(f32[64,64,256]{2,1,0:T(8,128)S(1)} %copy-done.1, f32[1]{0:T(128)} %get-tuple-element.91.refs_1_, s32[3]{0:T(128)S(1)} %copy-done.14, f32[64,64,256]{2,1,0:T(8,128)S(1)} %get-tuple-element.101.refs_3_), custom_call_target="tpu_custom_call" | custom-call | flops 1 | bytes 1 | tf_op jit(solution)/shard_map/cond/branch_1_fun/partial_inner_0/pallas_call | solution.py:474
  38.5 0.0 collective-permute-done.10.refs_7_
  38.5 1.0 %collective-permute-done.11.refs_8_ = f32[8,64,256]{2,1,0:T(8,128)S(1)} collective-permute-done((f32[8,64,256]{2,1,0:T(8,128)S(1)}, f32[8,64,256]{2,1,0:T(8,128)S(1)}, u32[]{:S(2)}, u32[]{:S(2)}) %collective-permute-start.11) | collective-permute-done | bytes 524320 | tf_op jit(solution)/shard_map/cond/branch_1_fun/ppermute | solution.py:540
  39.6 4.1 %partial_outer_0.1 = (f32[64,64,128]{2,1,0:T(8,128)}, f32[64,64,128]{2,1,0:T(8,128)}, f32[64,64,256]{2,1,0:T(8,128)}) custom-call(f32[64,64,256]{2,1,0:T(8,128)S(1)} %copy-done.1, f32[1]{0:T(128)} %get-tuple-element.91.refs_1_, s32[3]{0:T(128)S(1)} %copy-done.14, ...), custom_call_target="tpu_custom_call", output_to_operand_aliasing={{0}: (4, {}), {1}: (5, {}), {2}: (6, {})} | custom-call | flops 1 | bytes 1 | tf_op jit(solution)/shard_map/cond/branch_1_fun/partial_outer_0/pallas_call | solution.py:474
  43.8 0.3 collective-permute-start.37
  44.1 4.2 %collective-permute-done.36 = f32[64,64,128]{2,1,0:T(8,128)S(1)} collective-permute-done((f32[64,64,128]{2,1,0:T(8,128)}, f32[64,64,128]{2,1,0:T(8,128)S(1)}, u32[]{:S(2)}, u32[]{:S(2)}) %collective-permute-start.36) | collective-permute-done | bytes 2097184 | tf_op jit(solution)/shard_map/ppermute | solution.py:660
  48.3 23.9 %conditional.3 = (f32[64,64,256]{2,1,0:T(8,128)}) conditional(s32[]{:T(128)} %clamp.4, (f32[64,64,256]{2,1,0:T(8,128)}, f32[1]{0:T(128)}, f32[64,64,128]{2,1,0:T(8,128)S(1)}, f32[64,64,128]{2,1,0:T(8,128)}, s32[3]{0:T(128)}, /*index=5*/f32[64,64,256]{2,1,0:T(8,128)}) %tuple.30, (f32[64,64,256]{2,1,0:T(8,128)}, f32[1]{0:T(128)}, ...), branch_computations={%region_4.5_spmd, %region_5.6_spmd, %region_6.7_spmd} | conditional | flops 5 | bytes 46137672 | solution.py:665
  48.3 0.0 copy-start.10
  48.3 0.0 copy-start.12
  48.3 0.0 copy-start.17
  48.3 4.3 %cotangent_outer_0.1 = (f32[64,64,256]{2,1,0:T(8,128)S(1)}, f32[8,64,256]{2,1,0:T(8,128)S(1)}, f32[8,64,256]{2,1,0:T(8,128)S(1)}, bf16[768,256]{1,0:T(8,128)(2,1)S(1)}, bf16[64,192]{1,0:T(8,128)(2,1)S(1)}) custom-call(f32[64,64,256]{2,1,0:T(8,128)} %get-tuple-element.152.refs_0_, f32[1]{0:T(128)} %get-tuple-element.153.refs_1_, ...), custom_call_target="tpu_custom_call" | custom-call | flops 1 | bytes 1 | tf_op jit(solution)/shard_map/cond/branch_1_fun/cotangent_outer_0/pallas_call | solution.py:474
  52.7 2.1 %collective-permute-start.28 = (f32[8,64,256]{2,1,0:T(8,128)S(1)}, f32[8,64,256]{2,1,0:T(8,128)S(1)}, u32[]{:S(2)}, u32[]{:S(2)}) collective-permute-start(f32[8,64,256]{2,1,0:T(8,128)S(1)} %get-tuple-element.159), channel_id=1, source_target_pairs={{0,4},{8,12},{4,0},{12,8},{1,5},{9,13},{5,1},{13,9},{2,6},{10,14},... | collective-permute-start | bytes 1572872 | tf_op jit(solution)/shard_map/cond/branch_1_fun/ppermute | solution.py:540
  54.8 3.6 %collective-permute-start.29 = (f32[8,64,256]{2,1,0:T(8,128)S(1)}, f32[8,64,256]{2,1,0:T(8,128)S(1)}, u32[]{:S(2)}, u32[]{:S(2)}) collective-permute-start(f32[8,64,256]{2,1,0:T(8,128)S(1)} %get-tuple-element.160), channel_id=1, source_target_pairs={{4,8},{8,4},{5,9},{9,5},{6,10},{10,6},{7,11},{11,7},{20,24},{24,20... | collective-permute-start | bytes 1572872 | tf_op jit(solution)/shard_map/cond/branch_1_fun/ppermute | solution.py:540
  58.4 0.0 copy-done.10
  58.4 0.0 copy-done.12
  58.4 0.0 copy-done.17
  58.4 0.0 copy-start.4
  58.4 5.3 %cotangent_inner_0.1.refs_2_ = f32[64,64,256]{2,1,0:T(8,128)S(1)} custom-call(f32[64,64,256]{2,1,0:T(8,128)S(1)} %copy-done.10, f32[1]{0:T(128)} %get-tuple-element.153.refs_1_, f32[64,64,128]{2,1,0:T(8,128)S(1)} %get-tuple-element.154.refs_2_, f32[64,64,128]{2,1,0:T(8,128)S(1)} %copy-done.12, s32[3]{0:T(128)S(1)} %copy-done.17, ...), custom_call_target="tpu_custom_call", output_to_operand_aliasing={{}: (5, {})} | custom-call | flops 1 | bytes 1 | tf_op jit(solution)/shard_map/cond/branch_1_fun/cotangent_inner_0/pallas_call | solution.py:474
  63.7 0.0 copy-done.4
  63.7 5.6 %gradient_inner_0.1.refs_3_ = f32[64,64,256]{2,1,0:T(8,128)} custom-call(f32[64,64,256]{2,1,0:T(8,128)S(1)} %copy-done.4, s32[3]{0:T(128)S(1)} %copy-done.17, f32[64,64,256]{2,1,0:T(8,128)S(1)} %cotangent_inner_0.1.refs_2_), custom_call_target="tpu_custom_call" | custom-call | flops 1 | bytes 1 | tf_op jit(solution)/shard_map/cond/branch_1_fun/gradient_inner_0/pallas_call | solution.py:474
  69.3 0.0 collective-permute-done.28.refs_4_
  69.3 0.0 collective-permute-done.29.refs_5_
  69.3 2.9 %gradient_outer_0.1 = f32[64,64,256]{2,1,0:T(8,128)} custom-call(f32[64,64,256]{2,1,0:T(8,128)S(1)} %copy-done.4, s32[3]{0:T(128)S(1)} %copy-done.17, f32[64,64,256]{2,1,0:T(8,128)S(1)} %cotangent_inner_0.1.refs_2_, f32[64,64,256]{2,1,0:T(8,128)} %gradient_inner_0.1.refs_3_, ...), custom_call_target="tpu_custom_call", output_to_operand_aliasing={{}: (3, {})} | custom-call | flops 1 | bytes 1 | tf_op jit(solution)/shard_map/cond/branch_1_fun/gradient_outer_0/pallas_call | solution.py:474
  72.2 1.6 %fetch.1.keep = f32[64,64,128]{2,1,0:T(8,128)S(1)} custom-call(f32[64,64,128]{2,1,0:T(8,128)} %get-tuple-element.182.source, f32[64,64,256]{2,1,0:T(8,128)} %get-tuple-element.198.after), custom_call_target="tpu_custom_call" | custom-call | flops 1 | bytes 1 | tf_op jit(solution)/shard_map/fetch/pallas_call | solution.py:495
  73.8 19.5 %collective-permute-done.37.arrived = f32[64,64,128]{2,1,0:T(8,128)} collective-permute-done((f32[64,64,128]{2,1,0:T(8,128)}, f32[64,64,128]{2,1,0:T(8,128)}, u32[]{:S(2)}, u32[]{:S(2)}) %collective-permute-start.37) | collective-permute-done | bytes 2097184 | tf_op jit(solution)/shard_map/ppermute | solution.py:664
  93.4 2.4 %barycenter.1 = f32[64,64,128]{2,1,0:T(8,128)} custom-call(f32[64,64,128]{2,1,0:T(8,128)S(1)} %fetch.1.keep, f32[64,64,128]{2,1,0:T(8,128)} %collective-permute-done.37.arrived), custom_call_target="tpu_custom_call" | custom-call | flops 1 | bytes 1 | tf_op jit(solution)/shard_map/barycenter/pallas_call | solution.py:524
Async XLA Ops:
  0.6 47.7 %collective-permute-start.36 = (f32[64,64,128]{2,1,0:T(8,128)}, f32[64,64,128]{2,1,0:T(8,128)S(1)}, u32[]{:S(2)}, u32[]{:S(2)}) collective-permute-start(f32[64,64,128]{2,1,0:T(8,128)} %param.15), channel_id=1, source_target_pairs={{0,16},{16,0},{1,17},{17,1},{2,18},{18,2},{3,19},{19,3},{4,20},{20... | collective-permute-start | bytes 6291464 | tf_op jit(solution)/shard_map/ppermute | solution.py:660
  4.7 7.6 %copy-start.1 = (f32[64,64,256]{2,1,0:T(8,128)S(1)}, f32[64,64,256]{2,1,0:T(8,128)}, u32[]{:S(2)}) copy-start(f32[64,64,256]{2,1,0:T(8,128)} %get-tuple-element.90.refs_0_) | copy-start | bytes 12582916 | tf_op jit(solution)/shard_map/cond
  4.7 7.5 %copy-start.14 = (s32[3]{0:T(128)S(1)}, s32[3]{0:T(128)}, u32[]{:S(2)}) copy-start(s32[3]{0:T(128)} %get-tuple-element.92.refs_1_.refs_2_) | copy-start | bytes 40 | tf_op jit(solution)/shard_map/cond
  8.2 16.7 %collective-permute-start.8 = (f32[8,64,256]{2,1,0:T(8,128)S(1)}, f32[8,64,256]{2,1,0:T(8,128)S(1)}, u32[]{:S(2)}, u32[]{:S(2)}) collective-permute-start(f32[8,64,256]{2,1,0:T(8,128)S(1)} %get-tuple-element.99), channel_id=1, source_target_pairs={{0,4},{8,12},{4,0},{12,8},{1,5},{9,13},{5,1},{13,9},{2,6},{10,14},... | collective-permute-start | bytes 1572872 | tf_op jit(solution)/shard_map/cond/branch_1_fun/ppermute | solution.py:540
  9.3 15.7 %collective-permute-start.9 = (f32[8,64,256]{2,1,0:T(8,128)S(1)}, f32[8,64,256]{2,1,0:T(8,128)S(1)}, u32[]{:S(2)}, u32[]{:S(2)}) collective-permute-start(f32[8,64,256]{2,1,0:T(8,128)S(1)} %get-tuple-element.100), channel_id=1, source_target_pairs={{4,8},{8,4},{5,9},{9,5},{6,10},{10,6},{7,11},{11,7},{20,24},{24,20... | collective-permute-start | bytes 1572872 | tf_op jit(solution)/shard_map/cond/branch_1_fun/ppermute | solution.py:540
  12.3 4.0 %copy-start.7 = (f32[64,64,256]{2,1,0:T(8,128)S(1)}, f32[64,64,256]{2,1,0:T(8,128)}, u32[]{:S(2)}) copy-start(f32[64,64,256]{2,1,0:T(8,128)} %get-tuple-element.93.refs_0_) | copy-start | bytes 12582916 | tf_op jit(solution)/shard_map/cond
  28.7 9.8 %collective-permute-start.10 = (f32[8,64,256]{2,1,0:T(8,128)S(1)}, f32[8,64,256]{2,1,0:T(8,128)S(1)}, u32[]{:S(2)}, u32[]{:S(2)}) collective-permute-start(f32[8,64,256]{2,1,0:T(8,128)S(1)} %get-tuple-element.105), channel_id=1, source_target_pairs={{0,4},{8,12},{4,0},{12,8},{1,5},{9,13},{5,1},{13,9},{2,6},{10,14},... | collective-permute-start | bytes 1572872 | tf_op jit(solution)/shard_map/cond/branch_1_fun/ppermute | solution.py:540
  28.8 10.8 %collective-permute-start.11 = (f32[8,64,256]{2,1,0:T(8,128)S(1)}, f32[8,64,256]{2,1,0:T(8,128)S(1)}, u32[]{:S(2)}, u32[]{:S(2)}) collective-permute-start(f32[8,64,256]{2,1,0:T(8,128)S(1)} %get-tuple-element.106), channel_id=1, source_target_pairs={{4,8},{8,4},{5,9},{9,5},{6,10},{10,6},{7,11},{11,7},{20,24},{24,20... | collective-permute-start | bytes 1572872 | tf_op jit(solution)/shard_map/cond/branch_1_fun/ppermute | solution.py:540
  43.8 49.5 %collective-permute-start.37 = (f32[64,64,128]{2,1,0:T(8,128)}, f32[64,64,128]{2,1,0:T(8,128)}, u32[]{:S(2)}, u32[]{:S(2)}) collective-permute-start(f32[64,64,128]{2,1,0:T(8,128)} %get-tuple-element.185), channel_id=1, source_target_pairs={{0,16},{16,0},{1,17},{17,1},{2,18},{18,2},{3,19},{19,3},{4,20},{20... | collective-permute-start | bytes 6291464 | tf_op jit(solution)/shard_map/ppermute | solution.py:664
  48.3 10.0 %copy-start.10 = (f32[64,64,256]{2,1,0:T(8,128)S(1)}, f32[64,64,256]{2,1,0:T(8,128)}, u32[]{:S(2)}) copy-start(f32[64,64,256]{2,1,0:T(8,128)} %get-tuple-element.152.refs_0_) | copy-start | bytes 12582916 | tf_op jit(solution)/shard_map/cond
  48.3 10.0 %copy-start.12 = (f32[64,64,128]{2,1,0:T(8,128)S(1)}, f32[64,64,128]{2,1,0:T(8,128)}, u32[]{:S(2)}) copy-start(f32[64,64,128]{2,1,0:T(8,128)} %get-tuple-element.155.refs_3_) | copy-start | bytes 6291460 | tf_op jit(solution)/shard_map/cond
  48.3 10.0 %copy-start.17 = (s32[3]{0:T(128)S(1)}, s32[3]{0:T(128)}, u32[]{:S(2)}) copy-start(s32[3]{0:T(128)} %get-tuple-element.151.refs_4_.refs_1_) | copy-start | bytes 40 | tf_op jit(solution)/shard_map/cond
  52.7 16.6 %collective-permute-start.28 = (f32[8,64,256]{2,1,0:T(8,128)S(1)}, f32[8,64,256]{2,1,0:T(8,128)S(1)}, u32[]{:S(2)}, u32[]{:S(2)}) collective-permute-start(f32[8,64,256]{2,1,0:T(8,128)S(1)} %get-tuple-element.159), channel_id=1, source_target_pairs={{0,4},{8,12},{4,0},{12,8},{1,5},{9,13},{5,1},{13,9},{2,6},{10,14},... | collective-permute-start | bytes 1572872 | tf_op jit(solution)/shard_map/cond/branch_1_fun/ppermute | solution.py:540
  54.8 14.5 %collective-permute-start.29 = (f32[8,64,256]{2,1,0:T(8,128)S(1)}, f32[8,64,256]{2,1,0:T(8,128)S(1)}, u32[]{:S(2)}, u32[]{:S(2)}) collective-permute-start(f32[8,64,256]{2,1,0:T(8,128)S(1)} %get-tuple-element.160), channel_id=1, source_target_pairs={{4,8},{8,4},{5,9},{9,5},{6,10},{10,6},{7,11},{11,7},{20,24},{24,20... | collective-permute-start | bytes 1572872 | tf_op jit(solution)/shard_map/cond/branch_1_fun/ppermute | solution.py:540
  58.4 5.3 %copy-start.4 = (f32[64,64,256]{2,1,0:T(8,128)S(1)}, f32[64,64,256]{2,1,0:T(8,128)}, u32[]{:S(2)}) copy-start(f32[64,64,256]{2,1,0:T(8,128)} %get-tuple-element.150.refs_0_) | copy-start | bytes 12582916 | tf_op jit(solution)/shard_map/cond

commit v4 on v2

--- a/solution.py
+++ b/solution.py
@@ -492,7 +492,7 @@
         out_shape=pltpu.HBM(keep.shape, F32),
         in_specs=[pl.BlockSpec(memory_space=pltpu.VMEM), pl.BlockSpec(memory_space=pl.ANY)],
         out_specs=pl.BlockSpec(memory_space=pltpu.HBM),
-        scratch_shapes=[pltpu.VMEM(keep.shape, F32), pltpu.SemaphoreType.DMA((2, 8))],
+        scratch_shapes=[pltpu.VMEM(keep.shape, F32), pltpu.SemaphoreType.DMA((2, 16))],
         compiler_params=pltpu.CompilerParams(vmem_limit_bytes=8 * 2**20),
         cost_estimate=COST,
     )(pltpu.with_memory_space_constraint(keep, pltpu.VMEM), arrived)

time: 97.4 us -> 116 us (1.19)
  the two profiles are of different devices: /device:TPU:1 before, /device:TPU:17 now
where the time goes in v4:
time: 116 us
  Pallas kernels  55 us (47%)
  waiting for transfers between devices  31 us (27%)
  starting transfers between devices  26.5 us (23%)
  between operations  1.47 us (1%)
  other arithmetic  1.29 us (1%)
    pallas_call x11, Pallas kernels, __call__(): pl.pallas_call(lambda *refs: self.body(dict(zip(names, refs))), name=name...  50.8 us
    ppermute x18, starting transfers between devices, neighbours(): lax.ppermute(value, AXES[line], pairs + [(j, i) for i, j in pairs])  24.9 us
    ppermute x18, waiting for transfers between devices, neighbours(): lax.ppermute(value, AXES[line], pairs + [(j, i) for i, j in pairs])  17.1 us
    ppermute x1, waiting for transfers between devices, per_device(): arrived = lax.ppermute(send, 'inp', SWAP)  13.9 us
    pallas_call x1, Pallas kernels, add(): pl.pallas_call(add_body, name='barycenter', out_shape=pltpu.HBM(keep.shap...  2.58 us
  transfers between devices with their start and end apart: 20, of which 11 were waited for; matrix products, arithmetic and copies ran while one was open for 1% of the time, Pallas kernels for 45%

profile of v4, /device:TPU:17, one launch (start us, length us, event | category | flops | bytes accessed | tf_op | source)
XLA Modules:
  0.0 115.8 jit_solution(15629651193081922363)
XLA Ops:
  0.6 1.3 %collective-permute-start.36 = (f32[64,64,128]{2,1,0:T(8,128)}, f32[64,64,128]{2,1,0:T(8,128)S(1)}, u32[]{:S(2)}, u32[]{:S(2)}) collective-permute-start(f32[64,64,128]{2,1,0:T(8,128)} %param.15), channel_id=1, source_target_pairs={{0,16},{16,0},{1,17},{17,1},{2,18},{18,2},{3,19},{19,3},{4,20},{20... | collective-permute-start | bytes 6291464 | tf_op jit(solution)/shard_map/ppermute | solution.py:625
  1.9 1.3 %fusion = s32[]{:T(128)} fusion(s32[3]{0:T(128)} %param.14), kind=kLoop, calls=%fused_computation.1 | loop fusion | flops 8 | bytes 16 | tf_op jit(solution)/shard_map/reduce_sum | solution.py:622
  3.9 61.3 %conditional.2 = (f32[64,64,128]{2,1,0:T(8,128)}, f32[64,64,128]{2,1,0:T(8,128)}, f32[64,64,256]{2,1,0:T(8,128)}, f32[64,64,256]{2,1,0:T(8,128)}) conditional(s32[]{:T(128)} %clamp.4, (f32[64,64,256]{2,1,0:T(8,128)}, s32[3]{0:T(128)}, f32[64,64,256]{2,1,0:T(8,128)}, f32[1]{0:T(128)}) %tuple.41, (f32[64,64,256]{2,1,0:T(8,128)}, ...), branch_computations={%region_1.2_spmd, %region_2.3_spmd, %region_3.4_spmd} | conditional | flops 9 | bytes 52429444 | solution.py:626
  3.9 5.1 %scaling_0.3 = (f32[64,64,256]{2,1,0:T(8,128)S(1)}, f32[8,64,256]{2,1,0:T(8,128)S(1)}, f32[8,64,256]{2,1,0:T(8,128)S(1)}, f32[64,8,256]{2,1,0:T(8,128)S(1)}, f32...) custom-call(f32[64,64,256]{2,1,0:T(8,128)} %get-tuple-element.111.refs_0_, ...), custom_call_target="tpu_custom_call" | custom-call | flops 1 | bytes 1 | tf_op jit(solution)/shard_map/cond/branch_2_fun/scaling_0/pallas_call | solution.py:439
  9.0 1.0 collective-permute-start.12
  10.1 3.0 %collective-permute-start.13 = (f32[8,64,256]{2,1,0:T(8,128)S(1)}, f32[8,64,256]{2,1,0:T(8,128)S(1)}, u32[]{:S(2)}, u32[]{:S(2)}) collective-permute-start(f32[8,64,256]{2,1,0:T(8,128)S(1)} %get-tuple-element.117), channel_id=1, source_target_pairs={{4,8},{8,4},{5,9},{9,5},{6,10},{10,6},{7,11},{11,7},{20,24},{24,20... | collective-permute-start | bytes 1572872 | tf_op jit(solution)/shard_map/cond/branch_2_fun/ppermute | solution.py:505
  13.1 1.3 %collective-permute-start.14 = (f32[64,8,256]{2,1,0:T(8,128)S(1)}, f32[64,8,256]{2,1,0:T(8,128)S(1)}, u32[]{:S(2)}, u32[]{:S(2)}) collective-permute-start(f32[64,8,256]{2,1,0:T(8,128)S(1)} %get-tuple-element.118), channel_id=1, source_target_pairs={{0,1},{2,3},{1,0},{3,2},{4,5},{6,7},{5,4},{7,6},{8,9},{10,11},{9,8... | collective-permute-start | bytes 1572872 | tf_op jit(solution)/shard_map/cond/branch_2_fun/ppermute | solution.py:505
  14.4 1.9 %collective-permute-start.15 = (f32[64,8,256]{2,1,0:T(8,128)S(1)}, f32[64,8,256]{2,1,0:T(8,128)S(1)}, u32[]{:S(2)}, u32[]{:S(2)}) collective-permute-start(f32[64,8,256]{2,1,0:T(8,128)S(1)} %get-tuple-element.119), channel_id=1, source_target_pairs={{1,2},{2,1},{5,6},{6,5},{9,10},{10,9},{13,14},{14,13},{17,18},{18,... | collective-permute-start | bytes 1572872 | tf_op jit(solution)/shard_map/cond/branch_2_fun/ppermute | solution.py:505
  16.4 4.6 %dual_x_inner_0.1.refs_2_.after = f32[64,64,256]{2,1,0:T(8,128)S(1)} custom-call(s32[3]{0:T(128)S(1)} %copy-done.15, f32[64,64,256]{2,1,0:T(8,128)S(1)} %get-tuple-element.115.refs_1_), custom_call_target="tpu_custom_call" | custom-call | flops 1 | bytes 1 | tf_op jit(solution)/shard_map/cond/branch_2_fun/dual_x_inner_0/pallas_call | solution.py:439
  21.0 1.2 %collective-permute-start.16 = (f32[16,8,256]{2,1,0:T(8,128)S(1)}, f32[16,8,256]{2,1,0:T(8,128)S(1)}, u32[]{:S(2)}, u32[]{:S(2)}) collective-permute-start(f32[16,8,256]{2,1,0:T(8,128)S(1)} %get-tuple-element.120), channel_id=1, source_target_pairs={{0,1},{2,3},{1,0},{3,2},{4,5},{6,7},{5,4},{7,6},{8,9},{10,11},{9,8... | collective-permute-start | bytes 393224 | tf_op jit(solution)/shard_map/cond/branch_2_fun/ppermute | solution.py:505
  22.2 2.5 %collective-permute-start.17 = (f32[16,8,256]{2,1,0:T(8,128)S(1)}, f32[16,8,256]{2,1,0:T(8,128)S(1)}, u32[]{:S(2)}, u32[]{:S(2)}) collective-permute-start(f32[16,8,256]{2,1,0:T(8,128)S(1)} %get-tuple-element.121), channel_id=1, source_target_pairs={{1,2},{2,1},{5,6},{6,5},{9,10},{10,9},{13,14},{14,13},{17,18},{18,... | collective-permute-start | bytes 393224 | tf_op jit(solution)/shard_map/cond/branch_2_fun/ppermute | solution.py:505
  24.7 2.4 %dual_x_outer_0.1.refs_2_ = f32[64,64,256]{2,1,0:T(8,128)S(1)} custom-call(s32[3]{0:T(128)S(1)} %copy-done.15, f32[64,64,256]{2,1,0:T(8,128)S(1)} %get-tuple-element.115.refs_1_, f32[64,64,256]{2,1,0:T(8,128)S(1)} %dual_x_inner_0.1.refs_2_.after, f32[8,64,256]{2,1,0:T(8,128)S(1)} %collective-permute-done.12.refs_3_.even, ...), custom_call_target="tpu_custom_call", output_to_operand_aliasing={{}: (2, {})} | custom-call | flops 1 | bytes 1 | tf_op jit(solution)/shard_map/cond/branch_2_fun/dual_x_outer_0/pallas_call | solution.py:439
  27.1 3.0 %collective-permute-done.15.refs_4_ = f32[64,8,256]{2,1,0:T(8,128)S(1)} collective-permute-done((f32[64,8,256]{2,1,0:T(8,128)S(1)}, f32[64,8,256]{2,1,0:T(8,128)S(1)}, u32[]{:S(2)}, u32[]{:S(2)}) %collective-permute-start.15) | collective-permute-done | bytes 524320 | tf_op jit(solution)/shard_map/cond/branch_2_fun/ppermute | solution.py:505
  30.1 1.4 %collective-permute-done.17.refs_6_ = f32[16,8,256]{2,1,0:T(8,128)S(1)} collective-permute-done((f32[16,8,256]{2,1,0:T(8,128)S(1)}, f32[16,8,256]{2,1,0:T(8,128)S(1)}, u32[]{:S(2)}, u32[]{:S(2)}) %collective-permute-start.17) | collective-permute-done | bytes 131104 | tf_op jit(solution)/shard_map/cond/branch_2_fun/ppermute | solution.py:505
  31.5 7.1 %dual_0.3 = (f32[64,64,256]{2,1,0:T(8,128)}, f32[64,64,256]{2,1,0:T(8,128)S(1)}, f32[8,64,256]{2,1,0:T(8,128)S(1)}, f32[8,64,256]{2,1,0:T(8,128)S(1)}, f32[64,8,...) custom-call(f32[64,64,256]{2,1,0:T(8,128)S(1)} %copy-done.8, s32[3]{0:T(128)S(1)} %copy-done.15, ...), custom_call_target="tpu_custom_call" | custom-call | flops 1 | bytes 1 | tf_op jit(solution)/shard_map/cond/branch_2_fun/dual_0/pallas_call | solution.py:439
  38.6 0.1 collective-permute-start.18
  38.7 2.6 %collective-permute-start.19 = (f32[8,64,256]{2,1,0:T(8,128)S(1)}, f32[8,64,256]{2,1,0:T(8,128)S(1)}, u32[]{:S(2)}, u32[]{:S(2)}) collective-permute-start(f32[8,64,256]{2,1,0:T(8,128)S(1)} %get-tuple-element.126), channel_id=1, source_target_pairs={{4,8},{8,4},{5,9},{9,5},{6,10},{10,6},{7,11},{11,7},{20,24},{24,20... | collective-permute-start | bytes 1572872 | tf_op jit(solution)/shard_map/cond/branch_2_fun/ppermute | solution.py:505
  41.3 0.1 collective-permute-start.20
  41.4 1.9 %collective-permute-start.21 = (f32[64,8,256]{2,1,0:T(8,128)S(1)}, f32[64,8,256]{2,1,0:T(8,128)S(1)}, u32[]{:S(2)}, u32[]{:S(2)}) collective-permute-start(f32[64,8,256]{2,1,0:T(8,128)S(1)} %get-tuple-element.128), channel_id=1, source_target_pairs={{1,2},{2,1},{5,6},{6,5},{9,10},{10,9},{13,14},{14,13},{17,18},{18,... | collective-permute-start | bytes 1572872 | tf_op jit(solution)/shard_map/cond/branch_2_fun/ppermute | solution.py:505
  43.3 4.6 %partial_x_inner_0.1.refs_2_.after = f32[64,64,256]{2,1,0:T(8,128)S(1)} custom-call(s32[3]{0:T(128)S(1)} %copy-done.15, f32[64,64,256]{2,1,0:T(8,128)S(1)} %get-tuple-element.124.refs_1_), custom_call_target="tpu_custom_call" | custom-call | flops 1 | bytes 1 | tf_op jit(solution)/shard_map/cond/branch_2_fun/partial_x_inner_0/pallas_call | solution.py:439
  47.9 1.5 %collective-permute-done.19.refs_4_.odd = f32[8,64,256]{2,1,0:T(8,128)S(1)} collective-permute-done((f32[8,64,256]{2,1,0:T(8,128)S(1)}, f32[8,64,256]{2,1,0:T(8,128)S(1)}, u32[]{:S(2)}, u32[]{:S(2)}) %collective-permute-start.19) | collective-permute-done | bytes 524320 | tf_op jit(solution)/shard_map/cond/branch_2_fun/ppermute | solution.py:505
  49.5 0.1 collective-permute-start.22
  49.6 0.0 copy-start.2
  49.6 2.2 %collective-permute-start.23 = (f32[16,8,256]{2,1,0:T(8,128)S(1)}, f32[16,8,256]{2,1,0:T(8,128)S(1)}, u32[]{:S(2)}, u32[]{:S(2)}) collective-permute-start(f32[16,8,256]{2,1,0:T(8,128)S(1)} %get-tuple-element.130), channel_id=1, source_target_pairs={{1,2},{2,1},{5,6},{6,5},{9,10},{10,9},{13,14},{14,13},{17,18},{18,... | collective-permute-start | bytes 393224 | tf_op jit(solution)/shard_map/cond/branch_2_fun/ppermute | solution.py:505
  51.8 2.4 %partial_x_outer_0.1.refs_3_ = f32[64,64,256]{2,1,0:T(8,128)S(1)} custom-call(s32[3]{0:T(128)S(1)} %copy-done.15, f32[64,64,256]{2,1,0:T(8,128)S(1)} %get-tuple-element.124.refs_1_, f32[64,64,256]{2,1,0:T(8,128)S(1)} %partial_x_inner_0.1.refs_2_.after, f32[8,64,256]{2,1,0:T(8,128)S(1)} %collective-permute-done.18.refs_3_.even, ...), custom_call_target="tpu_custom_call", output_to_operand_aliasing={{}: (2, {})} | custom-call | flops 1 | bytes 1 | tf_op jit(solution)/shard_map/cond/branch_2_fun/partial_x_outer_0/pallas_call | solution.py:439
  54.1 1.2 %collective-permute-done.20.refs_4_ = f32[64,8,256]{2,1,0:T(8,128)S(1)} collective-permute-done((f32[64,8,256]{2,1,0:T(8,128)S(1)}, f32[64,8,256]{2,1,0:T(8,128)S(1)}, u32[]{:S(2)}, u32[]{:S(2)}) %collective-permute-start.20) | collective-permute-done | bytes 524320 | tf_op jit(solution)/shard_map/cond/branch_2_fun/ppermute | solution.py:505
  55.3 1.9 %collective-permute-done.21.refs_5_ = f32[64,8,256]{2,1,0:T(8,128)S(1)} collective-permute-done((f32[64,8,256]{2,1,0:T(8,128)S(1)}, f32[64,8,256]{2,1,0:T(8,128)S(1)}, u32[]{:S(2)}, u32[]{:S(2)}) %collective-permute-start.21) | collective-permute-done | bytes 524320 | tf_op jit(solution)/shard_map/cond/branch_2_fun/ppermute | solution.py:505
  57.2 1.5 %collective-permute-done.23.refs_7_ = f32[16,8,256]{2,1,0:T(8,128)S(1)} collective-permute-done((f32[16,8,256]{2,1,0:T(8,128)S(1)}, f32[16,8,256]{2,1,0:T(8,128)S(1)}, u32[]{:S(2)}, u32[]{:S(2)}) %collective-permute-start.23) | collective-permute-done | bytes 131104 | tf_op jit(solution)/shard_map/cond/branch_2_fun/ppermute | solution.py:505
  58.7 6.2 %partial_0.3 = (f32[64,64,128]{2,1,0:T(8,128)}, f32[64,64,128]{2,1,0:T(8,128)}, f32[64,64,256]{2,1,0:T(8,128)}) custom-call(f32[64,64,256]{2,1,0:T(8,128)S(1)} %copy-done.2, f32[1]{0:T(128)} %get-tuple-element.112.refs_1_, s32[3]{0:T(128)S(1)} %copy-done.15, f32[64,64,256]{2,1,0:T(8,128)S(1)} %partial_x_outer_0.1.refs_3_, ...), custom_call_target="tpu_custom_call" | custom-call | flops 1 | bytes 1 | tf_op jit(solution)/shard_map/cond/branch_2_fun/partial_0/pallas_call | solution.py:439
  65.2 0.3 collective-permute-start.37
  65.5 32.1 %conditional.3 = (f32[64,64,256]{2,1,0:T(8,128)}) conditional(s32[]{:T(128)} %clamp.4, (f32[64,64,256]{2,1,0:T(8,128)}, f32[1]{0:T(128)}, f32[64,64,128]{2,1,0:T(8,128)S(1)}, f32[64,64,128]{2,1,0:T(8,128)}, s32[3]{0:T(128)}, /*index=5*/f32[64,64,256]{2,1,0:T(8,128)}) %tuple.30, (f32[64,64,256]{2,1,0:T(8,128)}, f32[1]{0:T(128)}, ...), branch_computations={%region_4.5_spmd, %region_5.6_spmd, %region_6.7_spmd} | conditional | flops 5 | bytes 46137672 | solution.py:630
  65.5 6.4 %cotangent_0.3 = (f32[64,64,256]{2,1,0:T(8,128)S(1)}, f32[8,64,256]{2,1,0:T(8,128)S(1)}, f32[8,64,256]{2,1,0:T(8,128)S(1)}, f32[64,8,256]{2,1,0:T(8,128)S(1)}, f...) custom-call(f32[64,64,256]{2,1,0:T(8,128)} %get-tuple-element.162.refs_0_, ...), custom_call_target="tpu_custom_call" | custom-call | flops 1 | bytes 1 | tf_op jit(solution)/shard_map/cond/branch_2_fun/cotangent_0/pallas_call | solution.py:439
  71.9 0.1 collective-permute-start.30
  72.0 2.6 %collective-permute-start.31 = (f32[8,64,256]{2,1,0:T(8,128)S(1)}, f32[8,64,256]{2,1,0:T(8,128)S(1)}, u32[]{:S(2)}, u32[]{:S(2)}) collective-permute-start(f32[8,64,256]{2,1,0:T(8,128)S(1)} %get-tuple-element.168), channel_id=1, source_target_pairs={{4,8},{8,4},{5,9},{9,5},{6,10},{10,6},{7,11},{11,7},{20,24},{24,20... | collective-permute-start | bytes 1572872 | tf_op jit(solution)/shard_map/cond/branch_2_fun/ppermute | solution.py:505
  74.6 0.1 collective-permute-start.32
  74.7 1.9 %collective-permute-start.33 = (f32[64,8,256]{2,1,0:T(8,128)S(1)}, f32[64,8,256]{2,1,0:T(8,128)S(1)}, u32[]{:S(2)}, u32[]{:S(2)}) collective-permute-start(f32[64,8,256]{2,1,0:T(8,128)S(1)} %get-tuple-element.170), channel_id=1, source_target_pairs={{1,2},{2,1},{5,6},{6,5},{9,10},{10,9},{13,14},{14,13},{17,18},{18,... | collective-permute-start | bytes 1572872 | tf_op jit(solution)/shard_map/cond/branch_2_fun/ppermute | solution.py:505
  76.6 4.6 %gradient_x_inner_0.1.refs_2_.after = f32[64,64,256]{2,1,0:T(8,128)S(1)} custom-call(s32[3]{0:T(128)S(1)} %copy-done.18, f32[64,64,256]{2,1,0:T(8,128)S(1)} %get-tuple-element.166.refs_1_), custom_call_target="tpu_custom_call" | custom-call | flops 1 | bytes 1 | tf_op jit(solution)/shard_map/cond/branch_2_fun/gradient_x_inner_0/pallas_call | solution.py:439
  81.2 1.6 %collective-permute-done.31.refs_4_.odd = f32[8,64,256]{2,1,0:T(8,128)S(1)} collective-permute-done((f32[8,64,256]{2,1,0:T(8,128)S(1)}, f32[8,64,256]{2,1,0:T(8,128)S(1)}, u32[]{:S(2)}, u32[]{:S(2)}) %collective-permute-start.31) | collective-permute-done | bytes 524320 | tf_op jit(solution)/shard_map/cond/branch_2_fun/ppermute | solution.py:505
  82.9 0.1 collective-permute-start.34
  83.0 2.2 %collective-permute-start.35 = (f32[16,8,256]{2,1,0:T(8,128)S(1)}, f32[16,8,256]{2,1,0:T(8,128)S(1)}, u32[]{:S(2)}, u32[]{:S(2)}) collective-permute-start(f32[16,8,256]{2,1,0:T(8,128)S(1)} %get-tuple-element.172), channel_id=1, source_target_pairs={{1,2},{2,1},{5,6},{6,5},{9,10},{10,9},{13,14},{14,13},{17,18},{18,... | collective-permute-start | bytes 393224 | tf_op jit(solution)/shard_map/cond/branch_2_fun/ppermute | solution.py:505
  85.2 2.4 %gradient_x_outer_0.1.refs_2_ = f32[64,64,256]{2,1,0:T(8,128)S(1)} custom-call(s32[3]{0:T(128)S(1)} %copy-done.18, f32[64,64,256]{2,1,0:T(8,128)S(1)} %get-tuple-element.166.refs_1_, f32[64,64,256]{2,1,0:T(8,128)S(1)} %gradient_x_inner_0.1.refs_2_.after, f32[8,64,256]{2,1,0:T(8,128)S(1)} %collective-permute-done.30.refs_3_.even, ...), custom_call_target="tpu_custom_call", output_to_operand_aliasing={{}: (2, {})} | custom-call | flops 1 | bytes 1 | tf_op jit(solution)/shard_map/cond/branch_2_fun/gradient_x_outer_0/pallas_call | solution.py:439
  87.5 1.2 %collective-permute-done.32.refs_3_ = f32[64,8,256]{2,1,0:T(8,128)S(1)} collective-permute-done((f32[64,8,256]{2,1,0:T(8,128)S(1)}, f32[64,8,256]{2,1,0:T(8,128)S(1)}, u32[]{:S(2)}, u32[]{:S(2)}) %collective-permute-start.32) | collective-permute-done | bytes 524320 | tf_op jit(solution)/shard_map/cond/branch_2_fun/ppermute | solution.py:505
  88.7 1.9 %collective-permute-done.33.refs_4_ = f32[64,8,256]{2,1,0:T(8,128)S(1)} collective-permute-done((f32[64,8,256]{2,1,0:T(8,128)S(1)}, f32[64,8,256]{2,1,0:T(8,128)S(1)}, u32[]{:S(2)}, u32[]{:S(2)}) %collective-permute-start.33) | collective-permute-done | bytes 524320 | tf_op jit(solution)/shard_map/cond/branch_2_fun/ppermute | solution.py:505
  90.6 1.8 %collective-permute-done.35.refs_6_ = f32[16,8,256]{2,1,0:T(8,128)S(1)} collective-permute-done((f32[16,8,256]{2,1,0:T(8,128)S(1)}, f32[16,8,256]{2,1,0:T(8,128)S(1)}, u32[]{:S(2)}, u32[]{:S(2)}) %collective-permute-start.35) | collective-permute-done | bytes 131104 | tf_op jit(solution)/shard_map/cond/branch_2_fun/ppermute | solution.py:505
  92.5 5.1 %gradient_0.3 = f32[64,64,256]{2,1,0:T(8,128)} custom-call(f32[64,64,256]{2,1,0:T(8,128)S(1)} %copy-done.5, s32[3]{0:T(128)S(1)} %copy-done.18, f32[64,64,256]{2,1,0:T(8,128)S(1)} %gradient_x_outer_0.1.refs_2_, f32[64,8,256]{2,1,0:T(8,128)S(1)} %collective-permute-done.32.refs_3_, f32[64,8,256]{2,1,0:T(8,128)S(1)} %collective-permute-done.33.refs_4_, ...), custom_call_target="tpu_custom_call" | custom-call | flops 1 | bytes 1 | tf_op jit(solution)/shard_map/cond/branch_2_fun/gradient_0/pallas_call | solution.py:439
  97.6 1.6 %fetch.1.keep = f32[64,64,128]{2,1,0:T(8,128)S(1)} custom-call(f32[64,64,128]{2,1,0:T(8,128)} %get-tuple-element.180.source, f32[64,64,256]{2,1,0:T(8,128)} %get-tuple-element.196.after), custom_call_target="tpu_custom_call" | custom-call | flops 1 | bytes 1 | tf_op jit(solution)/shard_map/fetch/pallas_call | solution.py:460
  99.2 13.9 %collective-permute-done.37.arrived = f32[64,64,128]{2,1,0:T(8,128)} collective-permute-done((f32[64,64,128]{2,1,0:T(8,128)}, f32[64,64,128]{2,1,0:T(8,128)}, u32[]{:S(2)}, u32[]{:S(2)}) %collective-permute-start.37) | collective-permute-done | bytes 2097184 | tf_op jit(solution)/shard_map/ppermute | solution.py:629
  113.1 2.6 %barycenter.1 = f32[64,64,128]{2,1,0:T(8,128)} custom-call(f32[64,64,128]{2,1,0:T(8,128)S(1)} %fetch.1.keep, f32[64,64,128]{2,1,0:T(8,128)} %collective-permute-done.37.arrived), custom_call_target="tpu_custom_call" | custom-call | flops 1 | bytes 1 | tf_op jit(solution)/shard_map/barycenter/pallas_call | solution.py:489
  (21 shorter events, 0.1 us)
Async XLA Ops:
  0.6 64.8 %collective-permute-start.36 = (f32[64,64,128]{2,1,0:T(8,128)}, f32[64,64,128]{2,1,0:T(8,128)S(1)}, u32[]{:S(2)}, u32[]{:S(2)}) collective-permute-start(f32[64,64,128]{2,1,0:T(8,128)} %param.15), channel_id=1, source_target_pairs={{0,16},{16,0},{1,17},{17,1},{2,18},{18,2},{3,19},{19,3},{4,20},{20... | collective-permute-start | bytes 6291464 | tf_op jit(solution)/shard_map/ppermute | solution.py:625
  3.9 12.4 %copy-start.15 = (s32[3]{0:T(128)S(1)}, s32[3]{0:T(128)}, u32[]{:S(2)}) copy-start(s32[3]{0:T(128)} %get-tuple-element.113.refs_1_.refs_0_.refs_2_) | copy-start | bytes 40 | tf_op jit(solution)/shard_map/cond
  9.0 11.9 %collective-permute-start.12 = (f32[8,64,256]{2,1,0:T(8,128)S(1)}, f32[8,64,256]{2,1,0:T(8,128)S(1)}, u32[]{:S(2)}, u32[]{:S(2)}) collective-permute-start(f32[8,64,256]{2,1,0:T(8,128)S(1)} %get-tuple-element.116), channel_id=1, source_target_pairs={{0,4},{8,12},{4,0},{12,8},{1,5},{9,13},{5,1},{13,9},{2,6},{10,14},... | collective-permute-start | bytes 1572872 | tf_op jit(solution)/shard_map/cond/branch_2_fun/ppermute | solution.py:505
  10.1 10.9 %collective-permute-start.13 = (f32[8,64,256]{2,1,0:T(8,128)S(1)}, f32[8,64,256]{2,1,0:T(8,128)S(1)}, u32[]{:S(2)}, u32[]{:S(2)}) collective-permute-start(f32[8,64,256]{2,1,0:T(8,128)S(1)} %get-tuple-element.117), channel_id=1, source_target_pairs={{4,8},{8,4},{5,9},{9,5},{6,10},{10,6},{7,11},{11,7},{20,24},{24,20... | collective-permute-start | bytes 1572872 | tf_op jit(solution)/shard_map/cond/branch_2_fun/ppermute | solution.py:505
  13.1 14.0 %collective-permute-start.14 = (f32[64,8,256]{2,1,0:T(8,128)S(1)}, f32[64,8,256]{2,1,0:T(8,128)S(1)}, u32[]{:S(2)}, u32[]{:S(2)}) collective-permute-start(f32[64,8,256]{2,1,0:T(8,128)S(1)} %get-tuple-element.118), channel_id=1, source_target_pairs={{0,1},{2,3},{1,0},{3,2},{4,5},{6,7},{5,4},{7,6},{8,9},{10,11},{9,8... | collective-permute-start | bytes 1572872 | tf_op jit(solution)/shard_map/cond/branch_2_fun/ppermute | solution.py:505
  14.4 15.7 %collective-permute-start.15 = (f32[64,8,256]{2,1,0:T(8,128)S(1)}, f32[64,8,256]{2,1,0:T(8,128)S(1)}, u32[]{:S(2)}, u32[]{:S(2)}) collective-permute-start(f32[64,8,256]{2,1,0:T(8,128)S(1)} %get-tuple-element.119), channel_id=1, source_target_pairs={{1,2},{2,1},{5,6},{6,5},{9,10},{10,9},{13,14},{14,13},{17,18},{18,... | collective-permute-start | bytes 1572872 | tf_op jit(solution)/shard_map/cond/branch_2_fun/ppermute | solution.py:505
  21.0 9.1 %collective-permute-start.16 = (f32[16,8,256]{2,1,0:T(8,128)S(1)}, f32[16,8,256]{2,1,0:T(8,128)S(1)}, u32[]{:S(2)}, u32[]{:S(2)}) collective-permute-start(f32[16,8,256]{2,1,0:T(8,128)S(1)} %get-tuple-element.120), channel_id=1, source_target_pairs={{0,1},{2,3},{1,0},{3,2},{4,5},{6,7},{5,4},{7,6},{8,9},{10,11},{9,8... | collective-permute-start | bytes 393224 | tf_op jit(solution)/shard_map/cond/branch_2_fun/ppermute | solution.py:505
  22.2 9.3 %copy-start.8 = (f32[64,64,256]{2,1,0:T(8,128)S(1)}, f32[64,64,256]{2,1,0:T(8,128)}, u32[]{:S(2)}) copy-start(f32[64,64,256]{2,1,0:T(8,128)} %get-tuple-element.114.refs_0_) | copy-start | bytes 12582916 | tf_op jit(solution)/shard_map/cond
  22.2 9.3 %collective-permute-start.17 = (f32[16,8,256]{2,1,0:T(8,128)S(1)}, f32[16,8,256]{2,1,0:T(8,128)S(1)}, u32[]{:S(2)}, u32[]{:S(2)}) collective-permute-start(f32[16,8,256]{2,1,0:T(8,128)S(1)} %get-tuple-element.121), channel_id=1, source_target_pairs={{1,2},{2,1},{5,6},{6,5},{9,10},{10,9},{13,14},{14,13},{17,18},{18,... | collective-permute-start | bytes 393224 | tf_op jit(solution)/shard_map/cond/branch_2_fun/ppermute | solution.py:505
  38.6 9.3 %collective-permute-start.18 = (f32[8,64,256]{2,1,0:T(8,128)S(1)}, f32[8,64,256]{2,1,0:T(8,128)S(1)}, u32[]{:S(2)}, u32[]{:S(2)}) collective-permute-start(f32[8,64,256]{2,1,0:T(8,128)S(1)} %get-tuple-element.125), channel_id=1, source_target_pairs={{0,4},{8,12},{4,0},{12,8},{1,5},{9,13},{5,1},{13,9},{2,6},{10,14},... | collective-permute-start | bytes 1572872 | tf_op jit(solution)/shard_map/cond/branch_2_fun/ppermute | solution.py:505
  38.7 10.8 %collective-permute-start.19 = (f32[8,64,256]{2,1,0:T(8,128)S(1)}, f32[8,64,256]{2,1,0:T(8,128)S(1)}, u32[]{:S(2)}, u32[]{:S(2)}) collective-permute-start(f32[8,64,256]{2,1,0:T(8,128)S(1)} %get-tuple-element.126), channel_id=1, source_target_pairs={{4,8},{8,4},{5,9},{9,5},{6,10},{10,6},{7,11},{11,7},{20,24},{24,20... | collective-permute-start | bytes 1572872 | tf_op jit(solution)/shard_map/cond/branch_2_fun/ppermute | solution.py:505
  41.3 14.0 %collective-permute-start.20 = (f32[64,8,256]{2,1,0:T(8,128)S(1)}, f32[64,8,256]{2,1,0:T(8,128)S(1)}, u32[]{:S(2)}, u32[]{:S(2)}) collective-permute-start(f32[64,8,256]{2,1,0:T(8,128)S(1)} %get-tuple-element.127), channel_id=1, source_target_pairs={{0,1},{2,3},{1,0},{3,2},{4,5},{6,7},{5,4},{7,6},{8,9},{10,11},{9,8... | collective-permute-start | bytes 1572872 | tf_op jit(solution)/shard_map/cond/branch_2_fun/ppermute | solution.py:505
  41.4 15.8 %collective-permute-start.21 = (f32[64,8,256]{2,1,0:T(8,128)S(1)}, f32[64,8,256]{2,1,0:T(8,128)S(1)}, u32[]{:S(2)}, u32[]{:S(2)}) collective-permute-start(f32[64,8,256]{2,1,0:T(8,128)S(1)} %get-tuple-element.128), channel_id=1, source_target_pairs={{1,2},{2,1},{5,6},{6,5},{9,10},{10,9},{13,14},{14,13},{17,18},{18,... | collective-permute-start | bytes 1572872 | tf_op jit(solution)/shard_map/cond/branch_2_fun/ppermute | solution.py:505
  49.5 7.7 %collective-permute-start.22 = (f32[16,8,256]{2,1,0:T(8,128)S(1)}, f32[16,8,256]{2,1,0:T(8,128)S(1)}, u32[]{:S(2)}, u32[]{:S(2)}) collective-permute-start(f32[16,8,256]{2,1,0:T(8,128)S(1)} %get-tuple-element.129), channel_id=1, source_target_pairs={{0,1},{2,3},{1,0},{3,2},{4,5},{6,7},{5,4},{7,6},{8,9},{10,11},{9,8... | collective-permute-start | bytes 393224 | tf_op jit(solution)/shard_map/cond/branch_2_fun/ppermute | solution.py:505
  49.6 9.2 %copy-start.2 = (f32[64,64,256]{2,1,0:T(8,128)S(1)}, f32[64,64,256]{2,1,0:T(8,128)}, u32[]{:S(2)}) copy-start(f32[64,64,256]{2,1,0:T(8,128)} %get-tuple-element.111.refs_0_) | copy-start | bytes 12582916 | tf_op jit(solution)/shard_map/cond
  49.6 9.2 %collective-permute-start.23 = (f32[16,8,256]{2,1,0:T(8,128)S(1)}, f32[16,8,256]{2,1,0:T(8,128)S(1)}, u32[]{:S(2)}, u32[]{:S(2)}) collective-permute-start(f32[16,8,256]{2,1,0:T(8,128)S(1)} %get-tuple-element.130), channel_id=1, source_target_pairs={{1,2},{2,1},{5,6},{6,5},{9,10},{10,9},{13,14},{14,13},{17,18},{18,... | collective-permute-start | bytes 393224 | tf_op jit(solution)/shard_map/cond/branch_2_fun/ppermute | solution.py:505
  65.2 47.9 %collective-permute-start.37 = (f32[64,64,128]{2,1,0:T(8,128)}, f32[64,64,128]{2,1,0:T(8,128)}, u32[]{:S(2)}, u32[]{:S(2)}) collective-permute-start(f32[64,64,128]{2,1,0:T(8,128)} %get-tuple-element.183), channel_id=1, source_target_pairs={{0,16},{16,0},{1,17},{17,1},{2,18},{18,2},{3,19},{19,3},{4,20},{20... | collective-permute-start | bytes 6291464 | tf_op jit(solution)/shard_map/ppermute | solution.py:629
  65.5 11.2 %copy-start.18 = (s32[3]{0:T(128)S(1)}, s32[3]{0:T(128)}, u32[]{:S(2)}) copy-start(s32[3]{0:T(128)} %get-tuple-element.161.refs_4_.refs_0_.refs_1_) | copy-start | bytes 40 | tf_op jit(solution)/shard_map/cond
  71.9 9.3 %collective-permute-start.30 = (f32[8,64,256]{2,1,0:T(8,128)S(1)}, f32[8,64,256]{2,1,0:T(8,128)S(1)}, u32[]{:S(2)}, u32[]{:S(2)}) collective-permute-start(f32[8,64,256]{2,1,0:T(8,128)S(1)} %get-tuple-element.167), channel_id=1, source_target_pairs={{0,4},{8,12},{4,0},{12,8},{1,5},{9,13},{5,1},{13,9},{2,6},{10,14},... | collective-permute-start | bytes 1572872 | tf_op jit(solution)/shard_map/cond/branch_2_fun/ppermute | solution.py:505
  72.0 10.9 %collective-permute-start.31 = (f32[8,64,256]{2,1,0:T(8,128)S(1)}, f32[8,64,256]{2,1,0:T(8,128)S(1)}, u32[]{:S(2)}, u32[]{:S(2)}) collective-permute-start(f32[8,64,256]{2,1,0:T(8,128)S(1)} %get-tuple-element.168), channel_id=1, source_target_pairs={{4,8},{8,4},{5,9},{9,5},{6,10},{10,6},{7,11},{11,7},{20,24},{24,20... | collective-permute-start | bytes 1572872 | tf_op jit(solution)/shard_map/cond/branch_2_fun/ppermute | solution.py:505
  74.6 14.1 %collective-permute-start.32 = (f32[64,8,256]{2,1,0:T(8,128)S(1)}, f32[64,8,256]{2,1,0:T(8,128)S(1)}, u32[]{:S(2)}, u32[]{:S(2)}) collective-permute-start(f32[64,8,256]{2,1,0:T(8,128)S(1)} %get-tuple-element.169), channel_id=1, source_target_pairs={{0,1},{2,3},{1,0},{3,2},{4,5},{6,7},{5,4},{7,6},{8,9},{10,11},{9,8... | collective-permute-start | bytes 1572872 | tf_op jit(solution)/shard_map/cond/branch_2_fun/ppermute | solution.py:505
  74.7 15.9 %collective-permute-start.33 = (f32[64,8,256]{2,1,0:T(8,128)S(1)}, f32[64,8,256]{2,1,0:T(8,128)S(1)}, u32[]{:S(2)}, u32[]{:S(2)}) collective-permute-start(f32[64,8,256]{2,1,0:T(8,128)S(1)} %get-tuple-element.170), channel_id=1, source_target_pairs={{1,2},{2,1},{5,6},{6,5},{9,10},{10,9},{13,14},{14,13},{17,18},{18,... | collective-permute-start | bytes 1572872 | tf_op jit(solution)/shard_map/cond/branch_2_fun/ppermute | solution.py:505
  82.9 7.7 %collective-permute-start.34 = (f32[16,8,256]{2,1,0:T(8,128)S(1)}, f32[16,8,256]{2,1,0:T(8,128)S(1)}, u32[]{:S(2)}, u32[]{:S(2)}) collective-permute-start(f32[16,8,256]{2,1,0:T(8,128)S(1)} %get-tuple-element.171), channel_id=1, source_target_pairs={{0,1},{2,3},{1,0},{3,2},{4,5},{6,7},{5,4},{7,6},{8,9},{10,11},{9,8... | collective-permute-start | bytes 393224 | tf_op jit(solution)/shard_map/cond/branch_2_fun/ppermute | solution.py:505
  83.0 9.5 %copy-start.5 = (f32[64,64,256]{2,1,0:T(8,128)S(1)}, f32[64,64,256]{2,1,0:T(8,128)}, u32[]{:S(2)}) copy-start(f32[64,64,256]{2,1,0:T(8,128)} %get-tuple-element.160.refs_0_) | copy-start | bytes 12582916 | tf_op jit(solution)/shard_map/cond
  83.0 9.5 %collective-permute-start.35 = (f32[16,8,256]{2,1,0:T(8,128)S(1)}, f32[16,8,256]{2,1,0:T(8,128)S(1)}, u32[]{:S(2)}, u32[]{:S(2)}) collective-permute-start(f32[16,8,256]{2,1,0:T(8,128)S(1)} %get-tuple-element.172), channel_id=1, source_target_pairs={{1,2},{2,1},{5,6},{6,5},{9,10},{10,9},{13,14},{14,13},{17,18},{18,... | collective-permute-start | bytes 393224 | tf_op jit(solution)/shard_map/cond/branch_2_fun/ppermute | solution.py:505
